TPU v7x, 32 devices: a whole 2x2x4 slice. The times are simulated.
32 devices in a mesh: ctx: 16 (over z, y, core), head: 2 (over x).
Axes of the slice: x: 2, y: 2, z: 4, core: 2. Of those that a mesh axis runs over, the one named last changes fastest.
Arguments:
- queries: bfloat16 [2048, 64, 128], P('ctx', 'head'), may hold values from -200 to 200
- new_keys: bfloat16 [2048, 8, 128], P('ctx', 'head'), may hold values from -6 to 6
- new_values: bfloat16 [2048, 8, 128], P('ctx', 'head'), may hold values from -6 to 6
- pool_keys: bfloat16 [128, 32, 8, 128], P('ctx', None, 'head'), may hold values from -6 to 6
- pool_values: bfloat16 [128, 32, 8, 128], P('ctx', None, 'head'), may hold values from -6 to 6
- o_weight: bfloat16 [8192, 8192], P('head', 'ctx'), may hold values from -1.5 to 1.5
- page_list: int32 [32], replicated, may hold values from 0 to 127, as said below
Outputs:
- projected: bfloat16 [2048, 8192], P('ctx', 'head')
Inputs may be any that keep to these rules, and one draw needn't show every extreme that they name: page_list names 32 distinct pool slots; slot p lies on cycle position p // 8; one cycle position holds exactly 4 of them and none holds more; some hold none.
All inputs are finite; a program needn't handle non-finite values.
Results may differ from a plain program's by a relative error of at most 0.015.
Values may be sent and summed in bfloat16 or wider, within the bound.
No kernel may reach another device: no remote copies, remote signals or barrier semaphores. Data moves between devices by JAX's collectives and lax.ppermute only.
A program may use at most 192 MiB of HBM per device.

v0:
```python
import jax
import jax.numpy as jnp
from jax import lax
from jax.sharding import PartitionSpec as P

NEG = -1e30


def absorb(carry, query_block, keys, values, seen, scale):
    best, total, acc = carry
    scores = (
        jnp.einsum("rkgd,skd->kgrs", query_block, keys, preferred_element_type=jnp.float32) * scale
    )
    scores = jnp.where(seen, scores, NEG)
    fresh = jnp.maximum(best, jnp.max(scores, axis=-1))
    weights = jnp.where(seen, jnp.exp(scores - fresh[..., None]), 0.0)
    total = jnp.sum(weights, axis=-1)
    acc = jnp.einsum(
        "kgrs,skd->kgrd", weights.astype(jnp.bfloat16), values, preferred_element_type=jnp.float32
    )
    return (fresh, total, acc)


def joined(first, second):
    best = jnp.maximum(first[0], second[0])
    left = jnp.exp(first[0] - best)
    right = jnp.exp(second[0] - best)
    total = first[1] * left + second[1] * right
    acc = first[2] * left[..., None] + second[2] * right[..., None]
    return (best, total, acc)


def on_device(queries, new_keys, new_values, pool_keys, pool_values, o_weight, page_list):
    rows, qheads, width = queries.shape
    kvheads = new_keys.shape[1]
    group = qheads // kvheads
    page_len = pool_keys.shape[1]
    scale = width ** (-0.5)
    query_block = queries.reshape(rows, kvheads, group, width)
    my_start = lax.axis_index("ctx") * rows
    query_pos = my_start + jnp.arange(rows, dtype=jnp.int32)
    start_state = (
        jnp.full((kvheads, group, rows), NEG, jnp.float32),
        jnp.zeros((kvheads, group, rows), jnp.float32),
        jnp.zeros((kvheads, group, rows, width), jnp.float32),
    )
    keys = lax.all_gather(pool_keys, "ctx", axis=0, tiled=True)
    values = lax.all_gather(pool_values, "ctx", axis=0, tiled=True)
    count = keys.shape[0]
    slot_ids = jnp.arange(count, dtype=jnp.int32)
    live = jnp.any(page_list[None, :] == slot_ids[:, None], axis=1)
    seen = jnp.repeat(live, page_len)[None, None, None, :]
    prefix_state = absorb(
        start_state,
        query_block,
        keys.reshape(count * page_len, kvheads, width),
        values.reshape(count * page_len, kvheads, width),
        seen,
        scale,
    )
    keys = lax.all_gather(new_keys, "ctx", axis=0, tiled=True)
    values = lax.all_gather(new_values, "ctx", axis=0, tiled=True)
    count = keys.shape[0]
    key_pos = jnp.arange(count, dtype=jnp.int32)
    seen = (key_pos[None, :] <= query_pos[:, None])[None, None, :, :]
    span_state = absorb(start_state, query_block, keys, values, seen, scale)
    best, total, acc = joined(prefix_state, span_state)
    attended = (acc / total[..., None]).astype(jnp.bfloat16)
    attended = attended.transpose(2, 0, 1, 3).reshape(rows, qheads * width)
    row_partials = jnp.dot(
        lax.all_gather(attended, "ctx", axis=0, tiled=True),
        o_weight,
        preferred_element_type=jnp.float32,
    )
    regrouped = lax.all_to_all(
        row_partials.astype(jnp.bfloat16), "ctx", split_axis=0, concat_axis=1, tiled=True
    ).astype(row_partials.dtype)
    return lax.psum_scatter(regrouped.astype(jnp.bfloat16), "head", scatter_dimension=1, tiled=True)


def solution(mesh):
    in_specs = (
        P("ctx", "head", None),
        P("ctx", "head", None),
        P("ctx", "head", None),
        P("ctx", None, "head", None),
        P("ctx", None, "head", None),
        P("head", "ctx"),
        P(),
    )
    out_specs = P("ctx", "head")
    return jax.shard_map(
        on_device, mesh=mesh, in_specs=in_specs, out_specs=out_specs, check_vma=False
    )
```

profile of v0, /device:TPU:6, one launch (start us, length us, event | category | flops | bytes accessed | tf_op | source)
XLA Modules:
  0.0 446.0 jit_solution(18417657622563689720)
XLA Ops:
  6.5 0.0 copy-start
  6.5 0.0 all-gather.10.cloned.1.call-start
  6.5 1.7 copy.44
  8.2 0.0 all-gather.10.cloned.1.call-update
  8.2 0.0 all-gather.6.cloned.1.call-start
  8.3 1.7 copy.38
  10.0 0.0 all-gather.6.cloned.1.call-update
  10.0 0.0 all-gather.8.cloned.1.call-start
  10.1 1.7 copy.41
  11.8 0.0 all-gather.8.cloned.1.call-update
  11.8 0.0 all-gather.12.cloned.1.call-start
  11.8 1.7 copy.46
  13.5 0.0 all-gather.12.cloned.1.call-update
  13.5 0.0 all-gather.14.cloned.1.call-start
  13.6 0.7 fusion.30
  14.3 0.1 broadcast_in_dim.56
  14.4 0.1 broadcast_in_dim.57
  14.5 0.2 iota_compare_fusion
  14.7 36.5 %all-gather.10.cloned.1.call-done = bf16[2048,4,128]{2,0,1:T(8,128)(2,1)} async-done(((bf16[128,4,128]{2,0,1:T(8,128)(2,1)}), bf16[2048,4,128]{2,0,1:T(8,128)(2,1)}) %all-gather.10.cloned.1.call-update) | async-done | bytes 2097168 | tf_op jit(solution)/shard_map/all_gather | solution.py:61
  51.3 0.0 copy-done
  51.3 15.3 %fusion.8 = (f32[4,8,128]{2,1,0:T(8,128)S(1)}, f32[4,2048,128,8]{2,1,3,0:T(8,128)}) fusion(pred[128,2048]{0,1:T(8,128)(4,1)S(1)} %iota_compare_fusion, bf16[128,4,8,128]{3,2,1,0:T(8,128)(2,1)S(1)} %bitcast.90, bf16[2048,4,128]{2,0,1:T(8,128)(2,1)} %all-gather.10.cloned.1.call-done), kind=kOutput, calls=%fused_computation.12 | convolution fusion | flops 2172645376 | bytes 36978688 | tf_op jit(solution)/shard_map/rkgd,skd->kgrs/dot_general | solution.py:12
  66.6 15.0 %fusion.9 = f32[4,8,128]{2,1,0:T(8,128)S(1)} fusion(f32[4,2048,128,8]{2,1,3,0:T(8,128)} %get-tuple-element.11, f32[4,8,128]{2,1,0:T(8,128)S(1)} %broadcast_maximum_fusion, pred[128,2048]{0,1:T(8,128)(4,1)S(1)} %iota_compare_fusion), kind=kLoop, calls=%fused_computation.13 | loop fusion | flops 41938944 | bytes 33849344 | tf_op jit(solution)/shard_map/reduce_sum | solution.py:17
  81.6 21.2 %all-gather.6.cloned.1.call-done = bf16[128,32,4,128]{3,1,2,0:T(8,128)(2,1)} async-done(((bf16[8,32,4,128]{3,1,2,0:T(8,128)(2,1)}), bf16[128,32,4,128]{3,1,2,0:T(8,128)(2,1)}) %all-gather.6.cloned.1.call-update) | async-done | bytes 4194320 | tf_op jit(solution)/shard_map/all_gather | solution.py:47
  102.8 5.0 %copy.39 = bf16[128,32,4,128]{3,1,0,2:T(8,128)(2,1)} copy(bf16[128,32,4,128]{3,1,2,0:T(8,128)(2,1)} %all-gather.6.cloned.1.call-done) | data formatting | bytes 8388608 | tf_op jit(solution)/shard_map/all_gather | solution.py:47
  107.8 27.8 %bitcast_reduce_fusion = (f32[4,8,128]{2,1,0:T(8,128)S(1)}, f32[4,4096,128,8]{2,1,3,0:T(8,128)}) fusion(pred[4096]{0:T(1024)(128)(4,1)S(1)} %broadcast_in_dim.57, bf16[4096,4,128,1]{2,0,3,1:T(8,128)(2,1)} %bitcast.91, bf16[128,4,8,128]{3,2,1,0:T(8,128)(2,1)S(1)} %bitcast.89), kind=kOutput, calls=%fused_computation.1 | convolution fusion | flops 4345294848 | bytes 72372224 | tf_op jit(solution)/shard_map/rkgd,skd->kgrs/dot_general | solution.py:12
  135.7 22.2 %fusion.2 = f32[4,8,128]{2,1,0:T(8,128)S(1)} fusion(f32[4,4096,128,8]{2,1,3,0:T(8,128)} %get-tuple-element.9, f32[4,8,128]{2,1,0:T(8,128)S(1)} %broadcast_maximum_fusion.1, pred[4096]{0:T(1024)(128)(4,1)S(1)} %broadcast_in_dim.57), kind=kLoop, calls=%fused_computation.5 | loop fusion | flops 83881984 | bytes 67145728 | tf_op jit(solution)/shard_map/reduce_sum | solution.py:17
  157.9 0.0 all-gather.8.cloned.1.call-done
  157.9 26.0 %fusion.4 = f32[4,8,128,128]{2,3,1,0:T(8,128)S(1)} fusion(bf16[4096,4,128,1]{2,0,3,1:T(8,128)(2,1)} %bitcast.96, f32[4,4096,128,8]{2,1,3,0:T(8,128)} %get-tuple-element.9, f32[4,8,128]{2,1,0:T(8,128)S(1)} %broadcast_maximum_fusion.1, pred[4096]{0:T(1024)(128)(4,1)S(1)} %broadcast_in_dim.57), kind=kOutput, calls=%fused_computation.9 | convolution fusion | flops 4378853376 | bytes 73420800 | tf_op jit(solution)/shard_map/kgrs,skd->kgrd/dot_general | solution.py:18
  183.9 12.6 %all-gather.12.cloned.1.call-done = bf16[2048,4,128]{0,2,1:T(8,128)(2,1)} async-done(((bf16[128,4,128]{0,2,1:T(8,128)(2,1)}), bf16[2048,4,128]{0,2,1:T(8,128)(2,1)}) %all-gather.12.cloned.1.call-update) | async-done | bytes 2097168 | tf_op jit(solution)/shard_map/all_gather | solution.py:62
  196.5 0.0 copy-start.1
  196.5 16.2 %fusion.19 = bf16[128,4,8,128]{0,3,2,1:T(8,128)(2,1)} fusion(f32[4,8,128,128]{2,3,1,0:T(8,128)S(1)} %fusion.4, f32[4,2048,128,8]{2,1,3,0:T(8,128)} %get-tuple-element.11, f32[4,8,128]{2,1,0:T(8,128)S(1)} %broadcast_maximum_fusion, pred[128,2048]{0,1:T(8,128)(4,1)S(1)} %iota_compare_fusion, bf16[2048,4,128]{0,2,1:T(8,128)(2,1)} %all-gather.12.cloned.1.call-done, ...), kind=kOutput, calls=%fused_computation.24 | convolution fusion | flops 2192048128 | bytes 39124992 | tf_op jit(solution)/shard_map/kgrs,skd->kgrd/dot_general | solution.py:18
  212.7 0.0 all-gather.14.cloned.1.call-update
  212.7 0.0 reduce-scatter.2.cloned.1.call-start
  212.8 129.6 %all-gather.14.cloned.1.call-done = bf16[2048,4096]{0,1:T(8,128)(2,1)} async-done(((bf16[128,4096]{0,1:T(8,128)(2,1)}), bf16[2048,4096]{0,1:T(8,128)(2,1)}) %all-gather.14.cloned.1.call-update) | async-done | bytes 16777232 | tf_op jit(solution)/shard_map/all_gather | solution.py:71
  342.4 13.6 %convolution_convert_fusion = bf16[2048,512]{1,0:T(8,128)(2,1)S(1)} fusion(bf16[2048,4096]{0,1:T(8,128)(2,1)} %all-gather.14.cloned.1.call-done, bf16[4096,512]{1,0:T(8,128)(2,1)} %param.12), kind=kOutput, calls=%fused_computation.17 | convolution fusion | flops 8590983168 | bytes 23068672 | tf_op jit(solution)/shard_map/dot_general | solution.py:70
  356.0 49.8 %all_to_all.19 = bf16[16,128,512]{2,1,0:T(8,128)(2,1)S(1)} all-to-all(bf16[16,128,512]{2,1,0:T(8,128)(2,1)S(1)} %bitcast.94), channel_id=1, replica_groups=mesh['ctx'=16,'head'=2] {'ctx'}, dimensions={0} | all-to-all | bytes 4194304 | tf_op jit(solution)/shard_map/all_to_all | solution.py:75
  405.9 1.6 copy.57
  407.4 0.0 reduce-scatter.2.cloned.1.call-update
  407.5 31.7 %reduce-scatter.2.cloned.1.call-done = bf16[128,4096]{1,0:T(8,128)(2,1)} async-done(((bf16[128,8192]{1,0:T(8,128)(2,1)}), bf16[128,4096]{1,0:T(8,128)(2,1)}) %reduce-scatter.2.cloned.1.call-update) | async-done | bytes 1048592 | tf_op jit(solution)/shard_map/reduce_scatter | solution.py:78
  439.1 0.0 copy-done.1
  (4 shorter events, 0.0 us)
Async XLA Ops:
  6.5 44.7 %copy-start = (bf16[128,32,128]{2,1,0:T(8,128)(2,1)S(1)}, bf16[128,32,128]{2,1,0:T(8,128)(2,1)}, u32[]{:S(2)}) copy-start(bf16[128,32,128]{2,1,0:T(8,128)(2,1)} %param.7) | copy-start | bytes 3145732
  6.5 44.7 %all-gather.10.cloned.1.call-start = ((), (), s32[]{:S(2)}) async-start(), calls=%async_computation.4 | async-start | bytes 2228224 | tf_op jit(solution)/shard_map/all_gather | solution.py:61
  8.2 94.6 %all-gather.6.cloned.1.call-start = ((), (), s32[]{:S(2)}) async-start(), calls=%async_computation.2 | async-start | bytes 4456448 | tf_op jit(solution)/shard_map/all_gather | solution.py:47
  10.0 147.9 %all-gather.8.cloned.1.call-start = ((), (), s32[]{:S(2)}) async-start(), calls=%async_computation.3 | async-start | bytes 4456448 | tf_op jit(solution)/shard_map/all_gather | solution.py:48
  11.8 184.7 %all-gather.12.cloned.1.call-start = ((), (), s32[]{:S(2)}) async-start(), calls=%async_computation.5 | async-start | bytes 2228224 | tf_op jit(solution)/shard_map/all_gather | solution.py:62
  13.5 328.9 %all-gather.14.cloned.1.call-start = ((), (), s32[]{:S(2)}) async-start(), calls=%async_computation.6 | async-start | bytes 17825792 | tf_op jit(solution)/shard_map/all_gather | solution.py:71
  196.5 242.7 %copy-start.1 = (bf16[128,32,128]{2,1,0:T(8,128)(2,1)S(1)}, bf16[128,32,128]{2,1,0:T(8,128)(2,1)}, u32[]{:S(2)}) copy-start(bf16[128,32,128]{2,1,0:T(8,128)(2,1)} %param.7) | copy-start | bytes 3145732
  212.7 226.4 %reduce-scatter.2.cloned.1.call-start = ((), (), s32[]{:S(2)}) async-start(), calls=%async_computation.7 | async-start | bytes 3145728 | tf_op jit(solution)/shard_map/reduce_scatter | solution.py:78
Sparse Core Ops, SparseCore 0:
  9.5 41.6 all-gather.9
  53.4 49.3 all-gather.5
  105.0 49.0 all-gather.7
  156.1 40.3 all-gather.11
  212.8 129.5 all-gather.13
  407.6 31.5 reduce-scatter.1
where the time goes:
time: 449 us; the launch traced here: 446 us
  waiting for transfers between devices  232 us (52%)
  matrix products  99 us (22%)
  blocking collectives  49.8 us (11%)
  other arithmetic  38.1 us (8%)
  between operations  13.6 us (3%)
  local copies, waits for them, and re-layouts  13.5 us (3%)
    all_gather x1, waiting for transfers between devices, on_device(): lax.all_gather(attended, 'ctx', axis=0, tiled=True)  130 us
    all_to_all x1, blocking collectives, on_device(): lax.all_to_all(row_partials.astype(jnp.bfloat16), 'ctx', split_axis=0, co...  49.8 us
    dot_general x2, matrix products, absorb(): jnp.einsum('rkgd,skd->kgrs', query_block, keys, preferred_element_type=jn...  43.1 us
    dot_general x2, matrix products, absorb(): jnp.einsum('kgrs,skd->kgrd', weights.astype(jnp.bfloat16), values, prefer...  42.2 us
    reduce_sum x2, other arithmetic, absorb(): total = jnp.sum(weights, axis=-1)  37.1 us
    all_gather x1, waiting for transfers between devices, on_device(): keys = lax.all_gather(new_keys, 'ctx', axis=0, tiled=True)  36.5 us
    reduce_scatter x1, waiting for transfers between devices, on_device(): lax.psum_scatter(regrouped.astype(jnp.bfloat16), 'head', scatter_dimensio...  31.7 us
    all_gather x1, waiting for transfers between devices, on_device(): keys = lax.all_gather(pool_keys, 'ctx', axis=0, tiled=True)  21.2 us
  transfers between devices with their start and end apart: 6, of which 5 were waited for; matrix products, arithmetic and copies ran while one was open for 26% of the time, Pallas kernels for 0%

commit v1 on v0

v1 whole, which is shorter than its diff:
```python
import functools
import math

import jax
import jax.numpy as jnp
from jax import lax
from jax.experimental import pallas as pl
from jax.experimental.pallas import tpu as pltpu
from jax.sharding import PartitionSpec as P

CORES = 2
LINES = 2
NEG = -1e30
VMEM_LIMIT = 48 * 1024 * 1024


def cycle_of(sites):
    length = sites // LINES
    order = []
    for line in range(LINES):
        steps = range(length) if line % 2 == 0 else range(length - 1, -1, -1)
        order += [z * LINES + line for z in steps]
    return order


def place_of(site, sites):
    z, line = site // LINES, site % LINES
    length = sites // LINES
    return jnp.where(line == 0, z, 2 * length - 1 - z)


def site_perm(sites, shift):
    order = cycle_of(sites)
    return [
        (order[i] * CORES + k, order[(i + shift) % sites] * CORES + k)
        for i in range(sites)
        for k in range(CORES)
    ]


def core_swap(x, count):
    return lax.ppermute(x, "ctx", [(i, i ^ 1) for i in range(count)])


def ring_gather(block, sites):
    ahead = site_perm(sites, 1)
    back = site_perm(sites, -1)
    blocks = {0: [block]}
    f = b = block
    for step in range(1, (sites - 1) // 2 + 1):
        f = lax.ppermute(f, "ctx", ahead)
        b = lax.ppermute(b, "ctx", back)
        blocks[step] = [f]
        blocks[sites - step] = [b]
    if sites % 2 == 0:
        half = block.shape[0] // 2
        blocks[sites // 2] = [
            lax.ppermute(f[:half], "ctx", ahead),
            lax.ppermute(b[half:], "ctx", back),
        ]
    return blocks


def pack_kernel(slots, pages_ref, me_ref, nk_ref, nv_ref, pk_ref, pv_ref, out_ref):
    rows = nk_ref.shape[0]
    page = pk_ref.shape[1]
    kept = (out_ref.shape[0] // 2 - rows) // page
    half = out_ref.shape[0] // 2
    out_ref[...] = jnp.zeros_like(out_ref)
    out_ref[0:rows, :] = nk_ref[...]
    out_ref[half : half + rows, :] = nv_ref[...]
    me = me_ref[0]

    def one(p, count):
        slot = pages_ref[p]
        mine = slot // slots == me

        @pl.when(jnp.logical_and(mine, count < kept))
        def _():
            local = slot % slots
            at = pl.multiple_of(rows + count * page, page)
            out_ref[pl.ds(at, page), :] = pk_ref[local]
            out_ref[pl.ds(pl.multiple_of(half + at, page), page), :] = pv_ref[local]

        return count + mine.astype(jnp.int32)

    lax.fori_loop(0, pages_ref.shape[0], one, jnp.int32(0))


def attend_kernel(cfg, pages_ref, me_ref, q_ref, *refs):
    n, rows, kvheads, group, width, page, slots, kept, key_block = cfg
    sites = n // CORES
    length = sites // LINES
    ins, (o_ref, kbuf, vbuf, table, counts, sem) = refs[:-6], refs[-6:]
    npages = pages_ref.shape[0]
    prefix = npages * page
    me = me_ref[0]
    my_site, my_core = me // CORES, me % CORES
    my_place = jnp.where(my_site % LINES == 0, my_site // LINES, 2 * length - 1 - my_site // LINES)

    for i in range(n):
        counts[i] = 0

    def note(p, _):
        owner = pages_ref[p] // slots
        j = counts[owner]
        table[owner * kept + jnp.minimum(j, kept - 1)] = p
        counts[owner] = j + 1
        return 0

    lax.fori_loop(0, npages, note, 0)

    def copies(go):
        for d in range(sites):
            for swap in range(CORES):
                k_ref, k_at, v_ref, v_at = ins[d * CORES + swap]
                place = lax.rem(my_place + sites - d, sites)
                line = place // length
                z = jnp.where(line == 0, place, 2 * length - 1 - place)
                owner = (z * LINES + line) * CORES + lax.rem(my_core + swap, CORES)
                at = pl.multiple_of(prefix + owner * rows, rows)
                for src, off, dst in ((k_ref, k_at, kbuf), (v_ref, v_at, vbuf)):
                    go(src.at[pl.ds(off, rows)], dst.at[pl.ds(at, rows)])
                for j in range(kept):

                    @pl.when(j < counts[owner])
                    def _():
                        to = pl.multiple_of(table[owner * kept + j] * page, page)
                        for src, off, dst in ((k_ref, k_at, kbuf), (v_ref, v_at, vbuf)):
                            go(src.at[pl.ds(off + rows + j * page, page)], dst.at[pl.ds(to, page)])

    copies(lambda s, t: pltpu.make_async_copy(s, t, sem).start())
    copies(lambda s, t: pltpu.make_async_copy(s, t, sem).wait())

    pair = 2 if group % 2 == 0 else 1
    scale = math.log2(math.e) * width ** (-0.5)
    seen_all = prefix + me * rows
    full = seen_all // key_block

    def one(index, _):
        h = index // (group // pair)
        first = index * pair
        lane = pl.multiple_of(h * width, width)
        q = jnp.concatenate(
            [
                q_ref[:, pl.ds(pl.multiple_of((first + g) * width, width), width)]
                for g in range(pair)
            ],
            axis=0,
        )

        def step(kb, carry, masked):
            top, total, acc = carry
            at = pl.multiple_of(kb * key_block, key_block)
            k = kbuf[pl.ds(at, key_block), pl.ds(lane, width)]
            v = vbuf[pl.ds(at, key_block), pl.ds(lane, width)]
            s = lax.dot_general(q, k, (((1,), (1,)), ((), ())), preferred_element_type=jnp.float32)
            if masked:
                shape = (rows, key_block)
                row = lax.broadcasted_iota(jnp.int32, shape, 0)
                col = lax.broadcasted_iota(jnp.int32, shape, 1)
                seen = col - row <= seen_all - at
                seen = jnp.concatenate([seen] * pair, axis=0)
                s = jnp.where(seen, s, NEG)
            fresh = jnp.maximum(top, jnp.max(s, axis=1, keepdims=True))
            w = jnp.exp2((s - fresh) * scale)
            left = jnp.exp2((top - fresh) * scale)
            total = total * left + jnp.sum(w, axis=1, keepdims=True)
            acc = acc * left + jnp.dot(
                w.astype(jnp.bfloat16), v, preferred_element_type=jnp.float32
            )
            return fresh, total, acc

        carry = (
            jnp.full((pair * rows, 1), NEG, jnp.float32),
            jnp.zeros((pair * rows, 1), jnp.float32),
            jnp.zeros((pair * rows, width), jnp.float32),
        )
        carry = lax.fori_loop(0, full, lambda kb, c: step(kb, c, False), carry)
        top, total, acc = step(full, carry, True)
        out = (acc / total).astype(jnp.bfloat16)
        for g in range(pair):
            o_ref[:, pl.ds(pl.multiple_of((first + g) * width, width), width)] = out[
                g * rows : (g + 1) * rows
            ]
        return 0

    lax.fori_loop(0, kvheads * group // pair, one, 0)


def on_device(n, heads, queries, new_keys, new_values, pool_keys, pool_values, o_weight, page_list):
    rows, qheads, width = queries.shape
    kvheads = new_keys.shape[1]
    group = qheads // kvheads
    slots, page = pool_keys.shape[:2]
    npages = page_list.shape[0]
    kept = min(slots, 2 * npages // n)
    wide = kvheads * width
    sites = n // CORES
    me = lax.axis_index("ctx")
    head = lax.axis_index("head")
    me_ref = me.reshape(1)
    smem = pl.BlockSpec(memory_space=pltpu.SMEM)
    vmem = pl.BlockSpec(memory_space=pltpu.VMEM)
    hbm = pl.BlockSpec(memory_space=pl.ANY)

    half = rows + kept * page
    payload = pl.pallas_call(
        functools.partial(pack_kernel, slots),
        out_shape=jax.ShapeDtypeStruct((2 * half, wide), jnp.bfloat16),
        in_specs=[smem, smem, vmem, vmem, vmem, vmem],
        out_specs=vmem,
        name="pack_pages",
    )(
        page_list,
        me_ref,
        new_keys.reshape(rows, wide),
        new_values.reshape(rows, wide),
        pool_keys.reshape(slots, page, wide),
        pool_values.reshape(slots, page, wide),
    )
    w_other = core_swap(o_weight, n)
    gathered = ring_gather(payload, sites)
    operands, spots = [], []
    for d in range(sites):
        for swap in range(CORES):
            pieces = gathered[d]
            if swap:
                pieces = [core_swap(p, n) for p in pieces]
            base = len(operands)
            operands += pieces
            spots.append((base, 0, base, half) if len(pieces) == 1 else (base, 0, base + 1, 0))

    total_keys = npages * page + n * rows
    key_block = math.gcd(total_keys, 512)
    cfg = (n, rows, kvheads, group, width, page, slots, kept, key_block)

    def attend(pages_ref, me_ref, q_ref, *refs):
        ins = [(refs[a], b, refs[c], e) for a, b, c, e in spots]
        attend_kernel(cfg, pages_ref, me_ref, q_ref, *ins, *refs[len(operands) :])

    attended = pl.pallas_call(
        attend,
        out_shape=jax.ShapeDtypeStruct((rows, qheads * width), jnp.bfloat16),
        in_specs=[smem, smem, vmem] + [hbm] * len(operands),
        out_specs=vmem,
        scratch_shapes=[
            pltpu.VMEM((total_keys, wide), jnp.bfloat16),
            pltpu.VMEM((total_keys, wide), jnp.bfloat16),
            pltpu.SMEM((n * kept,), jnp.int32),
            pltpu.SMEM((n,), jnp.int32),
            pltpu.SemaphoreType.DMA,
        ],
        compiler_params=pltpu.CompilerParams(vmem_limit_bytes=VMEM_LIMIT),
        cost_estimate=pl.CostEstimate(
            flops=4 * rows * qheads * width * total_keys,
            bytes_accessed=8 * total_keys * wide,
            transcendentals=rows * qheads * total_keys,
        ),
        name="attend",
    )(page_list, me_ref, queries.reshape(rows, qheads * width), *operands)

    blocks = ring_gather(attended, sites)
    cols = o_weight.shape[1]
    place = place_of(me // CORES, sites)

    def product(pieces):
        parts = []
        for w in (o_weight, w_other):
            out = [jnp.dot(p, w, preferred_element_type=jnp.float32) for p in pieces]
            parts.append(out[0] if len(out) == 1 else jnp.concatenate(out, axis=0))
        return parts

    part_rows = rows // heads
    summed = {}
    for d in range(sites):
        own, other = product(blocks[d])
        full = jnp.concatenate([own, other], axis=1)
        mine = lax.dynamic_slice_in_dim(full, head * part_rows, part_rows, 0)
        sent = full.astype(jnp.bfloat16)
        if heads == 2:
            away = lax.dynamic_slice_in_dim(sent, (1 - head) * part_rows, part_rows, 0)
            got = lax.ppermute(away, "head", [(0, 1), (1, 0)])
            summed[d] = (mine + got.astype(jnp.float32)).astype(jnp.bfloat16)
        else:
            summed[d] = lax.psum_scatter(sent, "head", scatter_dimension=0, tiled=True)

    returned = []
    for d in range(sites):
        back = summed[d]
        if d:
            back = lax.ppermute(back, "ctx", site_perm(sites, -d))
        returned.append(back)
    stack = jnp.stack(returned, axis=0)
    order = jnp.stack([jnp.mod(place_of(jnp.int32(s), sites) - place, sites) for s in range(sites)])
    stack = jnp.take(stack, order, axis=0)
    stack = stack.reshape(sites, part_rows, CORES, cols)
    stack = jnp.where(me % CORES == 0, stack, stack[:, :, ::-1])
    stack = stack.transpose(1, 0, 2, 3).reshape(part_rows, sites * CORES * cols)
    return lax.all_to_all(stack, "head", split_axis=1, concat_axis=0, tiled=True)


def solution(mesh):
    n, heads = mesh.shape["ctx"], mesh.shape["head"]
    in_specs = (
        P("ctx", "head", None),
        P("ctx", "head", None),
        P("ctx", "head", None),
        P("ctx", None, "head", None),
        P("ctx", None, "head", None),
        P("head", "ctx"),
        P(),
    )
    out_specs = P("ctx", "head")
    return jax.shard_map(
        functools.partial(on_device, n, heads),
        mesh=mesh,
        in_specs=in_specs,
        out_specs=out_specs,
        check_vma=False,
    )
```

time: 449 us -> 279 us (0.62)
  waiting for transfers between devices: 232 us -> 110 us
  matrix products: 99 us -> 36.1 us
  starting transfers between devices: 0.21 us -> 61.9 us
  blocking collectives: 49.8 us -> 10.5 us
  Pallas kernels: 0 us -> 37.4 us
  other arithmetic: 38.1 us -> 2.78 us
  between operations: 13.6 us -> 0.59 us
  local copies, waits for them, and re-layouts: 13.5 us -> 18.1 us
    all_gather x5 -> x0, waiting for transfers between devices: 200 us -> none  [the longest x1 130 us: on_device(): lax.all_gather(attended, 'ctx', axis=0, tiled=True)]
    ppermute x0 -> x41, waiting for transfers between devices: none -> 110 us  [the longest x6 64.8 us: ring_gather(): f = lax.ppermute(f, 'ctx', ahead)]
    dot_general x5 -> x18, matrix products: 99 us -> 36.1 us  [product(): out = [jnp.dot(p, w, preferred_element_type=jnp.float32) for p in pieces]]
    ppermute x0 -> x41, starting transfers between devices: none -> 61.9 us  [the longest x6 21.7 us: ring_gather(): b = lax.ppermute(b, 'ctx', back)]
    all_to_all x1, blocking collectives: 49.8 us -> 10.5 us  [on_device(): lax.all_to_all(stack, 'head', split_axis=1, concat_axis=0, tiled=True)]
    pallas_call x0 -> x2, Pallas kernels: none -> 37.4 us  [the longest x1 34.8 us: on_device(): pl.pallas_call(attend, out_shape=jax.ShapeDtypeStruct((rows, qheads * wid...]
    reduce_sum x2 -> x0, other arithmetic: 37.1 us -> none  [absorb(): total = jnp.sum(weights, axis=-1)]
    reduce_scatter x1 -> x0, waiting for transfers between devices: 31.7 us -> none  [on_device(): lax.psum_scatter(regrouped.astype(jnp.bfloat16), 'head', scatter_dimensio...]
  transfers between devices with their start and end apart: 6 -> 41, of which waited for: 5 -> 15; matrix products, arithmetic and copies ran while one was open for 26% -> 14% of each run, Pallas kernels for 0% -> 13%
where the time goes in v1:
time: 279 us; the launch traced here: 277 us
  waiting for transfers between devices  110 us (39%)
  starting transfers between devices  61.9 us (22%)
  Pallas kernels  37.4 us (13%)
  matrix products  36.1 us (13%)
  local copies, waits for them, and re-layouts  18.1 us (6%)
  blocking collectives  10.5 us (4%)
    ppermute x6, waiting for transfers between devices, ring_gather(): f = lax.ppermute(f, 'ctx', ahead)  64.8 us
    dot_general x18, matrix products, product(): out = [jnp.dot(p, w, preferred_element_type=jnp.float32) for p in pieces]  36.1 us
    pallas_call x1, Pallas kernels, on_device(): pl.pallas_call(attend, out_shape=jax.ShapeDtypeStruct((rows, qheads * wid...  34.8 us
    ppermute x7, waiting for transfers between devices, on_device(): back = lax.ppermute(back, 'ctx', site_perm(sites, -d))  29.6 us
    ppermute x6, starting transfers between devices, ring_gather(): b = lax.ppermute(b, 'ctx', back)  21.7 us
    ppermute x7, starting transfers between devices, on_device(): back = lax.ppermute(back, 'ctx', site_perm(sites, -d))  14.2 us
    ppermute x6, starting transfers between devices, ring_gather(): f = lax.ppermute(f, 'ctx', ahead)  11.4 us
    all_to_all x1, blocking collectives, on_device(): lax.all_to_all(stack, 'head', split_axis=1, concat_axis=0, tiled=True)  10.5 us
  transfers between devices with their start and end apart: 41, of which 15 were waited for; matrix products, arithmetic and copies ran while one was open for 14% of the time, Pallas kernels for 13%

profile of v1, /device:TPU:6, one launch (start us, length us, event | category | flops | bytes accessed | tf_op | source)
XLA Modules:
  0.0 276.9 jit_solution(7235277773882250099)
XLA Ops:
  0.0 1.8 reshape.378.pk_ref
  1.8 1.7 reshape.379.pv_ref
  3.6 1.7 copy_bitcast_fusion.1
  5.3 2.7 pack_pages.1.refs_0_
  8.5 1.5 collective-permute-start.8
  10.0 11.9 %collective-permute-done.1.refs_2_ = bf16[512,512]{1,0:T(8,128)(2,1)S(1)} collective-permute-done((bf16[512,512]{1,0:T(8,128)(2,1)}, bf16[512,512]{1,0:T(8,128)(2,1)S(1)}, u32[]{:S(2)}, u32[]{:S(2)}) %collective-permute-start.1) | collective-permute-done | bytes 524320 | tf_op jit(solution)/shard_map/ppermute | solution.py:51
  22.4 1.5 collective-permute-start.9
  24.4 10.3 %collective-permute-done.3.refs_4_ = bf16[512,512]{1,0:T(8,128)(2,1)S(1)} collective-permute-done((bf16[512,512]{1,0:T(8,128)(2,1)S(1)}, bf16[512,512]{1,0:T(8,128)(2,1)S(1)}, u32[]{:S(2)}, u32[]{:S(2)}) %collective-permute-start.3) | collective-permute-done | bytes 524320 | tf_op jit(solution)/shard_map/ppermute | solution.py:51
  35.1 1.6 collective-permute-start.10
  37.2 9.4 %collective-permute-done.5.refs_6_ = bf16[512,512]{1,0:T(8,128)(2,1)S(1)} collective-permute-done((bf16[512,512]{1,0:T(8,128)(2,1)S(1)}, bf16[512,512]{1,0:T(8,128)(2,1)S(1)}, u32[]{:S(2)}, u32[]{:S(2)}) %collective-permute-start.5) | collective-permute-done | bytes 524320 | tf_op jit(solution)/shard_map/ppermute | solution.py:51
  47.2 1.3 collective-permute-start.7
  49.8 5.8 %collective-permute-done.7.refs_8_ = bf16[256,512]{1,0:T(8,128)(2,1)S(1)} collective-permute-done((bf16[256,512]{1,0:T(8,128)(2,1)S(1)}, bf16[256,512]{1,0:T(8,128)(2,1)S(1)}, u32[]{:S(2)}, u32[]{:S(2)}) %collective-permute-start.7) | collective-permute-done | bytes 262176 | tf_op jit(solution)/shard_map/ppermute | solution.py:58
  55.5 1.4 collective-permute-done.11.refs_9_
  56.9 1.4 copy.22
  60.3 34.8 %attend.1 = bf16[128,4096]{1,0:T(8,128)(2,1)} custom-call(s32[32]{0:T(128)S(1)} %copy-done.1, s32[1]{0:T(128)} %bitcast.8.me_ref, bf16[128,4096]{1,0:T(8,128)(2,1)} %bitcast.90, bf16[512,512]{1,0:T(8,128)(2,1)S(1)} %copy-done, bf16[512,512]{1,0:T(8,128)(2,1)S(1)} %collective-permute-done.refs_1_, bf16[512,512]{1,0:T(8,128)(2,1)S(1)} %collective-permute-done.1.refs_2_, ...), custom_call_target="tpu_custom_call" | custom-call | flops 6442450944 | bytes 12582912 | tf_op jit(solution)/shard_map/attend/pallas_call | solution.py:242
  95.0 1.6 collective-permute-start.19
  96.7 6.8 %collective-permute-start.29 = (bf16[128,4096]{1,0:T(8,128)(2,1)}, bf16[128,4096]{1,0:T(8,128)(2,1)S(1)}, u32[]{:S(2)}, u32[]{:S(2)}) collective-permute-start(bf16[128,4096]{1,0:T(8,128)(2,1)} %attend.1), channel_id=1, source_target_pairs={{0,4},{2,6},{8,0},{10,2},{16,8},{18,10},{24,16},{26,18},{28,24},{3... | collective-permute-start | bytes 3145736 | tf_op jit(solution)/shard_map/ppermute | solution.py:52
  103.6 3.4 %fusion.39 = f32[128,512]{1,0:T(8,128)S(1)} fusion(bf16[128,4096]{1,0:T(8,128)(2,1)} %attend.1, bf16[4096,512]{1,0:T(8,128)(2,1)} %param.12), kind=kOutput, calls=%fused_computation.87 | convolution fusion | flops 536870912 | bytes 5505024 | tf_op jit(solution)/shard_map/dot_general | solution.py:270
  107.0 20.1 %collective-permute-done.19 = bf16[128,4096]{1,0:T(8,128)(2,1)S(1)} collective-permute-done((bf16[128,4096]{1,0:T(8,128)(2,1)}, bf16[128,4096]{1,0:T(8,128)(2,1)S(1)}, u32[]{:S(2)}, u32[]{:S(2)}) %collective-permute-start.19) | collective-permute-done | bytes 1048608 | tf_op jit(solution)/shard_map/ppermute | solution.py:51
  127.1 2.5 collective-permute-start.22
  130.0 6.1 %collective-permute-start.30 = (bf16[128,4096]{1,0:T(8,128)(2,1)S(1)}, bf16[128,4096]{1,0:T(8,128)(2,1)S(1)}, u32[]{:S(2)}, u32[]{:S(2)}) collective-permute-start(bf16[128,4096]{1,0:T(8,128)(2,1)S(1)} %collective-permute-done.29), channel_id=1, source_target_pairs={{0,4},{2,6},{8,0},{10,2},{16,8},{18,10},{24,16},{26,18},{28,24},{3... | collective-permute-start | bytes 3145736 | tf_op jit(solution)/shard_map/ppermute | solution.py:52
  137.7 3.0 %fusion.40 = f32[128,512]{1,0:T(8,128)S(1)} fusion(bf16[128,4096]{1,0:T(8,128)(2,1)S(1)} %copy-done.3, bf16[4096,512]{1,0:T(8,128)(2,1)} %collective-permute-done.17), kind=kOutput, calls=%fused_computation.88 | convolution fusion | flops 536870912 | bytes 5505024 | tf_op jit(solution)/shard_map/dot_general | solution.py:270
  141.3 2.9 %fusion.42 = f32[128,512]{1,0:T(8,128)S(1)} fusion(bf16[128,4096]{1,0:T(8,128)(2,1)S(1)} %collective-permute-done.19, bf16[4096,512]{1,0:T(8,128)(2,1)} %collective-permute-done.17), kind=kOutput, calls=%fused_computation.90 | convolution fusion | flops 536870912 | bytes 5505024 | tf_op jit(solution)/shard_map/dot_general | solution.py:270
  144.2 1.6 collective-permute-start.20
  145.8 13.2 %collective-permute-done.22 = bf16[128,4096]{1,0:T(8,128)(2,1)S(1)} collective-permute-done((bf16[128,4096]{1,0:T(8,128)(2,1)S(1)}, bf16[128,4096]{1,0:T(8,128)(2,1)S(1)}, u32[]{:S(2)}, u32[]{:S(2)}) %collective-permute-start.22) | collective-permute-done | bytes 1048608 | tf_op jit(solution)/shard_map/ppermute | solution.py:51
  159.7 3.0 %fusion.44 = f32[128,512]{1,0:T(8,128)S(1)} fusion(bf16[128,4096]{1,0:T(8,128)(2,1)S(1)} %collective-permute-done.22, bf16[4096,512]{1,0:T(8,128)(2,1)} %collective-permute-done.17), kind=kOutput, calls=%fused_computation.92 | convolution fusion | flops 536870912 | bytes 5505024 | tf_op jit(solution)/shard_map/dot_general | solution.py:270
  164.0 3.0 %fusion.54 = f32[128,512]{1,0:T(8,128)S(1)} fusion(bf16[128,4096]{1,0:T(8,128)(2,1)S(1)} %collective-permute-done.30, bf16[4096,512]{1,0:T(8,128)(2,1)} %collective-permute-done.17), kind=kOutput, calls=%fused_computation.102 | convolution fusion | flops 536870912 | bytes 5505024 | tf_op jit(solution)/shard_map/dot_general | solution.py:270
  167.0 1.6 collective-permute-start.37
  168.6 2.9 %fusion.56 = f32[128,512]{1,0:T(8,128)S(1)} fusion(bf16[128,4096]{1,0:T(8,128)(2,1)S(1)} %collective-permute-done.29, bf16[4096,512]{1,0:T(8,128)(2,1)} %collective-permute-done.17), kind=kOutput, calls=%fused_computation.104 | convolution fusion | flops 536870912 | bytes 5505024 | tf_op jit(solution)/shard_map/dot_general | solution.py:270
  172.1 5.9 %collective-permute-start.25 = (bf16[128,4096]{1,0:T(8,128)(2,1)S(1)}, bf16[128,4096]{1,0:T(8,128)(2,1)S(1)}, u32[]{:S(2)}, u32[]{:S(2)}) collective-permute-start(bf16[128,4096]{1,0:T(8,128)(2,1)S(1)} %collective-permute-done.22), channel_id=1, source_target_pairs={{0,8},{2,10},{8,16},{10,18},{16,24},{18,26},{24,28},{26,30},{28,20... | collective-permute-start | bytes 3145736 | tf_op jit(solution)/shard_map/ppermute | solution.py:51
  178.0 4.2 %collective-permute-start.31 = (bf16[128,4096]{1,0:T(8,128)(2,1)S(1)}, bf16[128,4096]{1,0:T(8,128)(2,1)S(1)}, u32[]{:S(2)}, u32[]{:S(2)}) collective-permute-start(bf16[128,4096]{1,0:T(8,128)(2,1)S(1)} %collective-permute-done.30), channel_id=1, source_target_pairs={{0,4},{2,6},{8,0},{10,2},{16,8},{18,10},{24,16},{26,18},{28,24},{3... | collective-permute-start | bytes 3145736 | tf_op jit(solution)/shard_map/ppermute | solution.py:52
  182.3 2.1 collective-permute-start.21
  184.4 2.8 %collective-permute-start.24 = (bf16[64,1024]{1,0:T(8,128)(2,1)S(1)}, bf16[64,1024]{1,0:T(8,128)(2,1)S(1)}, u32[]{:S(2)}, u32[]{:S(2)}) collective-permute-start(bf16[64,1024]{1,0:T(8,128)(2,1)S(1)} %fusion.25), channel_id=1, source_target_pairs={{0,12},{2,14},{8,4},{10,6},{16,0},{18,2},{24,8},{26,10},{28,16},{3... | collective-permute-start | bytes 393224 | tf_op jit(solution)/shard_map/ppermute | solution.py:292
  187.5 21.2 %collective-permute-done.21 = bf16[64,1024]{1,0:T(8,128)(2,1)S(1)} collective-permute-done((bf16[64,1024]{1,0:T(8,128)(2,1)S(1)}, bf16[64,1024]{1,0:T(8,128)(2,1)S(1)}, u32[]{:S(2)}, u32[]{:S(2)}) %collective-permute-start.21) | collective-permute-done | bytes 131104 | tf_op jit(solution)/shard_map/ppermute | solution.py:292
  208.7 1.1 collective-permute-start.40
  211.5 2.9 %fusion.46 = f32[128,512]{1,0:T(8,128)S(1)} fusion(bf16[128,4096]{1,0:T(8,128)(2,1)S(1)} %collective-permute-done.25, bf16[4096,512]{1,0:T(8,128)(2,1)} %collective-permute-done.17), kind=kOutput, calls=%fused_computation.94 | convolution fusion | flops 536870912 | bytes 5505024 | tf_op jit(solution)/shard_map/dot_general | solution.py:270
  214.4 1.6 collective-permute-start.26
  216.0 3.0 %collective-permute-start.32 = (bf16[64,4096]{1,0:T(8,128)(2,1)S(1)}, bf16[64,4096]{1,0:T(8,128)(2,1)S(1)}, u32[]{:S(2)}, u32[]{:S(2)}) collective-permute-start(bf16[64,4096]{1,0:T(8,128)(2,1)S(1)} %slice.21), channel_id=1, source_target_pairs={{0,4},{2,6},{8,0},{10,2},{16,8},{18,10},{24,16},{26,18},{28,24},{3... | collective-permute-start | bytes 1572872 | tf_op jit(solution)/shard_map/ppermute | solution.py:59
  219.8 3.0 %fusion.52 = f32[128,512]{1,0:T(8,128)S(1)} fusion(bf16[128,4096]{1,0:T(8,128)(2,1)S(1)} %collective-permute-done.31, bf16[4096,512]{1,0:T(8,128)(2,1)} %collective-permute-done.17), kind=kOutput, calls=%fused_computation.100 | convolution fusion | flops 536870912 | bytes 5505024 | tf_op jit(solution)/shard_map/dot_general | solution.py:270
  223.4 3.2 %collective-permute-done.32 = bf16[64,4096]{1,0:T(8,128)(2,1)S(1)} collective-permute-done((bf16[64,4096]{1,0:T(8,128)(2,1)S(1)}, bf16[64,4096]{1,0:T(8,128)(2,1)S(1)}, u32[]{:S(2)}, u32[]{:S(2)}) %collective-permute-start.32) | collective-permute-done | bytes 524320 | tf_op jit(solution)/shard_map/ppermute | solution.py:59
  226.6 7.5 %collective-permute-start.27 = (bf16[64,1024]{1,0:T(8,128)(2,1)S(1)}, bf16[64,1024]{1,0:T(8,128)(2,1)S(1)}, u32[]{:S(2)}, u32[]{:S(2)}) collective-permute-start(bf16[64,1024]{1,0:T(8,128)(2,1)S(1)} %fusion.20), channel_id=1, source_target_pairs={{0,20},{2,22},{8,12},{10,14},{16,4},{18,6},{24,0},{26,2},{28,8},{3... | collective-permute-start | bytes 393224 | tf_op jit(solution)/shard_map/ppermute | solution.py:292
  234.1 3.0 %fusion.50 = f32[64,512]{1,0:T(8,128)S(1)} fusion(bf16[64,4096]{1,0:T(8,128)(2,1)S(1)} %collective-permute-done.32, bf16[4096,512]{1,0:T(8,128)(2,1)} %collective-permute-done.17), kind=kOutput, calls=%fused_computation.98 | convolution fusion | flops 268435456 | bytes 4849664 | tf_op jit(solution)/shard_map/dot_general | solution.py:270
  238.0 3.0 %fusion.49 = f32[64,512]{1,0:T(8,128)S(1)} fusion(bf16[64,4096]{1,0:T(8,128)(2,1)S(1)} %collective-permute-done.28, bf16[4096,512]{1,0:T(8,128)(2,1)} %collective-permute-done.17), kind=kOutput, calls=%fused_computation.97 | convolution fusion | flops 268435456 | bytes 4849664 | tf_op jit(solution)/shard_map/dot_general | solution.py:270
  242.8 4.2 %collective-permute-done.33 = bf16[64,1024]{1,0:T(8,128)(2,1)S(1)} collective-permute-done((bf16[64,1024]{1,0:T(8,128)(2,1)S(1)}, bf16[64,1024]{1,0:T(8,128)(2,1)S(1)}, u32[]{:S(2)}, u32[]{:S(2)}) %collective-permute-start.33) | collective-permute-done | bytes 131104 | tf_op jit(solution)/shard_map/ppermute | solution.py:283
  247.2 7.6 %collective-permute-done.34 = bf16[64,1024]{1,0:T(8,128)(2,1)S(1)} collective-permute-done((bf16[64,1024]{1,0:T(8,128)(2,1)S(1)}, bf16[64,1024]{1,0:T(8,128)(2,1)S(1)}, u32[]{:S(2)}, u32[]{:S(2)}) %collective-permute-start.34) | collective-permute-done | bytes 131104 | tf_op jit(solution)/shard_map/ppermute | solution.py:292
  257.3 5.5 %rev.3 = bf16[8,64,2,512]{3,2,0,1:T(2,128)(2,1)S(1)} reverse(bf16[8,64,2,512]{3,2,0,1:T(2,128)(2,1)S(1)} %broadcast_select_fusion), dimensions={2} | reverse | bytes 2097152 | tf_op jit(solution)/shard_map/rev | solution.py:298
  262.8 1.3 fusion
  265.4 10.5 %all_to_all.19 = bf16[64,2,4096]{2,0,1:T(8,128)(2,1)S(1)} all-to-all(bf16[64,2,4096]{2,0,1:T(8,128)(2,1)S(1)} %copy.12), channel_id=1, replica_groups=mesh['ctx'=16,'head'=2] {'head'}, dimensions={1} | all-to-all | bytes 2097152 | tf_op jit(solution)/shard_map/all_to_all | solution.py:300
  (120 shorter events, 22.8 us)
Async XLA Ops:
  0.0 59.2 %copy-start.1 = (s32[32]{0:T(128)S(1)}, s32[32]{0:T(128)}, u32[]{:S(2)}) copy-start(s32[32]{0:T(128)} %pages_ref.3) | copy-start | bytes 388
  0.0 56.9 %copy-start.4 = (bf16[128,32,128]{2,1,0:T(8,128)(2,1)S(1)}, bf16[128,32,128]{2,1,0:T(8,128)(2,1)}, u32[]{:S(2)}) copy-start(bf16[128,32,128]{2,1,0:T(8,128)(2,1)} %param.7) | copy-start | bytes 3145732
  8.0 13.9 %collective-permute-start.1 = (bf16[512,512]{1,0:T(8,128)(2,1)}, bf16[512,512]{1,0:T(8,128)(2,1)S(1)}, u32[]{:S(2)}, u32[]{:S(2)}) collective-permute-start(bf16[512,512]{1,0:T(8,128)(2,1)} %pack_pages.1.refs_0_), channel_id=1, source_target_pairs={{0,8},{2,10},{8,16},{10,18},{16,24},{18,26},{24,28},{26,30},{28,20... | collective-permute-start | bytes 1572872 | tf_op jit(solution)/shard_map/ppermute | solution.py:51
  8.5 13.9 %collective-permute-start.8 = (bf16[512,512]{1,0:T(8,128)(2,1)}, bf16[512,512]{1,0:T(8,128)(2,1)S(1)}, u32[]{:S(2)}, u32[]{:S(2)}) collective-permute-start(bf16[512,512]{1,0:T(8,128)(2,1)} %pack_pages.1.refs_0_), channel_id=1, source_target_pairs={{0,4},{2,6},{8,0},{10,2},{16,8},{18,10},{24,16},{26,18},{28,24},{3... | collective-permute-start | bytes 1572872 | tf_op jit(solution)/shard_map/ppermute | solution.py:52
  21.9 12.8 %collective-permute-start.3 = (bf16[512,512]{1,0:T(8,128)(2,1)S(1)}, bf16[512,512]{1,0:T(8,128)(2,1)S(1)}, u32[]{:S(2)}, u32[]{:S(2)}) collective-permute-start(bf16[512,512]{1,0:T(8,128)(2,1)S(1)} %collective-permute-done.1.refs_2_), channel_id=1, source_target_pairs={{0,8},{2,10},{8,16},{10,18},{16,24},{18,26},{24,28},{26,30},{28,20... | collective-permute-start | bytes 1572872 | tf_op jit(solution)/shard_map/ppermute | solution.py:51
  22.4 36.1 %copy-start.5 = (bf16[512,512]{1,0:T(8,128)(2,1)}, bf16[512,512]{1,0:T(8,128)(2,1)S(1)}, u32[]{:S(2)}) copy-start(bf16[512,512]{1,0:T(8,128)(2,1)S(1)} %collective-permute-done.8.refs_16_) | copy-start | bytes 1572868
  22.4 12.8 %collective-permute-start.9 = (bf16[512,512]{1,0:T(8,128)(2,1)S(1)}, bf16[512,512]{1,0:T(8,128)(2,1)S(1)}, u32[]{:S(2)}, u32[]{:S(2)}) collective-permute-start(bf16[512,512]{1,0:T(8,128)(2,1)S(1)} %collective-permute-done.8.refs_16_), channel_id=1, source_target_pairs={{0,4},{2,6},{8,0},{10,2},{16,8},{18,10},{24,16},{26,18},{28,24},{3... | collective-permute-start | bytes 1572872 | tf_op jit(solution)/shard_map/ppermute | solution.py:52
  23.9 113.7 %collective-permute-start.17 = (bf16[4096,512]{1,0:T(8,128)(2,1)}, bf16[4096,512]{1,0:T(8,128)(2,1)}, u32[]{:S(2)}, u32[]{:S(2)}) collective-permute-start(bf16[4096,512]{1,0:T(8,128)(2,1)} %param.12), channel_id=1, source_target_pairs={{0,2},{2,0},{4,6},{6,4},{8,10},{10,8},{12,14},{14,12},{16,18},{18,... | collective-permute-start | bytes 12582920 | tf_op jit(solution)/shard_map/ppermute | solution.py:42
  23.9 12.8 %collective-permute-start = (bf16[512,512]{1,0:T(8,128)(2,1)}, bf16[512,512]{1,0:T(8,128)(2,1)S(1)}, u32[]{:S(2)}, u32[]{:S(2)}) collective-permute-start(bf16[512,512]{1,0:T(8,128)(2,1)} %pack_pages.1.refs_0_), channel_id=1, source_target_pairs={{0,2},{2,0},{4,6},{6,4},{8,10},{10,8},{12,14},{14,12},{16,18},{18,... | collective-permute-start | bytes 1572872 | tf_op jit(solution)/shard_map/ppermute | solution.py:42
  34.7 11.9 %collective-permute-start.5 = (bf16[512,512]{1,0:T(8,128)(2,1)S(1)}, bf16[512,512]{1,0:T(8,128)(2,1)S(1)}, u32[]{:S(2)}, u32[]{:S(2)}) collective-permute-start(bf16[512,512]{1,0:T(8,128)(2,1)S(1)} %collective-permute-done.3.refs_4_), channel_id=1, source_target_pairs={{0,8},{2,10},{8,16},{10,18},{16,24},{18,26},{24,28},{26,30},{28,20... | collective-permute-start | bytes 1572872 | tf_op jit(solution)/shard_map/ppermute | solution.py:51
  35.1 23.3 %copy-start.6 = (bf16[512,512]{1,0:T(8,128)(2,1)}, bf16[512,512]{1,0:T(8,128)(2,1)S(1)}, u32[]{:S(2)}) copy-start(bf16[512,512]{1,0:T(8,128)(2,1)S(1)} %collective-permute-done.9.refs_14_) | copy-start | bytes 1572868
  35.1 11.6 %collective-permute-start.10 = (bf16[512,512]{1,0:T(8,128)(2,1)S(1)}, bf16[512,512]{1,0:T(8,128)(2,1)S(1)}, u32[]{:S(2)}, u32[]{:S(2)}) collective-permute-start(bf16[512,512]{1,0:T(8,128)(2,1)S(1)} %collective-permute-done.9.refs_14_), channel_id=1, source_target_pairs={{0,4},{2,6},{8,0},{10,2},{16,8},{18,10},{24,16},{26,18},{28,24},{3... | collective-permute-start | bytes 1572872 | tf_op jit(solution)/shard_map/ppermute | solution.py:52
  36.7 10.4 %collective-permute-start.2 = (bf16[512,512]{1,0:T(8,128)(2,1)S(1)}, bf16[512,512]{1,0:T(8,128)(2,1)S(1)}, u32[]{:S(2)}, u32[]{:S(2)}) collective-permute-start(bf16[512,512]{1,0:T(8,128)(2,1)S(1)} %collective-permute-done.1.refs_2_), channel_id=1, source_target_pairs={{0,2},{2,0},{4,6},{6,4},{8,10},{10,8},{12,14},{14,12},{16,18},{18,... | collective-permute-start | bytes 1572872 | tf_op jit(solution)/shard_map/ppermute | solution.py:42
  36.7 11.7 %collective-permute-start.16 = (bf16[512,512]{1,0:T(8,128)(2,1)S(1)}, bf16[512,512]{1,0:T(8,128)(2,1)S(1)}, u32[]{:S(2)}, u32[]{:S(2)}) collective-permute-start(bf16[512,512]{1,0:T(8,128)(2,1)S(1)} %collective-permute-done.8.refs_16_), channel_id=1, source_target_pairs={{0,2},{2,0},{4,6},{6,4},{8,10},{10,8},{12,14},{14,12},{16,18},{18,... | collective-permute-start | bytes 1572872 | tf_op jit(solution)/shard_map/ppermute | solution.py:42
  46.6 2.7 collective-permute-start.4
  46.7 2.6 collective-permute-start.15
  47.2 8.4 %collective-permute-start.7 = (bf16[256,512]{1,0:T(8,128)(2,1)S(1)}, bf16[256,512]{1,0:T(8,128)(2,1)S(1)}, u32[]{:S(2)}, u32[]{:S(2)}) collective-permute-start(bf16[256,512]{1,0:T(8,128)(2,1)S(1)} %slice.18), channel_id=1, source_target_pairs={{0,8},{2,10},{8,16},{10,18},{16,24},{18,26},{24,28},{26,30},{28,20... | collective-permute-start | bytes 786440 | tf_op jit(solution)/shard_map/ppermute | solution.py:58
  48.5 10.0 %copy-start.7 = (bf16[512,512]{1,0:T(8,128)(2,1)}, bf16[512,512]{1,0:T(8,128)(2,1)S(1)}, u32[]{:S(2)}) copy-start(bf16[512,512]{1,0:T(8,128)(2,1)S(1)} %collective-permute-done.16.refs_17_) | copy-start | bytes 1572868
  48.5 8.4 %collective-permute-start.11 = (bf16[256,512]{1,0:T(8,128)(2,1)S(1)}, bf16[256,512]{1,0:T(8,128)(2,1)S(1)}, u32[]{:S(2)}, u32[]{:S(2)}) collective-permute-start(bf16[256,512]{1,0:T(8,128)(2,1)S(1)} %slice.19), channel_id=1, source_target_pairs={{0,4},{2,6},{8,0},{10,2},{16,8},{18,10},{24,16},{26,18},{28,24},{3... | collective-permute-start | bytes 786440 | tf_op jit(solution)/shard_map/ppermute | solution.py:59
  49.3 9.2 %collective-permute-start.6 = (bf16[512,512]{1,0:T(8,128)(2,1)S(1)}, bf16[512,512]{1,0:T(8,128)(2,1)S(1)}, u32[]{:S(2)}, u32[]{:S(2)}) collective-permute-start(bf16[512,512]{1,0:T(8,128)(2,1)S(1)} %collective-permute-done.5.refs_6_), channel_id=1, source_target_pairs={{0,2},{2,0},{4,6},{6,4},{8,10},{10,8},{12,14},{14,12},{16,18},{18,... | collective-permute-start | bytes 1572872 | tf_op jit(solution)/shard_map/ppermute | solution.py:42
  49.3 9.2 %collective-permute-start.14 = (bf16[512,512]{1,0:T(8,128)(2,1)S(1)}, bf16[512,512]{1,0:T(8,128)(2,1)S(1)}, u32[]{:S(2)}, u32[]{:S(2)}) collective-permute-start(bf16[512,512]{1,0:T(8,128)(2,1)S(1)} %collective-permute-done.10.refs_12_), channel_id=1, source_target_pairs={{0,2},{2,0},{4,6},{6,4},{8,10},{10,8},{12,14},{14,12},{16,18},{18,... | collective-permute-start | bytes 1572872 | tf_op jit(solution)/shard_map/ppermute | solution.py:42
  55.5 2.8 %collective-permute-start.12 = (bf16[256,512]{1,0:T(8,128)(2,1)S(1)}, bf16[256,512]{1,0:T(8,128)(2,1)S(1)}, u32[]{:S(2)}, u32[]{:S(2)}) collective-permute-start(bf16[256,512]{1,0:T(8,128)(2,1)S(1)} %collective-permute-done.7.refs_8_), channel_id=1, source_target_pairs={{0,2},{2,0},{4,6},{6,4},{8,10},{10,8},{12,14},{14,12},{16,18},{18,... | collective-permute-start | bytes 786440 | tf_op jit(solution)/shard_map/ppermute | solution.py:42
  56.9 1.5 collective-permute-start.13
  95.0 32.0 %collective-permute-start.19 = (bf16[128,4096]{1,0:T(8,128)(2,1)}, bf16[128,4096]{1,0:T(8,128)(2,1)S(1)}, u32[]{:S(2)}, u32[]{:S(2)}) collective-permute-start(bf16[128,4096]{1,0:T(8,128)(2,1)} %attend.1), channel_id=1, source_target_pairs={{0,8},{2,10},{8,16},{10,18},{16,24},{18,26},{24,28},{26,30},{28,20... | collective-permute-start | bytes 3145736 | tf_op jit(solution)/shard_map/ppermute | solution.py:51
  96.7 33.3 %collective-permute-start.29 = (bf16[128,4096]{1,0:T(8,128)(2,1)}, bf16[128,4096]{1,0:T(8,128)(2,1)S(1)}, u32[]{:S(2)}, u32[]{:S(2)}) collective-permute-start(bf16[128,4096]{1,0:T(8,128)(2,1)} %attend.1), channel_id=1, source_target_pairs={{0,4},{2,6},{8,0},{10,2},{16,8},{18,10},{24,16},{26,18},{28,24},{3... | collective-permute-start | bytes 3145736 | tf_op jit(solution)/shard_map/ppermute | solution.py:52
  103.6 32.5 %copy-start.2 = (bf16[4096,512]{1,0:T(8,128)(2,1)S(1)}, bf16[4096,512]{1,0:T(8,128)(2,1)}, u32[]{:S(2)}) copy-start(bf16[4096,512]{1,0:T(8,128)(2,1)} %param.12) | copy-start | bytes 12582916
  107.0 30.6 %copy-start.3 = (bf16[128,4096]{1,0:T(8,128)(2,1)S(1)}, bf16[128,4096]{1,0:T(8,128)(2,1)}, u32[]{:S(2)}) copy-start(bf16[128,4096]{1,0:T(8,128)(2,1)} %attend.1) | copy-start | bytes 3145732
  127.1 31.9 %collective-permute-start.22 = (bf16[128,4096]{1,0:T(8,128)(2,1)S(1)}, bf16[128,4096]{1,0:T(8,128)(2,1)S(1)}, u32[]{:S(2)}, u32[]{:S(2)}) collective-permute-start(bf16[128,4096]{1,0:T(8,128)(2,1)S(1)} %collective-permute-done.19), channel_id=1, source_target_pairs={{0,8},{2,10},{8,16},{10,18},{16,24},{18,26},{24,28},{26,30},{28,20... | collective-permute-start | bytes 3145736 | tf_op jit(solution)/shard_map/ppermute | solution.py:51
  130.0 33.3 %collective-permute-start.30 = (bf16[128,4096]{1,0:T(8,128)(2,1)S(1)}, bf16[128,4096]{1,0:T(8,128)(2,1)S(1)}, u32[]{:S(2)}, u32[]{:S(2)}) collective-permute-start(bf16[128,4096]{1,0:T(8,128)(2,1)S(1)} %collective-permute-done.29), channel_id=1, source_target_pairs={{0,4},{2,6},{8,0},{10,2},{16,8},{18,10},{24,16},{26,18},{28,24},{3... | collective-permute-start | bytes 3145736 | tf_op jit(solution)/shard_map/ppermute | solution.py:52
  140.7 31.5 %collective-permute-start.18 = (bf16[64,1024]{1,0:T(8,128)(2,1)S(1)}, bf16[64,1024]{1,0:T(8,128)(2,1)S(1)}, u32[]{:S(2)}, u32[]{:S(2)}) collective-permute-start(bf16[64,1024]{1,0:T(8,128)(2,1)S(1)} %fusion.32), channel_id=1, source_target_pairs={{0,1},{1,0},{2,3},{3,2},{4,5},{5,4},{6,7},{7,6},{8,9},{9,8},{10,11... | collective-permute-start | bytes 393224 | tf_op jit(solution)/shard_map/ppermute | solution.py:283
  144.2 33.8 %collective-permute-start.20 = (bf16[64,1024]{1,0:T(8,128)(2,1)S(1)}, bf16[64,1024]{1,0:T(8,128)(2,1)S(1)}, u32[]{:S(2)}, u32[]{:S(2)}) collective-permute-start(bf16[64,1024]{1,0:T(8,128)(2,1)S(1)} %fusion.27), channel_id=1, source_target_pairs={{0,1},{1,0},{2,3},{3,2},{4,5},{5,4},{6,7},{7,6},{8,9},{9,8},{10,11... | collective-permute-start | bytes 393224 | tf_op jit(solution)/shard_map/ppermute | solution.py:283
  162.7 19.6 %collective-permute-start.23 = (bf16[64,1024]{1,0:T(8,128)(2,1)S(1)}, bf16[64,1024]{1,0:T(8,128)(2,1)S(1)}, u32[]{:S(2)}, u32[]{:S(2)}) collective-permute-start(bf16[64,1024]{1,0:T(8,128)(2,1)S(1)} %fusion.22), channel_id=1, source_target_pairs={{0,1},{1,0},{2,3},{3,2},{4,5},{5,4},{6,7},{7,6},{8,9},{9,8},{10,11... | collective-permute-start | bytes 393224 | tf_op jit(solution)/shard_map/ppermute | solution.py:283
  167.0 17.4 %collective-permute-start.37 = (bf16[64,1024]{1,0:T(8,128)(2,1)S(1)}, bf16[64,1024]{1,0:T(8,128)(2,1)S(1)}, u32[]{:S(2)}, u32[]{:S(2)}) collective-permute-start(bf16[64,1024]{1,0:T(8,128)(2,1)S(1)} %fusion.7), channel_id=1, source_target_pairs={{0,1},{1,0},{2,3},{3,2},{4,5},{5,4},{6,7},{7,6},{8,9},{9,8},{10,11... | collective-permute-start | bytes 393224 | tf_op jit(solution)/shard_map/ppermute | solution.py:283
  171.5 15.7 %collective-permute-start.39 = (bf16[64,1024]{1,0:T(8,128)(2,1)S(1)}, bf16[64,1024]{1,0:T(8,128)(2,1)S(1)}, u32[]{:S(2)}, u32[]{:S(2)}) collective-permute-start(bf16[64,1024]{1,0:T(8,128)(2,1)S(1)} %fusion.2), channel_id=1, source_target_pairs={{0,1},{1,0},{2,3},{3,2},{4,5},{5,4},{6,7},{7,6},{8,9},{9,8},{10,11... | collective-permute-start | bytes 393224 | tf_op jit(solution)/shard_map/ppermute | solution.py:283
  172.1 38.6 %collective-permute-start.25 = (bf16[128,4096]{1,0:T(8,128)(2,1)S(1)}, bf16[128,4096]{1,0:T(8,128)(2,1)S(1)}, u32[]{:S(2)}, u32[]{:S(2)}) collective-permute-start(bf16[128,4096]{1,0:T(8,128)(2,1)S(1)} %collective-permute-done.22), channel_id=1, source_target_pairs={{0,8},{2,10},{8,16},{10,18},{16,24},{18,26},{24,28},{26,30},{28,20... | collective-permute-start | bytes 3145736 | tf_op jit(solution)/shard_map/ppermute | solution.py:51
  178.0 37.9 %collective-permute-start.31 = (bf16[128,4096]{1,0:T(8,128)(2,1)S(1)}, bf16[128,4096]{1,0:T(8,128)(2,1)S(1)}, u32[]{:S(2)}, u32[]{:S(2)}) collective-permute-start(bf16[128,4096]{1,0:T(8,128)(2,1)S(1)} %collective-permute-done.30), channel_id=1, source_target_pairs={{0,4},{2,6},{8,0},{10,2},{16,8},{18,10},{24,16},{26,18},{28,24},{3... | collective-permute-start | bytes 3145736 | tf_op jit(solution)/shard_map/ppermute | solution.py:52
  182.3 26.4 %collective-permute-start.21 = (bf16[64,1024]{1,0:T(8,128)(2,1)S(1)}, bf16[64,1024]{1,0:T(8,128)(2,1)S(1)}, u32[]{:S(2)}, u32[]{:S(2)}) collective-permute-start(bf16[64,1024]{1,0:T(8,128)(2,1)S(1)} %fusion.30), channel_id=1, source_target_pairs={{0,4},{2,6},{8,0},{10,2},{16,8},{18,10},{24,16},{26,18},{28,24},{3... | collective-permute-start | bytes 393224 | tf_op jit(solution)/shard_map/ppermute | solution.py:292
  184.4 26.2 %collective-permute-start.24 = (bf16[64,1024]{1,0:T(8,128)(2,1)S(1)}, bf16[64,1024]{1,0:T(8,128)(2,1)S(1)}, u32[]{:S(2)}, u32[]{:S(2)}) collective-permute-start(bf16[64,1024]{1,0:T(8,128)(2,1)S(1)} %fusion.25), channel_id=1, source_target_pairs={{0,12},{2,14},{8,4},{10,6},{16,0},{18,2},{24,8},{26,10},{28,16},{3... | collective-permute-start | bytes 393224 | tf_op jit(solution)/shard_map/ppermute | solution.py:292
  187.3 67.5 %collective-permute-start.38 = (bf16[64,1024]{1,0:T(8,128)(2,1)S(1)}, bf16[64,1024]{1,0:T(8,128)(2,1)S(1)}, u32[]{:S(2)}, u32[]{:S(2)}) collective-permute-start(bf16[64,1024]{1,0:T(8,128)(2,1)S(1)} %fusion.10), channel_id=1, source_target_pairs={{0,16},{2,18},{8,24},{10,26},{16,28},{18,30},{24,20},{26,22},{28,1... | collective-permute-start | bytes 393224 | tf_op jit(solution)/shard_map/ppermute | solution.py:292
  208.7 46.1 %collective-permute-start.40 = (bf16[64,1024]{1,0:T(8,128)(2,1)S(1)}, bf16[64,1024]{1,0:T(8,128)(2,1)S(1)}, u32[]{:S(2)}, u32[]{:S(2)}) collective-permute-start(bf16[64,1024]{1,0:T(8,128)(2,1)S(1)} %fusion.5), channel_id=1, source_target_pairs={{0,8},{2,10},{8,16},{10,18},{16,24},{18,26},{24,28},{26,30},{28,20... | collective-permute-start | bytes 393224 | tf_op jit(solution)/shard_map/ppermute | solution.py:292
  214.4 8.4 %collective-permute-start.26 = (bf16[64,1024]{1,0:T(8,128)(2,1)S(1)}, bf16[64,1024]{1,0:T(8,128)(2,1)S(1)}, u32[]{:S(2)}, u32[]{:S(2)}) collective-permute-start(bf16[64,1024]{1,0:T(8,128)(2,1)S(1)} %fusion.17), channel_id=1, source_target_pairs={{0,1},{1,0},{2,3},{3,2},{4,5},{5,4},{6,7},{7,6},{8,9},{9,8},{10,11... | collective-permute-start | bytes 393224 | tf_op jit(solution)/shard_map/ppermute | solution.py:283
  216.0 10.6 %collective-permute-start.32 = (bf16[64,4096]{1,0:T(8,128)(2,1)S(1)}, bf16[64,4096]{1,0:T(8,128)(2,1)S(1)}, u32[]{:S(2)}, u32[]{:S(2)}) collective-permute-start(bf16[64,4096]{1,0:T(8,128)(2,1)S(1)} %slice.21), channel_id=1, source_target_pairs={{0,4},{2,6},{8,0},{10,2},{16,8},{18,10},{24,16},{26,18},{28,24},{3... | collective-permute-start | bytes 1572872 | tf_op jit(solution)/shard_map/ppermute | solution.py:59
  219.0 19.0 %collective-permute-start.28 = (bf16[64,4096]{1,0:T(8,128)(2,1)S(1)}, bf16[64,4096]{1,0:T(8,128)(2,1)S(1)}, u32[]{:S(2)}, u32[]{:S(2)}) collective-permute-start(bf16[64,4096]{1,0:T(8,128)(2,1)S(1)} %slice.20), channel_id=1, source_target_pairs={{0,8},{2,10},{8,16},{10,18},{16,24},{18,26},{24,28},{26,30},{28,20... | collective-permute-start | bytes 1572872 | tf_op jit(solution)/shard_map/ppermute | solution.py:58
  222.8 19.7 %collective-permute-start.35 = (bf16[64,1024]{1,0:T(8,128)(2,1)S(1)}, bf16[64,1024]{1,0:T(8,128)(2,1)S(1)}, u32[]{:S(2)}, u32[]{:S(2)}) collective-permute-start(bf16[64,1024]{1,0:T(8,128)(2,1)S(1)} %fusion.12), channel_id=1, source_target_pairs={{0,1},{1,0},{2,3},{3,2},{4,5},{5,4},{6,7},{7,6},{8,9},{9,8},{10,11... | collective-permute-start | bytes 393224 | tf_op jit(solution)/shard_map/ppermute | solution.py:283
  226.6 20.5 %collective-permute-start.27 = (bf16[64,1024]{1,0:T(8,128)(2,1)S(1)}, bf16[64,1024]{1,0:T(8,128)(2,1)S(1)}, u32[]{:S(2)}, u32[]{:S(2)}) collective-permute-start(bf16[64,1024]{1,0:T(8,128)(2,1)S(1)} %fusion.20), channel_id=1, source_target_pairs={{0,20},{2,22},{8,12},{10,14},{16,4},{18,6},{24,0},{26,2},{28,8},{3... | collective-permute-start | bytes 393224 | tf_op jit(solution)/shard_map/ppermute | solution.py:292
  242.0 5.0 %collective-permute-start.33 = (bf16[64,1024]{1,0:T(8,128)(2,1)S(1)}, bf16[64,1024]{1,0:T(8,128)(2,1)S(1)}, u32[]{:S(2)}, u32[]{:S(2)}) collective-permute-start(bf16[64,1024]{1,0:T(8,128)(2,1)S(1)} %dynamic-slice_convert_fusion), channel_id=1, source_target_pairs={{0,1},{1,0},{2,3},{3,2},{4,5},{5,4},{6,7},{7,6},{8,9},{9,8},{10,11... | collective-permute-start | bytes 393224 | tf_op jit(solution)/shard_map/ppermute | solution.py:283
  242.5 12.2 %collective-permute-start.36 = (bf16[64,1024]{1,0:T(8,128)(2,1)S(1)}, bf16[64,1024]{1,0:T(8,128)(2,1)S(1)}, u32[]{:S(2)}, u32[]{:S(2)}) collective-permute-start(bf16[64,1024]{1,0:T(8,128)(2,1)S(1)} %fusion.15), channel_id=1, source_target_pairs={{0,24},{2,26},{8,28},{10,30},{16,20},{18,22},{24,12},{26,14},{28,4... | collective-permute-start | bytes 393224 | tf_op jit(solution)/shard_map/ppermute | solution.py:292
  247.0 7.7 %collective-permute-start.34 = (bf16[64,1024]{1,0:T(8,128)(2,1)S(1)}, bf16[64,1024]{1,0:T(8,128)(2,1)S(1)}, u32[]{:S(2)}, u32[]{:S(2)}) collective-permute-start(bf16[64,1024]{1,0:T(8,128)(2,1)S(1)} %add_convert_fusion), channel_id=1, source_target_pairs={{0,28},{2,30},{8,20},{10,22},{16,12},{18,14},{24,4},{26,6},{28,0},... | collective-permute-start | bytes 393224 | tf_op jit(solution)/shard_map/ppermute | solution.py:292
  (3 other events, 11.1 us)

commit v2 on v0

v2 whole, which is shorter than its diff:
```python
import functools
import math

import jax
import jax.numpy as jnp
from jax import lax
from jax.experimental import pallas as pl
from jax.experimental.pallas import tpu as pltpu
from jax.sharding import PartitionSpec as P

CORES = 2
LINES = 2
NEG = -1e30
VMEM_LIMIT = 32 * 1024 * 1024
FREE = pl.CostEstimate(flops=0, bytes_accessed=0, transcendentals=0)


def cycle_of(sites):
    length = sites // LINES
    order = []
    for line in range(LINES):
        steps = range(length) if line % 2 == 0 else range(length - 1, -1, -1)
        order += [z * LINES + line for z in steps]
    return order


def place_of(site, sites):
    z, line = site // LINES, site % LINES
    length = sites // LINES
    return jnp.where(line == 0, z, 2 * length - 1 - z)


def site_perm(sites, shift):
    order = cycle_of(sites)
    return [
        (order[i] * CORES + k, order[(i + shift) % sites] * CORES + k)
        for i in range(sites)
        for k in range(CORES)
    ]


def core_swap(x, count):
    return lax.ppermute(x, "ctx", [(i, i ^ 1) for i in range(count)])


def ring_walk(block, sites, work):
    ahead = site_perm(sites, 1)
    back = site_perm(sites, -1)
    here, done = {0: [block]}, None
    f = b = block
    steps = sites // 2
    for step in range(1, steps + 1):
        if step < steps or sites % 2:
            f = lax.ppermute(f, "ctx", ahead)
            b = lax.ppermute(b, "ctx", back)
            arrived = {step: [f], sites - step: [b]}
        else:
            half = block.shape[0] // 2
            f = lax.ppermute(f[:half], "ctx", ahead)
            b = lax.ppermute(b[half:], "ctx", back)
            arrived = {step: [f, b]}
        done = work(step - 1, here, done)
        f, b, done = lax.optimization_barrier((f, b, done))
        here = {d: [f, b] if len(p) == 2 else [f] if d == step else [b] for d, p in arrived.items()}
    return work(steps, here, done)


def pack_kernel(slots, pages_ref, me_ref, nk_ref, nv_ref, pk_ref, pv_ref, out_ref):
    rows = nk_ref.shape[0]
    page = pk_ref.shape[1]
    kept = (out_ref.shape[0] // 2 - rows) // page
    half = out_ref.shape[0] // 2
    out_ref[...] = jnp.zeros_like(out_ref)
    out_ref[0:rows, :] = nk_ref[...]
    out_ref[half : half + rows, :] = nv_ref[...]
    me = me_ref[0]

    def one(p, count):
        slot = pages_ref[p]
        mine = slot // slots == me

        @pl.when(jnp.logical_and(mine, count < kept))
        def _():
            local = slot % slots
            at = pl.multiple_of(rows + count * page, page)
            out_ref[pl.ds(at, page), :] = pk_ref[local]
            out_ref[pl.ds(pl.multiple_of(half + at, page), page), :] = pv_ref[local]

        return count + mine.astype(jnp.int32)

    lax.fori_loop(0, pages_ref.shape[0], one, jnp.int32(0))


def attend_kernel(cfg, first, last, counts, me_ref, q_ref, own_ref, ins, state, outs, scratch):
    n, rows, kvheads, group, width, page, slots, kept = cfg
    kbuf, vbuf, sbuf, dup, sem = scratch
    sites = n // CORES
    length = sites // LINES
    span = rows + kept * page
    total_keys = kbuf.shape[0]
    me = me_ref[0]
    my_site, my_core = me // CORES, me % CORES
    my_place = jnp.where(my_site % LINES == 0, my_site // LINES, 2 * length - 1 - my_site // LINES)

    pair = math.gcd(group, 4)
    tall = pair * rows
    steps = kvheads * group // pair
    scale = math.log2(math.e) * width ** (-0.5)
    chunk = CORES * span

    copies = [pltpu.make_async_copy(own_ref.at[0:16], dup, sem)]
    for b, (_, _, k_ref, k_at, v_ref, v_at) in enumerate(ins):
        at = pl.ds(b * span, span)
        copies.append(pltpu.make_async_copy(k_ref.at[pl.ds(k_at, span)], kbuf.at[at], sem))
        for h in range(kvheads):
            copies.append(
                pltpu.make_async_copy(
                    v_ref.at[pl.ds(v_at, span), pl.ds(h * width, width)],
                    vbuf.at[at, pl.ds(2 * h * width, width)],
                    sem,
                )
            )
    for copy in copies:
        copy.start()
    for h in range(kvheads):
        vbuf[:, (2 * h + 1) * width : (2 * h + 2) * width] = jnp.ones(
            (total_keys, width), jnp.bfloat16
        )
    for copy in copies:
        copy.wait()

    seen_key = dup[0:1, :]
    for b, (d, swap, *_) in enumerate(ins):
        place = lax.rem(my_place + sites - d, sites)
        line = place // length
        z = jnp.where(line == 0, place, 2 * length - 1 - place)
        owner = (z * LINES + line) * CORES + lax.rem(my_core + swap, CORES)

        def blank(at, size):
            kbuf[at : at + size, :] = jnp.broadcast_to(seen_key, (size, kbuf.shape[1]))
            vbuf[at : at + size, :] = jnp.zeros((size, vbuf.shape[1]), jnp.bfloat16)

        @pl.when(owner > me)
        def _():
            blank(b * span, rows)

        for j in range(kept):

            @pl.when(j >= counts[owner])
            def _():
                blank(b * span + rows + j * page, page)

    def lanes(i):
        return pl.ds(pl.multiple_of(i * width, width), width)

    def scores(i, slot):
        h = i // (group // pair)
        q = jnp.concatenate([q_ref[:, lanes(i * pair + g)] for g in range(pair)], axis=0)
        top = jnp.full((tall, width), NEG, jnp.float32)
        for j in range(total_keys // chunk):
            k = kbuf[j * chunk : (j + 1) * chunk, lanes(h)]
            s = lax.dot_general(q, k, (((1,), (1,)), ((), ())), preferred_element_type=jnp.float32)
            for a in range(chunk // width):
                piece = s[:, a * width : (a + 1) * width]
                at = j * chunk + a * width
                if first and at < rows:
                    row = lax.broadcasted_iota(jnp.int32, (rows, width), 0)
                    col = lax.broadcasted_iota(jnp.int32, (rows, width), 1) + at
                    seen = jnp.concatenate([col <= row] * pair, axis=0)
                    piece = jnp.where(seen, piece, NEG)
                sbuf[slot, :, at : at + width] = piece
                top = jnp.maximum(top, piece)
        return top

    def weigh(i, slot, top):
        h = i // (group // pair)
        at = pl.ds(pl.multiple_of(i * tall, tall), tall)
        best = jnp.max(top, axis=1, keepdims=True)
        if not first:
            was = state[1][at, 0:1]
            best = jnp.maximum(best, was)
        shift = best * scale
        acc = None
        for j in range(total_keys // chunk):
            s = sbuf[slot, :, j * chunk : (j + 1) * chunk]
            w = jnp.exp2(s * scale - shift).astype(jnp.bfloat16)
            v = vbuf[
                j * chunk : (j + 1) * chunk, pl.ds(pl.multiple_of(2 * h * width, width), 2 * width)
            ]
            part = jnp.dot(w, v, preferred_element_type=jnp.float32)
            acc = part if acc is None else acc + part
        mixed, total = acc[:, :width], acc[:, width:]
        if not first:
            left = jnp.exp2(was * scale - shift)
            mixed = mixed + state[0][at, :] * left
            total = total + state[1][at, width // 2 : width // 2 + 1] * left
        if last:
            out = (mixed / total).astype(jnp.bfloat16)
            for g in range(pair):
                outs[0][:, lanes(i * pair + g)] = out[g * rows : (g + 1) * rows]
        else:
            lane = lax.broadcasted_iota(jnp.int32, (tall, width), 1)
            outs[0][at, :] = mixed
            outs[1][at, :] = jnp.where(lane < width // 2, best, total)

    top = scores(0, 0)

    def two(t, top):
        after = scores(2 * t + 1, 1)
        weigh(2 * t, 0, top)
        top = scores(jnp.minimum(2 * t + 2, steps - 1), 0)
        weigh(2 * t + 1, 1, after)
        return top

    lax.fori_loop(0, steps // 2, two, top)


def attend(cfg, live, me_ref, queries, payload, blocks, state, last):
    n, rows, kvheads, group, width, page, slots, kept = cfg
    span = rows + kept * page
    smem = pl.BlockSpec(memory_space=pltpu.SMEM)
    vmem = pl.BlockSpec(memory_space=pltpu.VMEM)
    hbm = pl.BlockSpec(memory_space=pl.ANY)
    operands, spots = [], []
    for d, swap, pieces in blocks:
        base = len(operands)
        operands += pieces
        one = len(pieces) == 1
        spots.append((d, swap, base, 0, base if one else base + 1, span if one else 0))
    first = state is None
    state = [] if first else list(state)
    total_keys = len(blocks) * span
    tall = math.gcd(group, 4) * rows
    qrows = rows * kvheads * group
    if last:
        out_shape = [jax.ShapeDtypeStruct((rows, kvheads * group * width), jnp.bfloat16)]
    else:
        out_shape = [jax.ShapeDtypeStruct((qrows, width), jnp.float32)] * 2

    def body(live_ref, me_ref, q_ref, own_ref, *refs):
        ins = [(d, swap, refs[a], b, refs[c], e) for d, swap, a, b, c, e in spots]
        rest = refs[len(operands) :]
        held, rest = rest[: len(state)], rest[len(state) :]
        outs, scratch = rest[: len(out_shape)], rest[len(out_shape) :]
        attend_kernel(
            cfg, first, last, live_ref, me_ref, q_ref, own_ref, ins, held, outs, scratch
        )

    return pl.pallas_call(
        body,
        out_shape=out_shape,
        in_specs=[smem, smem, vmem, hbm] + [hbm] * len(operands) + [vmem] * len(state),
        out_specs=[vmem] * len(out_shape),
        scratch_shapes=[
            pltpu.VMEM((total_keys, kvheads * width), jnp.bfloat16),
            pltpu.VMEM((total_keys, 2 * kvheads * width), jnp.bfloat16),
            pltpu.VMEM((2, tall, total_keys), jnp.float32),
            pltpu.VMEM((16, kvheads * width), jnp.bfloat16),
            pltpu.SemaphoreType.DMA,
        ],
        compiler_params=pltpu.CompilerParams(vmem_limit_bytes=VMEM_LIMIT),
        cost_estimate=pl.CostEstimate(
            flops=4 * qrows * width * total_keys, bytes_accessed=0, transcendentals=0
        ),
        name="attend_last" if last else "attend",
    )(live, me_ref, queries, payload, *operands, *state)


def product(spots, pieces, own, other, split):
    depth, cols = own.shape
    tile = min(256, cols)
    half = cols // tile
    rows = sum(p.shape[0] for p in pieces)
    heads, blocks = (split, len(pieces)) if split else (1, 1)
    part = rows // blocks // heads
    assert heads <= 2

    def body(spots_ref, *refs):
        a_refs, rest = refs[: len(pieces)], refs[len(pieces) :]
        own_ref, other_ref, *outs = rest

        def run(w_ref):
            a = jnp.concatenate([r[...] for r in a_refs], axis=0)
            out = jnp.dot(a, w_ref[...], preferred_element_type=jnp.float32)
            if not split:
                outs[0][...] = out.astype(jnp.bfloat16)
                return
            keep_ref, sent_ref, acc = outs
            acc[...] = out
            head = spots_ref[1]
            for b in range(blocks):
                keep_ref[b * part : (b + 1) * part, :] = acc[
                    pl.ds(pl.multiple_of((b * heads + head) * part, part), part), :
                ]
                sent_ref[b * part : (b + 1) * part, :] = acc[
                    pl.ds(pl.multiple_of((b * heads + 1 - head) * part, part), part), :
                ].astype(jnp.bfloat16)

        t = pl.program_id(0)
        pl.when(t < half)(lambda: run(own_ref))
        pl.when(t >= half)(lambda: run(other_ref))

    out_spec = pl.BlockSpec(
        (rows // heads, tile), lambda t, s: (0, lax.rem(t + half * s[0], 2 * half))
    )
    shape = (rows // heads, 2 * cols)
    outs = [jax.ShapeDtypeStruct(shape, jnp.bfloat16)]
    if split:
        outs = [jax.ShapeDtypeStruct(shape, jnp.float32)] + outs
    return pl.pallas_call(
        body,
        out_shape=outs,
        grid_spec=pltpu.PrefetchScalarGridSpec(
            num_scalar_prefetch=1,
            grid=(2 * half,),
            in_specs=[pl.BlockSpec(p.shape, lambda t, s: (0, 0)) for p in pieces]
            + [
                pl.BlockSpec((depth, tile), lambda t, s: (0, jnp.minimum(t, half - 1))),
                pl.BlockSpec((depth, tile), lambda t, s: (0, jnp.maximum(t - half, 0))),
            ],
            out_specs=[out_spec] * len(outs),
            scratch_shapes=[pltpu.VMEM((rows, tile), jnp.float32)] if split else [],
        ),
        compiler_params=pltpu.CompilerParams(vmem_limit_bytes=VMEM_LIMIT),
        cost_estimate=pl.CostEstimate(
            flops=4 * rows * depth * cols, bytes_accessed=0, transcendentals=0
        ),
        name="product",
    )(spots, *pieces, own, other)


def back_perms(sites, heads, shift):
    order = cycle_of(sites)
    within, across = [], []
    for i in range(sites):
        source, target = order[i], order[(i - shift) % sites]
        goal = source * heads // sites
        for k in range(CORES):
            for h in range(heads):
                pair = ((source * CORES + k) * heads + h, (target * CORES + k) * heads + goal)
                (within if h == goal else across).append(pair)
    return within, across


def assemble_kernel(sites, heads, spots_ref, *refs):
    ins, (out_ref, left, right, sem) = refs[:-4], refs[-4:]
    length = sites // LINES
    cols = out_ref.shape[1] * heads // sites
    rows = out_ref.shape[0]
    part = rows // heads
    place, head = spots_ref[2], spots_ref[1]

    def each(go):
        for d in range(sites):
            at = lax.rem(place + d, sites)
            line = at // length
            z = jnp.where(line == 0, at, 2 * length - 1 - at)
            site = z * LINES + line
            first, second = ins[2 * d], ins[2 * d + 1]

            @pl.when(site * heads // sites == head)
            def _():
                lane = pl.multiple_of((site - head * (sites // heads)) * cols, cols)
                if first.shape[0] == rows:
                    slot = 0 if d == 0 else 1
                    if go is None:
                        total = left[slot].astype(jnp.float32) + right[slot].astype(jnp.float32)
                        out_ref[:, pl.ds(lane, cols)] = total.astype(jnp.bfloat16)
                        return
                    a = pltpu.make_async_copy(first, left.at[slot], sem)
                    b = pltpu.make_async_copy(second, right.at[slot], sem)
                elif go is None:
                    return
                else:
                    mine = pl.multiple_of(head * part, part)
                    other = pl.multiple_of((1 - head) * part, part)
                    a = pltpu.make_async_copy(
                        first, out_ref.at[pl.ds(mine, part), pl.ds(lane, cols)], sem
                    )
                    b = pltpu.make_async_copy(
                        second, out_ref.at[pl.ds(other, part), pl.ds(lane, cols)], sem
                    )
                go(a)
                go(b)

    each(lambda c: c.start())
    each(lambda c: c.wait())
    each(None)


def on_device(n, heads, queries, new_keys, new_values, pool_keys, pool_values, o_weight, page_list):
    rows, qheads, width = queries.shape
    kvheads = new_keys.shape[1]
    group = qheads // kvheads
    slots, page = pool_keys.shape[:2]
    npages = page_list.shape[0]
    kept = min(slots, 2 * npages // n)
    wide = kvheads * width
    sites = n // CORES
    cols = o_weight.shape[1]
    me = lax.axis_index("ctx")
    head = lax.axis_index("head")
    me_ref = me.reshape(1)
    place = place_of(me // CORES, sites)
    spots = jnp.stack([me % CORES, head, place]).astype(jnp.int32)
    smem = pl.BlockSpec(memory_space=pltpu.SMEM)
    vmem = pl.BlockSpec(memory_space=pltpu.VMEM)
    hbm = pl.BlockSpec(memory_space=pl.ANY)

    half = rows + kept * page
    payload = pl.pallas_call(
        functools.partial(pack_kernel, slots),
        out_shape=jax.ShapeDtypeStruct((2 * half, wide), jnp.bfloat16),
        in_specs=[smem, smem, vmem, vmem, vmem, vmem],
        out_specs=vmem,
        cost_estimate=FREE,
        name="pack_pages",
    )(
        page_list,
        me_ref,
        new_keys.reshape(rows, wide),
        new_values.reshape(rows, wide),
        pool_keys.reshape(slots, page, wide),
        pool_values.reshape(slots, page, wide),
    )
    w_other = core_swap(o_weight, n)
    q = queries.reshape(rows, qheads * width)
    cfg = (n, rows, kvheads, group, width, page, slots, kept)
    live = jnp.sum(
        (page_list // slots)[None, :] == jnp.arange(n, dtype=jnp.int32)[:, None], axis=1
    ).astype(jnp.int32)

    def look(step, here, state):
        blocks = []
        for d, pieces in here.items():
            blocks.append((d, 0, pieces))
            blocks.append((d, 1, [core_swap(p, n) for p in pieces]))
        return attend(cfg, live, me_ref, q, payload, blocks, state, step == sites // 2)

    (attended,) = ring_walk(payload, sites, look)

    if heads != 2 or sites % 2:
        parts = {}

        def multiply(step, here, _):
            for d, pieces in here.items():
                (part,) = product(spots, pieces, o_weight, w_other, 0)
                parts[d] = lax.ppermute(part, "ctx", site_perm(sites, -d)) if d else part
            return part

        ring_walk(attended, sites, multiply)
        order = jnp.stack(
            [jnp.mod(place_of(jnp.int32(s), sites) - place, sites) for s in range(sites)]
        )
        full = jnp.take(jnp.stack([parts[d] for d in range(sites)], axis=0), order, axis=0)
        full = full.transpose(1, 0, 2).reshape(rows, sites * CORES * cols)
        return lax.psum_scatter(full, "head", scatter_dimension=1, tiled=True)

    both = ("ctx", "head")
    arrived = {}

    def multiply(step, here, _):
        if step in (0, sites // 2):
            (part,) = product(spots, here[step], o_weight, w_other, 0)
            within, across = back_perms(sites, heads, step)
            first = lax.ppermute(part, both, within) if step else part
            arrived[step] = [first, lax.ppermute(part, both, across)]
            return part
        d, e = step, sites - step
        keep, sent = product(spots, here[d] + here[e], o_weight, w_other, heads)
        got = lax.ppermute(sent, "head", [(0, 1), (1, 0)])
        total = (keep + got.astype(jnp.float32)).astype(jnp.bfloat16)
        part = total.shape[0] // 2
        for at, piece in ((d, total[:part]), (e, total[part:])):
            arrived[at] = [
                lax.ppermute(piece, both, perm) for perm in back_perms(sites, heads, at)
            ]
        return sent

    ring_walk(attended, sites, multiply)
    return pl.pallas_call(
        functools.partial(assemble_kernel, sites, heads),
        out_shape=jax.ShapeDtypeStruct((rows, sites * CORES * cols // heads), jnp.bfloat16),
        in_specs=[smem] + [hbm] * (2 * sites),
        out_specs=vmem,
        scratch_shapes=[
            pltpu.VMEM((2, rows, CORES * cols), jnp.bfloat16),
            pltpu.VMEM((2, rows, CORES * cols), jnp.bfloat16),
            pltpu.SemaphoreType.DMA,
        ],
        cost_estimate=FREE,
        name="assemble",
    )(spots, *[a for d in range(sites) for a in arrived[d]])


def solution(mesh):
    n, heads = mesh.shape["ctx"], mesh.shape["head"]
    in_specs = (
        P("ctx", "head", None),
        P("ctx", "head", None),
        P("ctx", "head", None),
        P("ctx", None, "head", None),
        P("ctx", None, "head", None),
        P("head", "ctx"),
        P(),
    )
    out_specs = P("ctx", "head")
    return jax.shard_map(
        functools.partial(on_device, n, heads),
        mesh=mesh,
        in_specs=in_specs,
        out_specs=out_specs,
        check_vma=False,
    )
```

time: 449 us -> 224 us (0.50)
  waiting for transfers between devices: 232 us -> 75.3 us
  matrix products: 99 us -> 0 us
  Pallas kernels: 0 us -> 71.4 us
  starting transfers between devices: 0.21 us -> 65.8 us
  blocking collectives: 49.8 us -> 0 us
  other arithmetic: 38.1 us -> 0.37 us
  between operations: 13.6 us -> 0.78 us
    all_gather x5 -> x0, waiting for transfers between devices: 200 us -> none  [the longest x1 130 us: on_device(): lax.all_gather(attended, 'ctx', axis=0, tiled=True)]
    dot_general x5 -> x0, matrix products: 99 us -> none  [the longest x2 43.1 us: absorb(): jnp.einsum('rkgd,skd->kgrs', query_block, keys, preferred_element_type=jn...]
    ppermute x0 -> x44, waiting for transfers between devices: none -> 75.3 us  [the longest x6 49 us: ring_walk(): f = lax.ppermute(f, 'ctx', ahead)]
    pallas_call x0 -> x12, Pallas kernels: none -> 71.4 us  [the longest x5 35.7 us: attend(): pl.pallas_call(body, out_shape=out_shape, in_specs=[smem, smem, vmem, hbm...]
    ppermute x0 -> x44, starting transfers between devices: none -> 65.8 us  [the longest x12 31.3 us: multiply(): lax.ppermute(piece, both, perm)]
    all_to_all x1 -> x0, blocking collectives: 49.8 us -> none  [on_device(): lax.all_to_all(row_partials.astype(jnp.bfloat16), 'ctx', split_axis=0, co...]
    reduce_sum x2 -> x1, other arithmetic: 37.1 us -> 0.11 us  [on_device(): jnp.sum((page_list // slots)[None, :] == jnp.arange(n, dtype=jnp.int32)[:...]
    reduce_scatter x1 -> x0, waiting for transfers between devices: 31.7 us -> none  [on_device(): lax.psum_scatter(regrouped.astype(jnp.bfloat16), 'head', scatter_dimensio...]
  transfers between devices with their start and end apart: 6 -> 44, of which waited for: 5 -> 21; matrix products, arithmetic and copies ran while one was open for 26% -> 3% of each run, Pallas kernels for 0% -> 31%
where the time goes in v2:
time: 224 us; the launch traced here: 223 us
  waiting for transfers between devices  75.3 us (34%)
  Pallas kernels  71.4 us (32%)
  starting transfers between devices  65.8 us (29%)
  local copies, waits for them, and re-layouts  9.58 us (4%)
    ppermute x6, waiting for transfers between devices, ring_walk(): f = lax.ppermute(f, 'ctx', ahead)  49 us
    pallas_call x5, Pallas kernels, attend(): pl.pallas_call(body, out_shape=out_shape, in_specs=[smem, smem, vmem, hbm...  35.7 us
    ppermute x12, starting transfers between devices, multiply(): lax.ppermute(piece, both, perm)  31.3 us
    pallas_call x5, Pallas kernels, product(): pl.pallas_call(body, out_shape=outs, grid_spec=pltpu.PrefetchScalarGridSp...  29.9 us
    ppermute x12, waiting for transfers between devices, multiply(): lax.ppermute(piece, both, perm)  11.8 us
    ppermute x2, starting transfers between devices, multiply(): arrived[step] = [first, lax.ppermute(part, both, across)]  7.91 us
    ppermute x6, starting transfers between devices, ring_walk(): f = lax.ppermute(f, 'ctx', ahead)  7.35 us
    ppermute x3, waiting for transfers between devices, multiply(): got = lax.ppermute(sent, 'head', [(0, 1), (1, 0)])  6.91 us
  transfers between devices with their start and end apart: 44, of which 21 were waited for; matrix products, arithmetic and copies ran while one was open for 3% of the time, Pallas kernels for 31%

profile of v2, /device:TPU:6, one launch (start us, length us, event | category | flops | bytes accessed | tf_op | source)
XLA Modules:
  0.0 223.2 jit_solution(15595364726360924232)
XLA Ops:
  0.0 1.8 copy_bitcast_fusion.1
  1.8 1.8 reshape.23.pk_ref
  3.6 1.8 reshape.24.pv_ref
  5.4 2.7 %pack_pages.1.own_ref.refs_0_ = bf16[512,512]{1,0:T(8,128)(2,1)} custom-call(s32[32]{0:T(128)} %pages_ref.1, s32[1]{0:T(128)} %bitcast.3.me_ref, bf16[128,512]{1,0:T(8,128)(2,1)} %get-tuple-element.88.nk_ref, bf16[128,512]{1,0:T(8,128)(2,1)} %get-tuple-element.87.nv_ref, bf16[8,32,512]{2,1,0:T(8,128)(2,1)} %reshape.23.pk_ref, bf16[8,32,512]{2,1,0:T(8,128)(2,1)} %reshape.24.pv_ref), custom_call_target="tpu_custom_call" | custom-call | tf_op jit(solution)/shard_map/pack_pages/pallas_call | solution.py:411
  9.0 1.5 collective-permute-start.1
  11.1 4.8 %attend.4 = (f32[4096,128]{1,0:T(8,128)S(1)}, f32[4096,128]{1,0:T(8,128)S(1)}) custom-call(s32[16]{0:T(128)S(1)} %convert_reduce_fusion.live_ref, s32[1]{0:T(128)} %bitcast.3.me_ref, bf16[128,4096]{1,0:T(8,128)(2,1)S(1)} %bitcast.14, bf16[512,512]{1,0:T(8,128)(2,1)S(1)} %copy-done.2, bf16[512,512]{1,0:T(8,128)(2,1)S(1)} %copy-done.2, ...), custom_call_target="tpu_custom_call" | custom-call | flops 1073741824 | tf_op jit(solution)/shard_map/attend/pallas_call | solution.py:249
  15.9 6.7 %collective-permute-done.refs_0_ = bf16[512,512]{1,0:T(8,128)(2,1)S(1)} collective-permute-done((bf16[512,512]{1,0:T(8,128)(2,1)}, bf16[512,512]{1,0:T(8,128)(2,1)S(1)}, u32[]{:S(2)}, u32[]{:S(2)}) %collective-permute-start) | collective-permute-done | bytes 524320 | tf_op jit(solution)/shard_map/ppermute | solution.py:54
  23.3 1.6 collective-permute-start.3
  25.5 8.3 %attend.5 = (f32[4096,128]{1,0:T(8,128)S(1)}, f32[4096,128]{1,0:T(8,128)S(1)}) custom-call(s32[16]{0:T(128)S(1)} %convert_reduce_fusion.live_ref, s32[1]{0:T(128)} %bitcast.3.me_ref, bf16[128,4096]{1,0:T(8,128)(2,1)S(1)} %bitcast.15, bf16[512,512]{1,0:T(8,128)(2,1)S(1)} %copy-done.2, bf16[512,512]{1,0:T(8,128)(2,1)S(1)} %collective-permute-done.refs_0_, ...), custom_call_target="tpu_custom_call" | custom-call | flops 2147483648 | tf_op jit(solution)/shard_map/attend/pallas_call | solution.py:249
  33.8 3.4 %collective-permute-done.3.refs_0_ = bf16[512,512]{1,0:T(8,128)(2,1)S(1)} collective-permute-done((bf16[512,512]{1,0:T(8,128)(2,1)S(1)}, bf16[512,512]{1,0:T(8,128)(2,1)S(1)}, u32[]{:S(2)}, u32[]{:S(2)}) %collective-permute-start.3) | collective-permute-done | bytes 524320 | tf_op jit(solution)/shard_map/ppermute | solution.py:54
  37.2 1.3 collective-permute-done.4.refs_2_
  39.0 1.6 collective-permute-start.7
  41.1 8.3 %attend.6 = (f32[4096,128]{1,0:T(8,128)S(1)}, f32[4096,128]{1,0:T(8,128)S(1)}) custom-call(s32[16]{0:T(128)S(1)} %convert_reduce_fusion.live_ref, s32[1]{0:T(128)} %bitcast.3.me_ref, bf16[128,4096]{1,0:T(8,128)(2,1)S(1)} %bitcast.16, bf16[512,512]{1,0:T(8,128)(2,1)S(1)} %copy-done.2, bf16[512,512]{1,0:T(8,128)(2,1)S(1)} %collective-permute-done.3.refs_0_, ...), custom_call_target="tpu_custom_call" | custom-call | flops 2147483648 | tf_op jit(solution)/shard_map/attend/pallas_call | solution.py:249
  49.5 3.3 %collective-permute-done.7.refs_0_ = bf16[512,512]{1,0:T(8,128)(2,1)S(1)} collective-permute-done((bf16[512,512]{1,0:T(8,128)(2,1)S(1)}, bf16[512,512]{1,0:T(8,128)(2,1)S(1)}, u32[]{:S(2)}, u32[]{:S(2)}) %collective-permute-start.7) | collective-permute-done | bytes 524320 | tf_op jit(solution)/shard_map/ppermute | solution.py:54
  54.7 1.6 collective-permute-start.11
  56.8 8.7 %attend.7 = (f32[4096,128]{1,0:T(8,128)S(1)}, f32[4096,128]{1,0:T(8,128)S(1)}) custom-call(s32[16]{0:T(128)S(1)} %convert_reduce_fusion.live_ref, s32[1]{0:T(128)} %bitcast.3.me_ref, bf16[128,4096]{1,0:T(8,128)(2,1)S(1)} %bitcast.17, bf16[512,512]{1,0:T(8,128)(2,1)S(1)} %copy-done.2, bf16[512,512]{1,0:T(8,128)(2,1)S(1)} %collective-permute-done.7.refs_0_, ...), custom_call_target="tpu_custom_call" | custom-call | flops 2147483648 | tf_op jit(solution)/shard_map/attend/pallas_call | solution.py:249
  67.5 5.5 %attend_last.1.refs_0_ = bf16[128,4096]{1,0:T(8,128)(2,1)S(1)} custom-call(s32[16]{0:T(128)S(1)} %convert_reduce_fusion.live_ref, s32[1]{0:T(128)} %bitcast.3.me_ref, bf16[128,4096]{1,0:T(8,128)(2,1)S(1)} %bitcast.18, bf16[512,512]{1,0:T(8,128)(2,1)S(1)} %copy-done.2, bf16[256,512]{1,0:T(8,128)(2,1)S(1)} %collective-permute-done.11.refs_0_, ...), custom_call_target="tpu_custom_call" | custom-call | flops 1073741824 | tf_op jit(solution)/shard_map/attend_last/pallas_call | solution.py:249
  73.0 1.6 collective-permute-start.19
  75.2 2.2 copy-done
  77.4 5.7 %product.5.refs_0_ = bf16[128,1024]{1,0:T(8,128)(2,1)S(1)} custom-call(s32[3]{0:T(128)S(1)} %pad_add_fusion.spots_ref, bf16[128,4096]{1,0:T(8,128)(2,1)S(1)} %attend_last.1.refs_0_, bf16[4096,512]{1,0:T(8,128)(2,1)S(1)} %copy-done, bf16[4096,512]{1,0:T(8,128)(2,1)} %collective-permute-done.17.refs_2_.refs_3_), custom_call_target="tpu_custom_call" | custom-call | flops 1073741824 | tf_op jit(solution)/shard_map/product/pallas_call | solution.py:310
  83.1 15.2 %collective-permute-done.19.refs_0_ = bf16[128,4096]{1,0:T(8,128)(2,1)S(1)} collective-permute-done((bf16[128,4096]{1,0:T(8,128)(2,1)S(1)}, bf16[128,4096]{1,0:T(8,128)(2,1)S(1)}, u32[]{:S(2)}, u32[]{:S(2)}) %collective-permute-start.19) | collective-permute-done | bytes 1048608 | tf_op jit(solution)/shard_map/ppermute | solution.py:54
  99.5 1.5 collective-permute-start.24
  101.6 6.3 %product.6 = (f32[128,1024]{1,0:T(8,128)S(1)}, bf16[128,1024]{1,0:T(8,128)(2,1)S(1)}) custom-call(s32[3]{0:T(128)S(1)} %pad_add_fusion.spots_ref, bf16[128,4096]{1,0:T(8,128)(2,1)S(1)} %collective-permute-done.19.refs_0_, bf16[128,4096]{1,0:T(8,128)(2,1)S(1)} %collective-permute-done.20.refs_1_, bf16[4096,512]{1,0:T(8,128)(2,1)S(1)} %copy-done.1, ...), custom_call_target="tpu_custom_call" | custom-call | flops 2147483648 | tf_op jit(solution)/shard_map/product/pallas_call | solution.py:310
  107.8 15.8 %collective-permute-done.24.refs_0_ = bf16[128,4096]{1,0:T(8,128)(2,1)S(1)} collective-permute-done((bf16[128,4096]{1,0:T(8,128)(2,1)S(1)}, bf16[128,4096]{1,0:T(8,128)(2,1)S(1)}, u32[]{:S(2)}, u32[]{:S(2)}) %collective-permute-start.24) | collective-permute-done | bytes 1048608 | tf_op jit(solution)/shard_map/ppermute | solution.py:54
  125.4 1.4 collective-permute-start.30
  127.4 3.4 %collective-permute-start.18 = (bf16[128,1024]{1,0:T(8,128)(2,1)S(1)}, bf16[128,1024]{1,0:T(8,128)(2,1)S(1)}, u32[]{:S(2)}, u32[]{:S(2)}) collective-permute-start(bf16[128,1024]{1,0:T(8,128)(2,1)S(1)} %product.5.refs_0_), channel_id=1, source_target_pairs={{1,0},{3,2},{9,8},{11,10},{16,17},{18,19},{24,25},{26,27},{28,29},... | collective-permute-start | bytes 786440 | tf_op jit(solution)/shard_map/ppermute | solution.py:467
  130.8 2.6 %collective-permute-done.21 = bf16[128,1024]{1,0:T(8,128)(2,1)S(1)} collective-permute-done((bf16[128,1024]{1,0:T(8,128)(2,1)S(1)}, bf16[128,1024]{1,0:T(8,128)(2,1)S(1)}, u32[]{:S(2)}, u32[]{:S(2)}) %collective-permute-start.21) | collective-permute-done | bytes 262176 | tf_op jit(solution)/shard_map/ppermute | solution.py:471
  133.5 6.3 %product.7 = (f32[128,1024]{1,0:T(8,128)S(1)}, bf16[128,1024]{1,0:T(8,128)(2,1)S(1)}) custom-call(s32[3]{0:T(128)S(1)} %pad_add_fusion.spots_ref, bf16[128,4096]{1,0:T(8,128)(2,1)S(1)} %collective-permute-done.24.refs_0_, bf16[128,4096]{1,0:T(8,128)(2,1)S(1)} %collective-permute-done.25.refs_1_, bf16[4096,512]{1,0:T(8,128)(2,1)S(1)} %copy-done.1, ...), custom_call_target="tpu_custom_call" | custom-call | flops 2147483648 | tf_op jit(solution)/shard_map/product/pallas_call | solution.py:310
  139.8 2.5 %collective-permute-start.26 = (bf16[128,1024]{1,0:T(8,128)(2,1)S(1)}, bf16[128,1024]{1,0:T(8,128)(2,1)S(1)}, u32[]{:S(2)}, u32[]{:S(2)}) collective-permute-start(bf16[128,1024]{1,0:T(8,128)(2,1)S(1)} %get-tuple-element.74), channel_id=1, source_target_pairs={{0,1},{1,0},{2,3},{3,2},{4,5},{5,4},{6,7},{7,6},{8,9},{9,8},{10,11... | collective-permute-start | bytes 786440 | tf_op jit(solution)/shard_map/ppermute | solution.py:471
  143.1 4.6 %collective-permute-done.29.refs_0_ = bf16[128,4096]{1,0:T(8,128)(2,1)S(1)} collective-permute-done((bf16[128,4096]{1,0:T(8,128)(2,1)S(1)}, bf16[128,4096]{1,0:T(8,128)(2,1)S(1)}, u32[]{:S(2)}, u32[]{:S(2)}) %collective-permute-start.29) | collective-permute-done | bytes 1048608 | tf_op jit(solution)/shard_map/ppermute | solution.py:54
  148.9 1.5 collective-permute-start.35
  150.5 6.3 %product.8 = (f32[128,1024]{1,0:T(8,128)S(1)}, bf16[128,1024]{1,0:T(8,128)(2,1)S(1)}) custom-call(s32[3]{0:T(128)S(1)} %pad_add_fusion.spots_ref, bf16[128,4096]{1,0:T(8,128)(2,1)S(1)} %collective-permute-done.29.refs_0_, bf16[128,4096]{1,0:T(8,128)(2,1)S(1)} %collective-permute-done.30.refs_1_, bf16[4096,512]{1,0:T(8,128)(2,1)S(1)} %copy-done.1, ...), custom_call_target="tpu_custom_call" | custom-call | flops 2147483648 | tf_op jit(solution)/shard_map/product/pallas_call | solution.py:310
  156.7 3.3 %collective-permute-start.31 = (bf16[128,1024]{1,0:T(8,128)(2,1)S(1)}, bf16[128,1024]{1,0:T(8,128)(2,1)S(1)}, u32[]{:S(2)}, u32[]{:S(2)}) collective-permute-start(bf16[128,1024]{1,0:T(8,128)(2,1)S(1)} %get-tuple-element.78), channel_id=1, source_target_pairs={{0,1},{1,0},{2,3},{3,2},{4,5},{5,4},{6,7},{7,6},{8,9},{9,8},{10,11... | collective-permute-start | bytes 786440 | tf_op jit(solution)/shard_map/ppermute | solution.py:471
  160.1 4.3 %collective-permute-done.31 = bf16[128,1024]{1,0:T(8,128)(2,1)S(1)} collective-permute-done((bf16[128,1024]{1,0:T(8,128)(2,1)S(1)}, bf16[128,1024]{1,0:T(8,128)(2,1)S(1)}, u32[]{:S(2)}, u32[]{:S(2)}) %collective-permute-start.31) | collective-permute-done | bytes 262176 | tf_op jit(solution)/shard_map/ppermute | solution.py:471
  164.3 5.9 %collective-permute-start.23 = (bf16[64,1024]{1,0:T(8,128)(2,1)S(1)}, bf16[64,1024]{1,0:T(8,128)(2,1)S(1)}, u32[]{:S(2)}, u32[]{:S(2)}) collective-permute-start(bf16[64,1024]{1,0:T(8,128)(2,1)S(1)} %get-tuple-element.82), channel_id=1, source_target_pairs={{1,4},{3,6},{9,0},{11,2},{16,9},{18,11},{24,17},{26,19},{28,25},{3... | collective-permute-start | bytes 393224 | tf_op jit(solution)/shard_map/ppermute | solution.py:476
  171.0 3.4 %collective-permute-start.43 = (bf16[64,1024]{1,0:T(8,128)(2,1)S(1)}, bf16[64,1024]{1,0:T(8,128)(2,1)S(1)}, u32[]{:S(2)}, u32[]{:S(2)}) collective-permute-start(bf16[64,1024]{1,0:T(8,128)(2,1)S(1)} %get-tuple-element.81), channel_id=1, source_target_pairs={{1,8},{3,10},{9,16},{11,18},{16,25},{18,27},{24,29},{26,31},{28,21... | collective-permute-start | bytes 393224 | tf_op jit(solution)/shard_map/ppermute | solution.py:476
  175.1 4.1 %collective-permute-start.28 = (bf16[64,1024]{1,0:T(8,128)(2,1)S(1)}, bf16[64,1024]{1,0:T(8,128)(2,1)S(1)}, u32[]{:S(2)}, u32[]{:S(2)}) collective-permute-start(bf16[64,1024]{1,0:T(8,128)(2,1)S(1)} %get-tuple-element.84), channel_id=1, source_target_pairs={{1,12},{3,14},{9,4},{11,6},{16,1},{18,3},{24,9},{26,11},{28,17},{3... | collective-permute-start | bytes 393224 | tf_op jit(solution)/shard_map/ppermute | solution.py:476
  179.2 5.4 %product.9 = bf16[128,1024]{1,0:T(8,128)(2,1)S(1)} custom-call(s32[3]{0:T(128)S(1)} %pad_add_fusion.spots_ref, bf16[64,4096]{1,0:T(8,128)(2,1)S(1)} %collective-permute-done.34.refs_0_, bf16[64,4096]{1,0:T(8,128)(2,1)S(1)} %collective-permute-done.35.refs_1_, bf16[4096,512]{1,0:T(8,128)(2,1)S(1)} %copy-done.1, ...), custom_call_target="tpu_custom_call" | custom-call | flops 1073741824 | tf_op jit(solution)/shard_map/product/pallas_call | solution.py:310
  184.7 1.3 collective-permute-start.40
  186.0 6.1 %collective-permute-start.41 = (bf16[64,1024]{1,0:T(8,128)(2,1)S(1)}, bf16[64,1024]{1,0:T(8,128)(2,1)S(1)}, u32[]{:S(2)}, u32[]{:S(2)}) collective-permute-start(bf16[64,1024]{1,0:T(8,128)(2,1)S(1)} %get-tuple-element.83), channel_id=1, source_target_pairs={{1,16},{3,18},{9,24},{11,26},{16,29},{18,31},{24,21},{26,23},{28,1... | collective-permute-start | bytes 393224 | tf_op jit(solution)/shard_map/ppermute | solution.py:476
  193.5 1.3 collective-permute-start.36
  194.8 4.5 %collective-permute-start.37 = (bf16[128,1024]{1,0:T(8,128)(2,1)S(1)}, bf16[128,1024]{1,0:T(8,128)(2,1)S(1)}, u32[]{:S(2)}, u32[]{:S(2)}) collective-permute-start(bf16[128,1024]{1,0:T(8,128)(2,1)S(1)} %product.9), channel_id=1, source_target_pairs={{1,28},{3,30},{9,20},{11,22},{16,13},{18,15},{24,5},{26,7},{28,1},... | collective-permute-start | bytes 786440 | tf_op jit(solution)/shard_map/ppermute | solution.py:467
  199.3 4.1 %collective-permute-start.33 = (bf16[64,1024]{1,0:T(8,128)(2,1)S(1)}, bf16[64,1024]{1,0:T(8,128)(2,1)S(1)}, u32[]{:S(2)}, u32[]{:S(2)}) collective-permute-start(bf16[64,1024]{1,0:T(8,128)(2,1)S(1)} %get-tuple-element.86), channel_id=1, source_target_pairs={{1,20},{3,22},{9,12},{11,14},{16,5},{18,7},{24,1},{26,3},{28,9},{3... | collective-permute-start | bytes 393224 | tf_op jit(solution)/shard_map/ppermute | solution.py:476
  204.7 4.2 %collective-permute-done.32.refs_6_ = bf16[64,1024]{1,0:T(8,128)(2,1)S(1)} collective-permute-done((bf16[64,1024]{1,0:T(8,128)(2,1)S(1)}, bf16[64,1024]{1,0:T(8,128)(2,1)S(1)}, u32[]{:S(2)}, u32[]{:S(2)}) %collective-permute-start.32) | collective-permute-done | bytes 131104 | tf_op jit(solution)/shard_map/ppermute | solution.py:476
  208.9 1.9 collective-permute-start.39
  210.8 1.6 collective-permute-done.33.refs_7_
  212.4 6.0 %collective-permute-done.39.refs_11_ = bf16[64,1024]{1,0:T(8,128)(2,1)S(1)} collective-permute-done((bf16[64,1024]{1,0:T(8,128)(2,1)S(1)}, bf16[64,1024]{1,0:T(8,128)(2,1)S(1)}, u32[]{:S(2)}, u32[]{:S(2)}) %collective-permute-start.39) | collective-permute-done | bytes 131104 | tf_op jit(solution)/shard_map/ppermute | solution.py:476
  219.9 3.1 %assemble.1 = bf16[128,4096]{1,0:T(8,128)(2,1)} custom-call(s32[3]{0:T(128)} %copy-done.4, bf16[128,1024]{1,0:T(8,128)(2,1)} %copy-done.3, bf16[128,1024]{1,0:T(8,128)(2,1)} %copy-done.6, bf16[64,1024]{1,0:T(8,128)(2,1)} %copy-done.9, bf16[64,1024]{1,0:T(8,128)(2,1)} %copy-done.10, bf16[64,1024]{1,0:T(8,128)(2,1)} %copy-done.13, ...), custom_call_target="tpu_custom_call" | custom-call | tf_op jit(solution)/shard_map/assemble/pallas_call | solution.py:481
  (113 shorter events, 20.4 us)
Async XLA Ops:
  0.0 75.2 %collective-permute-start.17 = (bf16[4096,512]{1,0:T(8,128)(2,1)}, bf16[4096,512]{1,0:T(8,128)(2,1)}, u32[]{:S(2)}, u32[]{:S(2)}) collective-permute-start(bf16[4096,512]{1,0:T(8,128)(2,1)} %refs_2_.7), channel_id=1, source_target_pairs={{0,2},{2,0},{4,6},{6,4},{8,10},{10,8},{12,14},{14,12},{16,18},{18,... | collective-permute-start | bytes 12582920 | tf_op jit(solution)/shard_map/ppermute | solution.py:43
  8.1 3.0 %collective-permute-start.2 = (bf16[512,512]{1,0:T(8,128)(2,1)}, bf16[512,512]{1,0:T(8,128)(2,1)S(1)}, u32[]{:S(2)}, u32[]{:S(2)}) collective-permute-start(bf16[512,512]{1,0:T(8,128)(2,1)} %pack_pages.1.own_ref.refs_0_), channel_id=1, source_target_pairs={{0,2},{2,0},{4,6},{6,4},{8,10},{10,8},{12,14},{14,12},{16,18},{18,... | collective-permute-start | bytes 1572872 | tf_op jit(solution)/shard_map/ppermute | solution.py:43
  8.5 14.1 %collective-permute-start = (bf16[512,512]{1,0:T(8,128)(2,1)}, bf16[512,512]{1,0:T(8,128)(2,1)S(1)}, u32[]{:S(2)}, u32[]{:S(2)}) collective-permute-start(bf16[512,512]{1,0:T(8,128)(2,1)} %pack_pages.1.own_ref.refs_0_), channel_id=1, source_target_pairs={{0,8},{2,10},{8,16},{10,18},{16,24},{18,26},{24,28},{26,30},{28,20... | collective-permute-start | bytes 1572872 | tf_op jit(solution)/shard_map/ppermute | solution.py:54
  9.0 13.9 %collective-permute-start.1 = (bf16[512,512]{1,0:T(8,128)(2,1)}, bf16[512,512]{1,0:T(8,128)(2,1)S(1)}, u32[]{:S(2)}, u32[]{:S(2)}) collective-permute-start(bf16[512,512]{1,0:T(8,128)(2,1)} %pack_pages.1.own_ref.refs_0_), channel_id=1, source_target_pairs={{0,4},{2,6},{8,0},{10,2},{16,8},{18,10},{24,16},{26,18},{28,24},{3... | collective-permute-start | bytes 1572872 | tf_op jit(solution)/shard_map/ppermute | solution.py:55
  22.8 2.5 %collective-permute-start.5 = (bf16[512,512]{1,0:T(8,128)(2,1)S(1)}, bf16[512,512]{1,0:T(8,128)(2,1)S(1)}, u32[]{:S(2)}, u32[]{:S(2)}) collective-permute-start(bf16[512,512]{1,0:T(8,128)(2,1)S(1)} %collective-permute-done.refs_0_), channel_id=1, source_target_pairs={{0,2},{2,0},{4,6},{6,4},{8,10},{10,8},{12,14},{14,12},{16,18},{18,... | collective-permute-start | bytes 1572872 | tf_op jit(solution)/shard_map/ppermute | solution.py:43
  22.8 2.7 %collective-permute-start.6 = (bf16[512,512]{1,0:T(8,128)(2,1)S(1)}, bf16[512,512]{1,0:T(8,128)(2,1)S(1)}, u32[]{:S(2)}, u32[]{:S(2)}) collective-permute-start(bf16[512,512]{1,0:T(8,128)(2,1)S(1)} %collective-permute-done.1.refs_2_), channel_id=1, source_target_pairs={{0,2},{2,0},{4,6},{6,4},{8,10},{10,8},{12,14},{14,12},{16,18},{18,... | collective-permute-start | bytes 1572872 | tf_op jit(solution)/shard_map/ppermute | solution.py:43
  23.3 13.8 %collective-permute-start.3 = (bf16[512,512]{1,0:T(8,128)(2,1)S(1)}, bf16[512,512]{1,0:T(8,128)(2,1)S(1)}, u32[]{:S(2)}, u32[]{:S(2)}) collective-permute-start(bf16[512,512]{1,0:T(8,128)(2,1)S(1)} %collective-permute-done.refs_0_), channel_id=1, source_target_pairs={{0,8},{2,10},{8,16},{10,18},{16,24},{18,26},{24,28},{26,30},{28,20... | collective-permute-start | bytes 1572872 | tf_op jit(solution)/shard_map/ppermute | solution.py:54
  24.9 13.6 %collective-permute-start.4 = (bf16[512,512]{1,0:T(8,128)(2,1)S(1)}, bf16[512,512]{1,0:T(8,128)(2,1)S(1)}, u32[]{:S(2)}, u32[]{:S(2)}) collective-permute-start(bf16[512,512]{1,0:T(8,128)(2,1)S(1)} %collective-permute-done.1.refs_2_), channel_id=1, source_target_pairs={{0,4},{2,6},{8,0},{10,2},{16,8},{18,10},{24,16},{26,18},{28,24},{3... | collective-permute-start | bytes 1572872 | tf_op jit(solution)/shard_map/ppermute | solution.py:55
  38.5 2.5 %collective-permute-start.10 = (bf16[512,512]{1,0:T(8,128)(2,1)S(1)}, bf16[512,512]{1,0:T(8,128)(2,1)S(1)}, u32[]{:S(2)}, u32[]{:S(2)}) collective-permute-start(bf16[512,512]{1,0:T(8,128)(2,1)S(1)} %collective-permute-done.4.refs_2_), channel_id=1, source_target_pairs={{0,2},{2,0},{4,6},{6,4},{8,10},{10,8},{12,14},{14,12},{16,18},{18,... | collective-permute-start | bytes 1572872 | tf_op jit(solution)/shard_map/ppermute | solution.py:43
  38.5 2.7 %collective-permute-start.9 = (bf16[512,512]{1,0:T(8,128)(2,1)S(1)}, bf16[512,512]{1,0:T(8,128)(2,1)S(1)}, u32[]{:S(2)}, u32[]{:S(2)}) collective-permute-start(bf16[512,512]{1,0:T(8,128)(2,1)S(1)} %collective-permute-done.3.refs_0_), channel_id=1, source_target_pairs={{0,2},{2,0},{4,6},{6,4},{8,10},{10,8},{12,14},{14,12},{16,18},{18,... | collective-permute-start | bytes 1572872 | tf_op jit(solution)/shard_map/ppermute | solution.py:43
  39.0 13.8 %collective-permute-start.7 = (bf16[512,512]{1,0:T(8,128)(2,1)S(1)}, bf16[512,512]{1,0:T(8,128)(2,1)S(1)}, u32[]{:S(2)}, u32[]{:S(2)}) collective-permute-start(bf16[512,512]{1,0:T(8,128)(2,1)S(1)} %collective-permute-done.3.refs_0_), channel_id=1, source_target_pairs={{0,8},{2,10},{8,16},{10,18},{16,24},{18,26},{24,28},{26,30},{28,20... | collective-permute-start | bytes 1572872 | tf_op jit(solution)/shard_map/ppermute | solution.py:54
  40.5 13.6 %collective-permute-start.8 = (bf16[512,512]{1,0:T(8,128)(2,1)S(1)}, bf16[512,512]{1,0:T(8,128)(2,1)S(1)}, u32[]{:S(2)}, u32[]{:S(2)}) collective-permute-start(bf16[512,512]{1,0:T(8,128)(2,1)S(1)} %collective-permute-done.4.refs_2_), channel_id=1, source_target_pairs={{0,4},{2,6},{8,0},{10,2},{16,8},{18,10},{24,16},{26,18},{28,24},{3... | collective-permute-start | bytes 1572872 | tf_op jit(solution)/shard_map/ppermute | solution.py:55
  54.1 2.6 %collective-permute-start.13 = (bf16[512,512]{1,0:T(8,128)(2,1)S(1)}, bf16[512,512]{1,0:T(8,128)(2,1)S(1)}, u32[]{:S(2)}, u32[]{:S(2)}) collective-permute-start(bf16[512,512]{1,0:T(8,128)(2,1)S(1)} %collective-permute-done.7.refs_0_), channel_id=1, source_target_pairs={{0,2},{2,0},{4,6},{6,4},{8,10},{10,8},{12,14},{14,12},{16,18},{18,... | collective-permute-start | bytes 1572872 | tf_op jit(solution)/shard_map/ppermute | solution.py:43
  54.1 2.7 %collective-permute-start.14 = (bf16[512,512]{1,0:T(8,128)(2,1)S(1)}, bf16[512,512]{1,0:T(8,128)(2,1)S(1)}, u32[]{:S(2)}, u32[]{:S(2)}) collective-permute-start(bf16[512,512]{1,0:T(8,128)(2,1)S(1)} %collective-permute-done.8.refs_2_), channel_id=1, source_target_pairs={{0,2},{2,0},{4,6},{6,4},{8,10},{10,8},{12,14},{14,12},{16,18},{18,... | collective-permute-start | bytes 1572872 | tf_op jit(solution)/shard_map/ppermute | solution.py:43
  54.7 10.8 %collective-permute-start.11 = (bf16[256,512]{1,0:T(8,128)(2,1)S(1)}, bf16[256,512]{1,0:T(8,128)(2,1)S(1)}, u32[]{:S(2)}, u32[]{:S(2)}) collective-permute-start(bf16[256,512]{1,0:T(8,128)(2,1)S(1)} %slice.30), channel_id=1, source_target_pairs={{0,8},{2,10},{8,16},{10,18},{16,24},{18,26},{24,28},{26,30},{28,20... | collective-permute-start | bytes 786440 | tf_op jit(solution)/shard_map/ppermute | solution.py:59
  56.3 9.2 %collective-permute-start.12 = (bf16[256,512]{1,0:T(8,128)(2,1)S(1)}, bf16[256,512]{1,0:T(8,128)(2,1)S(1)}, u32[]{:S(2)}, u32[]{:S(2)}) collective-permute-start(bf16[256,512]{1,0:T(8,128)(2,1)S(1)} %slice.31), channel_id=1, source_target_pairs={{0,4},{2,6},{8,0},{10,2},{16,8},{18,10},{24,16},{26,18},{28,24},{3... | collective-permute-start | bytes 786440 | tf_op jit(solution)/shard_map/ppermute | solution.py:60
  65.5 1.6 collective-permute-start.15
  65.7 1.8 collective-permute-start.16
  73.0 25.3 %collective-permute-start.19 = (bf16[128,4096]{1,0:T(8,128)(2,1)S(1)}, bf16[128,4096]{1,0:T(8,128)(2,1)S(1)}, u32[]{:S(2)}, u32[]{:S(2)}) collective-permute-start(bf16[128,4096]{1,0:T(8,128)(2,1)S(1)} %attend_last.1.refs_0_), channel_id=1, source_target_pairs={{0,8},{2,10},{8,16},{10,18},{16,24},{18,26},{24,28},{26,30},{28,20... | collective-permute-start | bytes 3145736 | tf_op jit(solution)/shard_map/ppermute | solution.py:54
  74.6 24.9 %collective-permute-start.20 = (bf16[128,4096]{1,0:T(8,128)(2,1)S(1)}, bf16[128,4096]{1,0:T(8,128)(2,1)S(1)}, u32[]{:S(2)}, u32[]{:S(2)}) collective-permute-start(bf16[128,4096]{1,0:T(8,128)(2,1)S(1)} %attend_last.1.refs_0_), channel_id=1, source_target_pairs={{0,4},{2,6},{8,0},{10,2},{16,8},{18,10},{24,16},{26,18},{28,24},{3... | collective-permute-start | bytes 3145736 | tf_op jit(solution)/shard_map/ppermute | solution.py:55
  75.2 104.0 %copy-start.4 = (s32[3]{0:T(128)}, s32[3]{0:T(128)S(1)}, u32[]{:S(2)}) copy-start(s32[3]{0:T(128)S(1)} %pad_add_fusion.spots_ref) | copy-start | bytes 40
  83.1 44.3 %copy-start.3 = (bf16[128,1024]{1,0:T(8,128)(2,1)}, bf16[128,1024]{1,0:T(8,128)(2,1)S(1)}, u32[]{:S(2)}) copy-start(bf16[128,1024]{1,0:T(8,128)(2,1)S(1)} %product.5.refs_0_) | copy-start | bytes 786436
  99.5 24.0 %collective-permute-start.24 = (bf16[128,4096]{1,0:T(8,128)(2,1)S(1)}, bf16[128,4096]{1,0:T(8,128)(2,1)S(1)}, u32[]{:S(2)}, u32[]{:S(2)}) collective-permute-start(bf16[128,4096]{1,0:T(8,128)(2,1)S(1)} %collective-permute-done.19.refs_0_), channel_id=1, source_target_pairs={{0,8},{2,10},{8,16},{10,18},{16,24},{18,26},{24,28},{26,30},{28,20... | collective-permute-start | bytes 3145736 | tf_op jit(solution)/shard_map/ppermute | solution.py:54
  101.1 23.8 %collective-permute-start.25 = (bf16[128,4096]{1,0:T(8,128)(2,1)S(1)}, bf16[128,4096]{1,0:T(8,128)(2,1)S(1)}, u32[]{:S(2)}, u32[]{:S(2)}) collective-permute-start(bf16[128,4096]{1,0:T(8,128)(2,1)S(1)} %collective-permute-done.20.refs_1_), channel_id=1, source_target_pairs={{0,4},{2,6},{8,0},{10,2},{16,8},{18,10},{24,16},{26,18},{28,24},{3... | collective-permute-start | bytes 3145736 | tf_op jit(solution)/shard_map/ppermute | solution.py:55
  124.8 22.9 %collective-permute-start.29 = (bf16[128,4096]{1,0:T(8,128)(2,1)S(1)}, bf16[128,4096]{1,0:T(8,128)(2,1)S(1)}, u32[]{:S(2)}, u32[]{:S(2)}) collective-permute-start(bf16[128,4096]{1,0:T(8,128)(2,1)S(1)} %collective-permute-done.24.refs_0_), channel_id=1, source_target_pairs={{0,8},{2,10},{8,16},{10,18},{16,24},{18,26},{24,28},{26,30},{28,20... | collective-permute-start | bytes 3145736 | tf_op jit(solution)/shard_map/ppermute | solution.py:54
  125.4 22.8 %collective-permute-start.30 = (bf16[128,4096]{1,0:T(8,128)(2,1)S(1)}, bf16[128,4096]{1,0:T(8,128)(2,1)S(1)}, u32[]{:S(2)}, u32[]{:S(2)}) collective-permute-start(bf16[128,4096]{1,0:T(8,128)(2,1)S(1)} %collective-permute-done.25.refs_1_), channel_id=1, source_target_pairs={{0,4},{2,6},{8,0},{10,2},{16,8},{18,10},{24,16},{26,18},{28,24},{3... | collective-permute-start | bytes 3145736 | tf_op jit(solution)/shard_map/ppermute | solution.py:55
  126.9 6.6 %collective-permute-start.21 = (bf16[128,1024]{1,0:T(8,128)(2,1)S(1)}, bf16[128,1024]{1,0:T(8,128)(2,1)S(1)}, u32[]{:S(2)}, u32[]{:S(2)}) collective-permute-start(bf16[128,1024]{1,0:T(8,128)(2,1)S(1)} %get-tuple-element.70), channel_id=1, source_target_pairs={{0,1},{1,0},{2,3},{3,2},{4,5},{5,4},{6,7},{7,6},{8,9},{9,8},{10,11... | collective-permute-start | bytes 786440 | tf_op jit(solution)/shard_map/ppermute | solution.py:471
  127.4 42.9 %collective-permute-start.18 = (bf16[128,1024]{1,0:T(8,128)(2,1)S(1)}, bf16[128,1024]{1,0:T(8,128)(2,1)S(1)}, u32[]{:S(2)}, u32[]{:S(2)}) collective-permute-start(bf16[128,1024]{1,0:T(8,128)(2,1)S(1)} %product.5.refs_0_), channel_id=1, source_target_pairs={{1,0},{3,2},{9,8},{11,10},{16,17},{18,19},{24,25},{26,27},{28,29},... | collective-permute-start | bytes 786440 | tf_op jit(solution)/shard_map/ppermute | solution.py:467
  139.8 16.9 %collective-permute-start.26 = (bf16[128,1024]{1,0:T(8,128)(2,1)S(1)}, bf16[128,1024]{1,0:T(8,128)(2,1)S(1)}, u32[]{:S(2)}, u32[]{:S(2)}) collective-permute-start(bf16[128,1024]{1,0:T(8,128)(2,1)S(1)} %get-tuple-element.74), channel_id=1, source_target_pairs={{0,1},{1,0},{2,3},{3,2},{4,5},{5,4},{6,7},{7,6},{8,9},{9,8},{10,11... | collective-permute-start | bytes 786440 | tf_op jit(solution)/shard_map/ppermute | solution.py:471
  142.4 28.6 %collective-permute-start.22 = (bf16[64,1024]{1,0:T(8,128)(2,1)S(1)}, bf16[64,1024]{1,0:T(8,128)(2,1)S(1)}, u32[]{:S(2)}, u32[]{:S(2)}) collective-permute-start(bf16[64,1024]{1,0:T(8,128)(2,1)S(1)} %get-tuple-element.82), channel_id=1, source_target_pairs={{0,4},{2,6},{8,0},{10,2},{17,9},{19,11},{25,17},{27,19},{29,25},{3... | collective-permute-start | bytes 393224 | tf_op jit(solution)/shard_map/ppermute | solution.py:476
  148.3 26.1 %collective-permute-start.34 = (bf16[64,4096]{1,0:T(8,128)(2,1)S(1)}, bf16[64,4096]{1,0:T(8,128)(2,1)S(1)}, u32[]{:S(2)}, u32[]{:S(2)}) collective-permute-start(bf16[64,4096]{1,0:T(8,128)(2,1)S(1)} %slice.35), channel_id=1, source_target_pairs={{0,8},{2,10},{8,16},{10,18},{16,24},{18,26},{24,28},{26,30},{28,20... | collective-permute-start | bytes 1572872 | tf_op jit(solution)/shard_map/ppermute | solution.py:59
  148.9 26.2 %collective-permute-start.35 = (bf16[64,4096]{1,0:T(8,128)(2,1)S(1)}, bf16[64,4096]{1,0:T(8,128)(2,1)S(1)}, u32[]{:S(2)}, u32[]{:S(2)}) collective-permute-start(bf16[64,4096]{1,0:T(8,128)(2,1)S(1)} %slice.36), channel_id=1, source_target_pairs={{0,4},{2,6},{8,0},{10,2},{16,8},{18,10},{24,16},{26,18},{28,24},{3... | collective-permute-start | bytes 1572872 | tf_op jit(solution)/shard_map/ppermute | solution.py:60
  156.7 7.6 %collective-permute-start.31 = (bf16[128,1024]{1,0:T(8,128)(2,1)S(1)}, bf16[128,1024]{1,0:T(8,128)(2,1)S(1)}, u32[]{:S(2)}, u32[]{:S(2)}) collective-permute-start(bf16[128,1024]{1,0:T(8,128)(2,1)S(1)} %get-tuple-element.78), channel_id=1, source_target_pairs={{0,1},{1,0},{2,3},{3,2},{4,5},{5,4},{6,7},{7,6},{8,9},{9,8},{10,11... | collective-permute-start | bytes 786440 | tf_op jit(solution)/shard_map/ppermute | solution.py:471
  164.3 20.3 %collective-permute-start.23 = (bf16[64,1024]{1,0:T(8,128)(2,1)S(1)}, bf16[64,1024]{1,0:T(8,128)(2,1)S(1)}, u32[]{:S(2)}, u32[]{:S(2)}) collective-permute-start(bf16[64,1024]{1,0:T(8,128)(2,1)S(1)} %get-tuple-element.82), channel_id=1, source_target_pairs={{1,4},{3,6},{9,0},{11,2},{16,9},{18,11},{24,17},{26,19},{28,25},{3... | collective-permute-start | bytes 393224 | tf_op jit(solution)/shard_map/ppermute | solution.py:476
  170.3 15.7 %collective-permute-start.42 = (bf16[64,1024]{1,0:T(8,128)(2,1)S(1)}, bf16[64,1024]{1,0:T(8,128)(2,1)S(1)}, u32[]{:S(2)}, u32[]{:S(2)}) collective-permute-start(bf16[64,1024]{1,0:T(8,128)(2,1)S(1)} %get-tuple-element.81), channel_id=1, source_target_pairs={{0,8},{2,10},{8,16},{10,18},{17,25},{19,27},{25,29},{27,31},{29,21... | collective-permute-start | bytes 393224 | tf_op jit(solution)/shard_map/ppermute | solution.py:476
  171.0 21.1 %collective-permute-start.43 = (bf16[64,1024]{1,0:T(8,128)(2,1)S(1)}, bf16[64,1024]{1,0:T(8,128)(2,1)S(1)}, u32[]{:S(2)}, u32[]{:S(2)}) collective-permute-start(bf16[64,1024]{1,0:T(8,128)(2,1)S(1)} %get-tuple-element.81), channel_id=1, source_target_pairs={{1,8},{3,10},{9,16},{11,18},{16,25},{18,27},{24,29},{26,31},{28,21... | collective-permute-start | bytes 393224 | tf_op jit(solution)/shard_map/ppermute | solution.py:476
  174.4 19.0 %collective-permute-start.27 = (bf16[64,1024]{1,0:T(8,128)(2,1)S(1)}, bf16[64,1024]{1,0:T(8,128)(2,1)S(1)}, u32[]{:S(2)}, u32[]{:S(2)}) collective-permute-start(bf16[64,1024]{1,0:T(8,128)(2,1)S(1)} %get-tuple-element.84), channel_id=1, source_target_pairs={{0,12},{2,14},{8,4},{10,6},{17,1},{19,3},{25,9},{27,11},{29,17},{3... | collective-permute-start | bytes 393224 | tf_op jit(solution)/shard_map/ppermute | solution.py:476
  175.1 19.7 %collective-permute-start.28 = (bf16[64,1024]{1,0:T(8,128)(2,1)S(1)}, bf16[64,1024]{1,0:T(8,128)(2,1)S(1)}, u32[]{:S(2)}, u32[]{:S(2)}) collective-permute-start(bf16[64,1024]{1,0:T(8,128)(2,1)S(1)} %get-tuple-element.84), channel_id=1, source_target_pairs={{1,12},{3,14},{9,4},{11,6},{16,1},{18,3},{24,9},{26,11},{28,17},{3... | collective-permute-start | bytes 393224 | tf_op jit(solution)/shard_map/ppermute | solution.py:476
  184.7 33.8 %copy-start.10 = (bf16[64,1024]{1,0:T(8,128)(2,1)}, bf16[64,1024]{1,0:T(8,128)(2,1)S(1)}, u32[]{:S(2)}) copy-start(bf16[64,1024]{1,0:T(8,128)(2,1)S(1)} %collective-permute-done.23.refs_3_) | copy-start | bytes 393220
  184.7 14.6 %collective-permute-start.40 = (bf16[64,1024]{1,0:T(8,128)(2,1)S(1)}, bf16[64,1024]{1,0:T(8,128)(2,1)S(1)}, u32[]{:S(2)}, u32[]{:S(2)}) collective-permute-start(bf16[64,1024]{1,0:T(8,128)(2,1)S(1)} %get-tuple-element.83), channel_id=1, source_target_pairs={{0,16},{2,18},{8,24},{10,26},{17,29},{19,31},{25,21},{27,23},{29,1... | collective-permute-start | bytes 393224 | tf_op jit(solution)/shard_map/ppermute | solution.py:476
  186.0 32.5 %copy-start.11 = (bf16[64,1024]{1,0:T(8,128)(2,1)}, bf16[64,1024]{1,0:T(8,128)(2,1)S(1)}, u32[]{:S(2)}) copy-start(bf16[64,1024]{1,0:T(8,128)(2,1)S(1)} %collective-permute-done.42.refs_14_) | copy-start | bytes 393220
  186.0 17.4 %collective-permute-start.41 = (bf16[64,1024]{1,0:T(8,128)(2,1)S(1)}, bf16[64,1024]{1,0:T(8,128)(2,1)S(1)}, u32[]{:S(2)}, u32[]{:S(2)}) collective-permute-start(bf16[64,1024]{1,0:T(8,128)(2,1)S(1)} %get-tuple-element.83), channel_id=1, source_target_pairs={{1,16},{3,18},{9,24},{11,26},{16,29},{18,31},{24,21},{26,23},{28,1... | collective-permute-start | bytes 393224 | tf_op jit(solution)/shard_map/ppermute | solution.py:476
  192.1 16.7 %collective-permute-start.32 = (bf16[64,1024]{1,0:T(8,128)(2,1)S(1)}, bf16[64,1024]{1,0:T(8,128)(2,1)S(1)}, u32[]{:S(2)}, u32[]{:S(2)}) collective-permute-start(bf16[64,1024]{1,0:T(8,128)(2,1)S(1)} %get-tuple-element.86), channel_id=1, source_target_pairs={{0,20},{2,22},{8,12},{10,14},{17,5},{19,7},{25,1},{27,3},{29,9},{3... | collective-permute-start | bytes 393224 | tf_op jit(solution)/shard_map/ppermute | solution.py:476
  193.5 25.0 %collective-permute-start.36 = (bf16[128,1024]{1,0:T(8,128)(2,1)S(1)}, bf16[128,1024]{1,0:T(8,128)(2,1)S(1)}, u32[]{:S(2)}, u32[]{:S(2)}) collective-permute-start(bf16[128,1024]{1,0:T(8,128)(2,1)S(1)} %product.9), channel_id=1, source_target_pairs={{0,28},{2,30},{8,20},{10,22},{17,13},{19,15},{25,5},{27,7},{29,1},... | collective-permute-start | bytes 786440 | tf_op jit(solution)/shard_map/ppermute | solution.py:466
  194.8 23.7 %collective-permute-start.37 = (bf16[128,1024]{1,0:T(8,128)(2,1)S(1)}, bf16[128,1024]{1,0:T(8,128)(2,1)S(1)}, u32[]{:S(2)}, u32[]{:S(2)}) collective-permute-start(bf16[128,1024]{1,0:T(8,128)(2,1)S(1)} %product.9), channel_id=1, source_target_pairs={{1,28},{3,30},{9,20},{11,22},{16,13},{18,15},{24,5},{26,7},{28,1},... | collective-permute-start | bytes 786440 | tf_op jit(solution)/shard_map/ppermute | solution.py:467
  199.3 13.1 %collective-permute-start.33 = (bf16[64,1024]{1,0:T(8,128)(2,1)S(1)}, bf16[64,1024]{1,0:T(8,128)(2,1)S(1)}, u32[]{:S(2)}, u32[]{:S(2)}) collective-permute-start(bf16[64,1024]{1,0:T(8,128)(2,1)S(1)} %get-tuple-element.86), channel_id=1, source_target_pairs={{1,20},{3,22},{9,12},{11,14},{16,5},{18,7},{24,1},{26,3},{28,9},{3... | collective-permute-start | bytes 393224 | tf_op jit(solution)/shard_map/ppermute | solution.py:476
  203.4 9.0 %collective-permute-start.38 = (bf16[64,1024]{1,0:T(8,128)(2,1)S(1)}, bf16[64,1024]{1,0:T(8,128)(2,1)S(1)}, u32[]{:S(2)}, u32[]{:S(2)}) collective-permute-start(bf16[64,1024]{1,0:T(8,128)(2,1)S(1)} %get-tuple-element.85), channel_id=1, source_target_pairs={{0,24},{2,26},{8,28},{10,30},{17,21},{19,23},{25,13},{27,15},{29,5... | collective-permute-start | bytes 393224 | tf_op jit(solution)/shard_map/ppermute | solution.py:476
  208.9 9.5 %collective-permute-start.39 = (bf16[64,1024]{1,0:T(8,128)(2,1)S(1)}, bf16[64,1024]{1,0:T(8,128)(2,1)S(1)}, u32[]{:S(2)}, u32[]{:S(2)}) collective-permute-start(bf16[64,1024]{1,0:T(8,128)(2,1)S(1)} %get-tuple-element.85), channel_id=1, source_target_pairs={{1,24},{3,26},{9,28},{11,30},{16,21},{18,23},{24,13},{26,15},{28,5... | collective-permute-start | bytes 393224 | tf_op jit(solution)/shard_map/ppermute | solution.py:476
  (18 other events, 208.7 us)

commit v3 on v2

--- a/solution.py
+++ b/solution.py
@@ -46,7 +46,7 @@
 def ring_walk(block, sites, work):
     ahead = site_perm(sites, 1)
     back = site_perm(sites, -1)
-    here, done = {0: [block]}, None
+    here, done, late = {0: [block]}, None, []
     f = b = block
     steps = sites // 2
     for step in range(1, steps + 1):
@@ -59,10 +59,11 @@
             f = lax.ppermute(f[:half], "ctx", ahead)
             b = lax.ppermute(b[half:], "ctx", back)
             arrived = {step: [f, b]}
-        done = work(step - 1, here, done)
-        f, b, done = lax.optimization_barrier((f, b, done))
+        done, later = work(step - 1, here, done)
+        f, b, done, _ = lax.optimization_barrier((f, b, done, late))
+        late = later
         here = {d: [f, b] if len(p) == 2 else [f] if d == step else [b] for d, p in arrived.items()}
-    return work(steps, here, done)
+    return work(steps, here, done)[0]
 
 
 def pack_kernel(slots, pages_ref, me_ref, nk_ref, nv_ref, pk_ref, pv_ref, out_ref):
@@ -71,8 +72,11 @@
     kept = (out_ref.shape[0] // 2 - rows) // page
     half = out_ref.shape[0] // 2
     out_ref[...] = jnp.zeros_like(out_ref)
-    out_ref[0:rows, :] = nk_ref[...]
-    out_ref[half : half + rows, :] = nv_ref[...]
+    heads, width = nk_ref.shape[1:]
+    for h in range(heads):
+        lanes = slice(h * width, (h + 1) * width)
+        out_ref[0:rows, lanes] = nk_ref[:, h, :]
+        out_ref[half : half + rows, lanes] = nv_ref[:, h, :]
     me = me_ref[0]
 
     def one(p, count):
@@ -83,8 +87,12 @@
         def _():
             local = slot % slots
             at = pl.multiple_of(rows + count * page, page)
-            out_ref[pl.ds(at, page), :] = pk_ref[local]
-            out_ref[pl.ds(pl.multiple_of(half + at, page), page), :] = pv_ref[local]
+            for h in range(heads):
+                lanes = slice(h * width, (h + 1) * width)
+                out_ref[pl.ds(at, page), lanes] = pk_ref[local, :, h, :]
+                out_ref[pl.ds(pl.multiple_of(half + at, page), page), lanes] = pv_ref[
+                    local, :, h, :
+                ]
 
         return count + mine.astype(jnp.int32)
 
@@ -342,7 +350,7 @@
     return within, across
 
 
-def assemble_kernel(sites, heads, spots_ref, *refs):
+def assemble_kernel(sites, heads, spans, spots_ref, *refs):
     ins, (out_ref, left, right, sem) = refs[:-4], refs[-4:]
     length = sites // LINES
     cols = out_ref.shape[1] * heads // sites
@@ -356,12 +364,13 @@
             line = at // length
             z = jnp.where(line == 0, at, 2 * length - 1 - at)
             site = z * LINES + line
-            first, second = ins[2 * d], ins[2 * d + 1]
+            size = rows if d in (0, sites // 2) else part
+            first, second = [ins[i].at[pl.ds(off, size)] for i, off in spans[d]]
 
             @pl.when(site * heads // sites == head)
             def _():
                 lane = pl.multiple_of((site - head * (sites // heads)) * cols, cols)
-                if first.shape[0] == rows:
+                if size == rows:
                     slot = 0 if d == 0 else 1
                     if go is None:
                         total = left[slot].astype(jnp.float32) + right[slot].astype(jnp.float32)
@@ -418,10 +427,10 @@
     )(
         page_list,
         me_ref,
-        new_keys.reshape(rows, wide),
-        new_values.reshape(rows, wide),
-        pool_keys.reshape(slots, page, wide),
-        pool_values.reshape(slots, page, wide),
+        new_keys,
+        new_values,
+        pool_keys,
+        pool_values,
     )
     w_other = core_swap(o_weight, n)
     q = queries.reshape(rows, qheads * width)
@@ -435,7 +444,7 @@
         for d, pieces in here.items():
             blocks.append((d, 0, pieces))
             blocks.append((d, 1, [core_swap(p, n) for p in pieces]))
-        return attend(cfg, live, me_ref, q, payload, blocks, state, step == sites // 2)
+        return attend(cfg, live, me_ref, q, payload, blocks, state, step == sites // 2), []
 
     (attended,) = ring_walk(payload, sites, look)
 
@@ -446,7 +455,7 @@
             for d, pieces in here.items():
                 (part,) = product(spots, pieces, o_weight, w_other, 0)
                 parts[d] = lax.ppermute(part, "ctx", site_perm(sites, -d)) if d else part
-            return part
+            return part, []
 
         ring_walk(attended, sites, multiply)
         order = jnp.stack(
@@ -459,29 +468,63 @@
     both = ("ctx", "head")
     arrived = {}
 
+    last = sites // 2
+    summing, crossing = [], []
+
+    def swap_heads(x):
+        return lax.ppermute(x, "head", [(0, 1), (1, 0)])
+
+    def halves(d, keep, got):
+        total = (keep + got.astype(jnp.float32)).astype(jnp.bfloat16)
+        half = total.shape[0] // 2
+        return total, ((d, total[:half]), (sites - d, total[half:]))
+
+    def cross():
+        for d, first, second in crossing:
+            got = swap_heads(jnp.concatenate([first, second], axis=0))
+            half = first.shape[0]
+            arrived[d], arrived[sites - d] = [(first, 0), (got, 0)], [(second, 0), (got, half)]
+            crossing.clear()
+            return [got]
+        return []
+
     def multiply(step, here, _):
-        if step in (0, sites // 2):
+        if step in (0, last):
             (part,) = product(spots, here[step], o_weight, w_other, 0)
+            if summing:
+                d, keep, got = summing
+                keep, got, part = lax.optimization_barrier((keep, got, part))
             within, across = back_perms(sites, heads, step)
             first = lax.ppermute(part, both, within) if step else part
-            arrived[step] = [first, lax.ppermute(part, both, across)]
-            return part
-        d, e = step, sites - step
-        keep, sent = product(spots, here[d] + here[e], o_weight, w_other, heads)
-        got = lax.ppermute(sent, "head", [(0, 1), (1, 0)])
-        total = (keep + got.astype(jnp.float32)).astype(jnp.bfloat16)
-        part = total.shape[0] // 2
-        for at, piece in ((d, total[:part]), (e, total[part:])):
-            arrived[at] = [
-                lax.ppermute(piece, both, perm) for perm in back_perms(sites, heads, at)
-            ]
-        return sent
+            arrived[step] = [(first, 0), (lax.ppermute(part, both, across), 0)]
+            cross()
+            if summing:
+                for at, piece in halves(d, keep, got)[1]:
+                    arrived[at] = [
+                        (lax.ppermute(piece, both, perm), 0)
+                        for perm in back_perms(sites, heads, at)
+                    ]
+            return [part], [arrived[step][1][0]]
+        keep, sent = product(spots, here[step] + here[sites - step], o_weight, w_other, heads)
+        got = swap_heads(sent)
+        crossed = cross()
+        if step == last - 1:
+            summing.extend((step, keep, got))
+            return [sent], crossed
+        total, pieces = halves(step, keep, got)
+        back = [lax.ppermute(p, "ctx", site_perm(sites, -at)) for at, p in pieces]
+        crossing.append((step, *back))
+        return [total], back + crossed
 
     ring_walk(attended, sites, multiply)
+    operands, spans = [], []
+    for d in range(sites):
+        spans.append([(len(operands) + i, off) for i, (_, off) in enumerate(arrived[d])])
+        operands += [x for x, _ in arrived[d]]
     return pl.pallas_call(
-        functools.partial(assemble_kernel, sites, heads),
+        functools.partial(assemble_kernel, sites, heads, spans),
         out_shape=jax.ShapeDtypeStruct((rows, sites * CORES * cols // heads), jnp.bfloat16),
-        in_specs=[smem] + [hbm] * (2 * sites),
+        in_specs=[smem] + [hbm] * len(operands),
         out_specs=vmem,
         scratch_shapes=[
             pltpu.VMEM((2, rows, CORES * cols), jnp.bfloat16),
@@ -490,7 +533,7 @@
         ],
         cost_estimate=FREE,
         name="assemble",
-    )(spots, *[a for d in range(sites) for a in arrived[d]])
+    )(spots, *operands)
 
 
 def solution(mesh):

time: 224 us -> 203 us (0.906)
  starting transfers between devices: 65.8 us -> 46.6 us
  local copies, waits for them, and re-layouts: 9.58 us -> 5.51 us
    ppermute x12 -> x4, starting transfers between devices: 31.3 us -> 8.88 us  [multiply(): lax.ppermute(piece, both, perm)]
    ppermute x5 -> x11, waiting for transfers between devices: 6.91 us -> 25.3 us  [the longest x4 18.9 us: multiply(): back = [lax.ppermute(p, 'ctx', site_perm(sites, -at)) for at, p in pieces]]
    ppermute x6, waiting for transfers between devices: 49 us -> 32.6 us  [ring_walk(): f = lax.ppermute(f, 'ctx', ahead)]
    reshape x3 -> x0, local copies, waits for them, and re-layouts: 5.35 us -> none  [the longest x1 1.8 us: on_device(): new_values.reshape(rows, wide)]
    ppermute x5 -> x11, starting transfers between devices: 14.2 us -> 17.9 us  [the longest x2 8.28 us: multiply(): arrived[step] = [(first, 0), (lax.ppermute(part, both, across), 0)]]
    unnamed x45 -> x39, local copies, waits for them, and re-layouts: 4.07 us -> 5.35 us
    ppermute x12 -> x4, waiting for transfers between devices: 11.8 us -> 11.3 us  [multiply(): lax.ppermute(piece, both, perm)]
  transfers between devices with their start and end apart: 44 -> 42, of which waited for: 21 -> 22; matrix products, arithmetic and copies ran while one was open for 3% -> 1% of each run, Pallas kernels for 31% -> 34%
where the time goes in v3:
time: 203 us; the launch traced here: 202 us
  waiting for transfers between devices  76.6 us (38%)
  Pallas kernels  72.4 us (36%)
  starting transfers between devices  46.6 us (23%)
  local copies, waits for them, and re-layouts  5.51 us (3%)
    pallas_call x5, Pallas kernels, attend(): pl.pallas_call(body, out_shape=out_shape, in_specs=[smem, smem, vmem, hbm...  35.7 us
    ppermute x6, waiting for transfers between devices, ring_walk(): f = lax.ppermute(f, 'ctx', ahead)  32.6 us
    pallas_call x5, Pallas kernels, product(): pl.pallas_call(body, out_shape=outs, grid_spec=pltpu.PrefetchScalarGridSp...  29.9 us
    ppermute x4, waiting for transfers between devices, multiply(): back = [lax.ppermute(p, 'ctx', site_perm(sites, -at)) for at, p in pieces]  18.9 us
    ppermute x4, waiting for transfers between devices, multiply(): lax.ppermute(piece, both, perm)  11.3 us
    ppermute x4, starting transfers between devices, multiply(): lax.ppermute(piece, both, perm)  8.88 us
    ppermute x2, starting transfers between devices, multiply(): arrived[step] = [(first, 0), (lax.ppermute(part, both, across), 0)]  8.28 us
    ppermute x6, starting transfers between devices, ring_walk(): f = lax.ppermute(f, 'ctx', ahead)  7.44 us
  transfers between devices with their start and end apart: 42, of which 22 were waited for; matrix products, arithmetic and copies ran while one was open for 1% of the time, Pallas kernels for 34%

profile of v3, /device:TPU:6, one launch (start us, length us, event | category | flops | bytes accessed | tf_op | source)
XLA Modules:
  0.0 202.2 jit_solution(4575004279819146879)
XLA Ops:
  0.0 3.7 %pack_pages.1.own_ref.refs_0_ = bf16[512,512]{1,0:T(8,128)(2,1)} custom-call(s32[32]{0:T(128)} %pages_ref.1, s32[1]{0:T(128)} %bitcast.3.me_ref, bf16[128,4,128]{2,1,0:T(4,128)(2,1)} %nk_ref.1, bf16[128,4,128]{2,1,0:T(4,128)(2,1)} %nv_ref.1, bf16[8,32,4,128]{3,2,1,0:T(4,128)(2,1)} %pk_ref.1, bf16[8,32,4,128]{3,2,1,0:T(4,128)(2,1)} %pv_ref.1), custom_call_target="tpu_custom_call" | custom-call | tf_op jit(solution)/shard_map/pack_pages/pallas_call | solution.py:420
  4.4 1.4 collective-permute-start.1
  5.8 1.7 copy.10
  8.1 4.8 %attend.4 = (f32[4096,128]{1,0:T(8,128)S(1)}, f32[4096,128]{1,0:T(8,128)S(1)}) custom-call(s32[16]{0:T(128)S(1)} %convert_reduce_fusion.live_ref, s32[1]{0:T(128)} %bitcast.3.me_ref, bf16[128,4096]{1,0:T(8,128)(2,1)S(1)} %bitcast.8, bf16[512,512]{1,0:T(8,128)(2,1)S(1)} %copy-done.2, bf16[512,512]{1,0:T(8,128)(2,1)S(1)} %copy-done.2, ...), custom_call_target="tpu_custom_call" | custom-call | flops 1073741824 | tf_op jit(solution)/shard_map/attend/pallas_call | solution.py:257
  12.9 5.3 %collective-permute-done.refs_0_ = bf16[512,512]{1,0:T(8,128)(2,1)S(1)} collective-permute-done((bf16[512,512]{1,0:T(8,128)(2,1)}, bf16[512,512]{1,0:T(8,128)(2,1)S(1)}, u32[]{:S(2)}, u32[]{:S(2)}) %collective-permute-start) | collective-permute-done | bytes 524320 | tf_op jit(solution)/shard_map/ppermute | solution.py:54
  19.0 1.4 collective-permute-start.3
  21.2 8.3 %attend.5 = (f32[4096,128]{1,0:T(8,128)S(1)}, f32[4096,128]{1,0:T(8,128)S(1)}) custom-call(s32[16]{0:T(128)S(1)} %convert_reduce_fusion.live_ref, s32[1]{0:T(128)} %bitcast.3.me_ref, bf16[128,4096]{1,0:T(8,128)(2,1)S(1)} %bitcast.9, bf16[512,512]{1,0:T(8,128)(2,1)S(1)} %copy-done.2, bf16[512,512]{1,0:T(8,128)(2,1)S(1)} %collective-permute-done.refs_0_, ...), custom_call_target="tpu_custom_call" | custom-call | flops 2147483648 | tf_op jit(solution)/shard_map/attend/pallas_call | solution.py:257
  29.5 3.4 %collective-permute-done.3.refs_0_ = bf16[512,512]{1,0:T(8,128)(2,1)S(1)} collective-permute-done((bf16[512,512]{1,0:T(8,128)(2,1)S(1)}, bf16[512,512]{1,0:T(8,128)(2,1)S(1)}, u32[]{:S(2)}, u32[]{:S(2)}) %collective-permute-start.3) | collective-permute-done | bytes 524320 | tf_op jit(solution)/shard_map/ppermute | solution.py:54
  34.5 1.7 collective-permute-start.7
  36.7 8.4 %attend.6 = (f32[4096,128]{1,0:T(8,128)S(1)}, f32[4096,128]{1,0:T(8,128)S(1)}) custom-call(s32[16]{0:T(128)S(1)} %convert_reduce_fusion.live_ref, s32[1]{0:T(128)} %bitcast.3.me_ref, bf16[128,4096]{1,0:T(8,128)(2,1)S(1)} %bitcast.10, bf16[512,512]{1,0:T(8,128)(2,1)S(1)} %copy-done.2, bf16[512,512]{1,0:T(8,128)(2,1)S(1)} %collective-permute-done.3.refs_0_, ...), custom_call_target="tpu_custom_call" | custom-call | flops 2147483648 | tf_op jit(solution)/shard_map/attend/pallas_call | solution.py:257
  45.0 3.3 %collective-permute-done.7.refs_0_ = bf16[512,512]{1,0:T(8,128)(2,1)S(1)} collective-permute-done((bf16[512,512]{1,0:T(8,128)(2,1)S(1)}, bf16[512,512]{1,0:T(8,128)(2,1)S(1)}, u32[]{:S(2)}, u32[]{:S(2)}) %collective-permute-start.7) | collective-permute-done | bytes 524320 | tf_op jit(solution)/shard_map/ppermute | solution.py:54
  48.3 1.4 collective-permute-done.8.refs_2_
  50.3 1.4 collective-permute-start.11
  52.4 8.7 %attend.7 = (f32[4096,128]{1,0:T(8,128)S(1)}, f32[4096,128]{1,0:T(8,128)S(1)}) custom-call(s32[16]{0:T(128)S(1)} %convert_reduce_fusion.live_ref, s32[1]{0:T(128)} %bitcast.3.me_ref, bf16[128,4096]{1,0:T(8,128)(2,1)S(1)} %bitcast.11, bf16[512,512]{1,0:T(8,128)(2,1)S(1)} %copy-done.2, bf16[512,512]{1,0:T(8,128)(2,1)S(1)} %collective-permute-done.7.refs_0_, ...), custom_call_target="tpu_custom_call" | custom-call | flops 2147483648 | tf_op jit(solution)/shard_map/attend/pallas_call | solution.py:257
  63.1 5.5 %attend_last.1.refs_0_ = bf16[128,4096]{1,0:T(8,128)(2,1)S(1)} custom-call(s32[16]{0:T(128)S(1)} %convert_reduce_fusion.live_ref, s32[1]{0:T(128)} %bitcast.3.me_ref, bf16[128,4096]{1,0:T(8,128)(2,1)S(1)} %bitcast.12, bf16[512,512]{1,0:T(8,128)(2,1)S(1)} %copy-done.2, bf16[256,512]{1,0:T(8,128)(2,1)S(1)} %collective-permute-done.11.refs_0_, ...), custom_call_target="tpu_custom_call" | custom-call | flops 1073741824 | tf_op jit(solution)/shard_map/attend_last/pallas_call | solution.py:257
  68.7 1.4 collective-permute-start.19
  70.8 2.2 %copy-done = bf16[4096,512]{1,0:T(8,128)(2,1)S(1)} copy-done((bf16[4096,512]{1,0:T(8,128)(2,1)S(1)}, bf16[4096,512]{1,0:T(8,128)(2,1)}, u32[]{:S(2)}) %copy-start) | copy-done | bytes 4194328
  73.0 5.7 %product.5.refs_0_ = bf16[128,1024]{1,0:T(8,128)(2,1)S(1)} custom-call(s32[3]{0:T(128)S(1)} %pad_add_fusion.spots_ref, bf16[128,4096]{1,0:T(8,128)(2,1)S(1)} %attend_last.1.refs_0_, bf16[4096,512]{1,0:T(8,128)(2,1)S(1)} %copy-done, bf16[4096,512]{1,0:T(8,128)(2,1)} %collective-permute-done.17.refs_2_.refs_3_), custom_call_target="tpu_custom_call" | custom-call | flops 1073741824 | tf_op jit(solution)/shard_map/product/pallas_call | solution.py:318
  78.7 15.2 %collective-permute-done.19.refs_0_ = bf16[128,4096]{1,0:T(8,128)(2,1)S(1)} collective-permute-done((bf16[128,4096]{1,0:T(8,128)(2,1)S(1)}, bf16[128,4096]{1,0:T(8,128)(2,1)S(1)}, u32[]{:S(2)}, u32[]{:S(2)}) %collective-permute-start.19) | collective-permute-done | bytes 1048608 | tf_op jit(solution)/shard_map/ppermute | solution.py:54
  95.0 1.6 collective-permute-start.25
  97.0 6.3 %product.6 = (f32[128,1024]{1,0:T(8,128)S(1)}, bf16[128,1024]{1,0:T(8,128)(2,1)S(1)}) custom-call(s32[3]{0:T(128)S(1)} %pad_add_fusion.spots_ref, bf16[128,4096]{1,0:T(8,128)(2,1)S(1)} %collective-permute-done.19.refs_0_, bf16[128,4096]{1,0:T(8,128)(2,1)S(1)} %collective-permute-done.20.refs_1_, bf16[4096,512]{1,0:T(8,128)(2,1)S(1)} %copy-done.1, ...), custom_call_target="tpu_custom_call" | custom-call | flops 2147483648 | tf_op jit(solution)/shard_map/product/pallas_call | solution.py:318
  103.9 3.4 %collective-permute-start.18 = (bf16[128,1024]{1,0:T(8,128)(2,1)S(1)}, bf16[128,1024]{1,0:T(8,128)(2,1)S(1)}, u32[]{:S(2)}, u32[]{:S(2)}) collective-permute-start(bf16[128,1024]{1,0:T(8,128)(2,1)S(1)} %product.5.refs_0_), channel_id=1, source_target_pairs={{1,0},{3,2},{9,8},{11,10},{16,17},{18,19},{24,25},{26,27},{28,29},... | collective-permute-start | bytes 786440 | tf_op jit(solution)/shard_map/ppermute | solution.py:499
  107.3 3.3 %collective-permute-done.21 = bf16[128,1024]{1,0:T(8,128)(2,1)S(1)} collective-permute-done((bf16[128,1024]{1,0:T(8,128)(2,1)S(1)}, bf16[128,1024]{1,0:T(8,128)(2,1)S(1)}, u32[]{:S(2)}, u32[]{:S(2)}) %collective-permute-start.21) | collective-permute-done | bytes 262176 | tf_op jit(solution)/shard_map/ppermute | solution.py:475
  110.6 3.0 %collective-permute-done.18.refs_1_ = bf16[128,1024]{1,0:T(8,128)(2,1)S(1)} collective-permute-done((bf16[128,1024]{1,0:T(8,128)(2,1)S(1)}, bf16[128,1024]{1,0:T(8,128)(2,1)S(1)}, u32[]{:S(2)}, u32[]{:S(2)}) %collective-permute-start.18) | collective-permute-done | bytes 262176 | tf_op jit(solution)/shard_map/ppermute | solution.py:499
  113.7 5.4 %collective-permute-done.25.refs_0_ = bf16[128,4096]{1,0:T(8,128)(2,1)S(1)} collective-permute-done((bf16[128,4096]{1,0:T(8,128)(2,1)S(1)}, bf16[128,4096]{1,0:T(8,128)(2,1)S(1)}, u32[]{:S(2)}, u32[]{:S(2)}) %collective-permute-start.25) | collective-permute-done | bytes 1048608 | tf_op jit(solution)/shard_map/ppermute | solution.py:54
  119.0 1.4 collective-permute-done.26.refs_1_
  121.0 1.4 collective-permute-start.32
  122.4 6.3 %product.7 = (f32[128,1024]{1,0:T(8,128)S(1)}, bf16[128,1024]{1,0:T(8,128)(2,1)S(1)}) custom-call(s32[3]{0:T(128)S(1)} %pad_add_fusion.spots_ref, bf16[128,4096]{1,0:T(8,128)(2,1)S(1)} %collective-permute-done.25.refs_0_, bf16[128,4096]{1,0:T(8,128)(2,1)S(1)} %collective-permute-done.26.refs_1_, bf16[4096,512]{1,0:T(8,128)(2,1)S(1)} %copy-done.1, ...), custom_call_target="tpu_custom_call" | custom-call | flops 2147483648 | tf_op jit(solution)/shard_map/product/pallas_call | solution.py:318
  129.8 1.6 collective-permute-start.23
  131.5 15.0 %collective-permute-done.22.refs_2_ = bf16[64,1024]{1,0:T(8,128)(2,1)S(1)} collective-permute-done((bf16[64,1024]{1,0:T(8,128)(2,1)S(1)}, bf16[64,1024]{1,0:T(8,128)(2,1)S(1)}, u32[]{:S(2)}, u32[]{:S(2)}) %collective-permute-start.22) | collective-permute-done | bytes 131104 | tf_op jit(solution)/shard_map/ppermute | solution.py:515
  148.0 1.5 collective-permute-start.35
  149.5 1.2 collective-permute-start.28
  150.7 1.8 collective-permute-start.29
  152.5 6.3 %product.8 = (f32[128,1024]{1,0:T(8,128)S(1)}, bf16[128,1024]{1,0:T(8,128)(2,1)S(1)}) custom-call(s32[3]{0:T(128)S(1)} %pad_add_fusion.spots_ref, bf16[128,4096]{1,0:T(8,128)(2,1)S(1)} %collective-permute-done.31.refs_0_, bf16[128,4096]{1,0:T(8,128)(2,1)S(1)} %collective-permute-done.32.refs_1_, bf16[4096,512]{1,0:T(8,128)(2,1)S(1)} %copy-done.1, ...), custom_call_target="tpu_custom_call" | custom-call | flops 2147483648 | tf_op jit(solution)/shard_map/product/pallas_call | solution.py:318
  158.7 3.9 %collective-permute-done.28.refs_4_ = bf16[64,1024]{1,0:T(8,128)(2,1)S(1)} collective-permute-done((bf16[64,1024]{1,0:T(8,128)(2,1)S(1)}, bf16[64,1024]{1,0:T(8,128)(2,1)S(1)}, u32[]{:S(2)}, u32[]{:S(2)}) %collective-permute-start.28) | collective-permute-done | bytes 131104 | tf_op jit(solution)/shard_map/ppermute | solution.py:515
  162.6 1.5 collective-permute-start.33
  164.1 1.3 collective-permute-start.30
  165.4 5.4 %product.9 = bf16[128,1024]{1,0:T(8,128)(2,1)S(1)} custom-call(s32[3]{0:T(128)S(1)} %pad_add_fusion.spots_ref, bf16[64,4096]{1,0:T(8,128)(2,1)S(1)} %collective-permute-done.34.refs_0_, bf16[64,4096]{1,0:T(8,128)(2,1)S(1)} %collective-permute-done.35.refs_1_, bf16[4096,512]{1,0:T(8,128)(2,1)S(1)} %copy-done.1, ...), custom_call_target="tpu_custom_call" | custom-call | flops 1073741824 | tf_op jit(solution)/shard_map/product/pallas_call | solution.py:318
  171.0 1.3 collective-permute-start.36
  172.3 1.3 collective-permute-start.38
  173.6 4.9 %collective-permute-start.39 = (bf16[128,1024]{1,0:T(8,128)(2,1)S(1)}, bf16[128,1024]{1,0:T(8,128)(2,1)S(1)}, u32[]{:S(2)}, u32[]{:S(2)}) collective-permute-start(bf16[128,1024]{1,0:T(8,128)(2,1)S(1)} %product.9), channel_id=1, source_target_pairs={{1,28},{3,30},{9,20},{11,22},{16,13},{18,15},{24,5},{26,7},{28,1},... | collective-permute-start | bytes 786440 | tf_op jit(solution)/shard_map/ppermute | solution.py:499
  178.5 4.4 %collective-permute-start.37 = (bf16[64,1024]{1,0:T(8,128)(2,1)S(1)}, bf16[64,1024]{1,0:T(8,128)(2,1)S(1)}, u32[]{:S(2)}, u32[]{:S(2)}) collective-permute-start(bf16[64,1024]{1,0:T(8,128)(2,1)S(1)} %get-tuple-element.88), channel_id=1, source_target_pairs={{1,20},{3,22},{9,12},{11,14},{16,5},{18,7},{24,1},{26,3},{28,9},{3... | collective-permute-start | bytes 393224 | tf_op jit(solution)/shard_map/ppermute | solution.py:504
  182.9 1.3 collective-permute-start.40
  184.2 3.7 %collective-permute-done.36.refs_6_ = bf16[64,1024]{1,0:T(8,128)(2,1)S(1)} collective-permute-done((bf16[64,1024]{1,0:T(8,128)(2,1)S(1)}, bf16[64,1024]{1,0:T(8,128)(2,1)S(1)}, u32[]{:S(2)}, u32[]{:S(2)}) %collective-permute-start.36) | collective-permute-done | bytes 131104 | tf_op jit(solution)/shard_map/ppermute | solution.py:504
  187.9 1.9 collective-permute-start.41
  189.8 2.3 %collective-permute-done.37.refs_7_ = bf16[64,1024]{1,0:T(8,128)(2,1)S(1)} collective-permute-done((bf16[64,1024]{1,0:T(8,128)(2,1)S(1)}, bf16[64,1024]{1,0:T(8,128)(2,1)S(1)}, u32[]{:S(2)}, u32[]{:S(2)}) %collective-permute-start.37) | collective-permute-done | bytes 131104 | tf_op jit(solution)/shard_map/ppermute | solution.py:504
  192.1 5.3 %collective-permute-done.41.refs_11_ = bf16[64,1024]{1,0:T(8,128)(2,1)S(1)} collective-permute-done((bf16[64,1024]{1,0:T(8,128)(2,1)S(1)}, bf16[64,1024]{1,0:T(8,128)(2,1)S(1)}, u32[]{:S(2)}, u32[]{:S(2)}) %collective-permute-start.41) | collective-permute-done | bytes 131104 | tf_op jit(solution)/shard_map/ppermute | solution.py:504
  198.9 3.1 %assemble.1 = bf16[128,4096]{1,0:T(8,128)(2,1)} custom-call(s32[3]{0:T(128)} %copy-done.4, bf16[128,1024]{1,0:T(8,128)(2,1)} %copy-done.3, bf16[128,1024]{1,0:T(8,128)(2,1)} %copy-done.11, bf16[64,1024]{1,0:T(8,128)(2,1)} %copy-done.7, bf16[128,1024]{1,0:T(8,128)(2,1)} %copy-done.5, bf16[64,1024]{1,0:T(8,128)(2,1)} %copy-done.9, ...), custom_call_target="tpu_custom_call" | custom-call | tf_op jit(solution)/shard_map/assemble/pallas_call | solution.py:524
  (102 shorter events, 15.7 us)
Async XLA Ops:
  0.0 70.8 %collective-permute-start.17 = (bf16[4096,512]{1,0:T(8,128)(2,1)}, bf16[4096,512]{1,0:T(8,128)(2,1)}, u32[]{:S(2)}, u32[]{:S(2)}) collective-permute-start(bf16[4096,512]{1,0:T(8,128)(2,1)} %refs_2_.7), channel_id=1, source_target_pairs={{0,2},{2,0},{4,6},{6,4},{8,10},{10,8},{12,14},{14,12},{16,18},{18,... | collective-permute-start | bytes 12582920 | tf_op jit(solution)/shard_map/ppermute | solution.py:43
  3.7 4.4 %collective-permute-start.2 = (bf16[512,512]{1,0:T(8,128)(2,1)}, bf16[512,512]{1,0:T(8,128)(2,1)S(1)}, u32[]{:S(2)}, u32[]{:S(2)}) collective-permute-start(bf16[512,512]{1,0:T(8,128)(2,1)} %pack_pages.1.own_ref.refs_0_), channel_id=1, source_target_pairs={{0,2},{2,0},{4,6},{6,4},{8,10},{10,8},{12,14},{14,12},{16,18},{18,... | collective-permute-start | bytes 1572872 | tf_op jit(solution)/shard_map/ppermute | solution.py:43
  3.8 14.5 %collective-permute-start = (bf16[512,512]{1,0:T(8,128)(2,1)}, bf16[512,512]{1,0:T(8,128)(2,1)S(1)}, u32[]{:S(2)}, u32[]{:S(2)}) collective-permute-start(bf16[512,512]{1,0:T(8,128)(2,1)} %pack_pages.1.own_ref.refs_0_), channel_id=1, source_target_pairs={{0,8},{2,10},{8,16},{10,18},{16,24},{18,26},{24,28},{26,30},{28,20... | collective-permute-start | bytes 1572872 | tf_op jit(solution)/shard_map/ppermute | solution.py:54
  4.4 14.1 %collective-permute-start.1 = (bf16[512,512]{1,0:T(8,128)(2,1)}, bf16[512,512]{1,0:T(8,128)(2,1)S(1)}, u32[]{:S(2)}, u32[]{:S(2)}) collective-permute-start(bf16[512,512]{1,0:T(8,128)(2,1)} %pack_pages.1.own_ref.refs_0_), channel_id=1, source_target_pairs={{0,4},{2,6},{8,0},{10,2},{16,8},{18,10},{24,16},{26,18},{28,24},{3... | collective-permute-start | bytes 1572872 | tf_op jit(solution)/shard_map/ppermute | solution.py:55
  18.5 2.5 %collective-permute-start.5 = (bf16[512,512]{1,0:T(8,128)(2,1)S(1)}, bf16[512,512]{1,0:T(8,128)(2,1)S(1)}, u32[]{:S(2)}, u32[]{:S(2)}) collective-permute-start(bf16[512,512]{1,0:T(8,128)(2,1)S(1)} %collective-permute-done.refs_0_), channel_id=1, source_target_pairs={{0,2},{2,0},{4,6},{6,4},{8,10},{10,8},{12,14},{14,12},{16,18},{18,... | collective-permute-start | bytes 1572872 | tf_op jit(solution)/shard_map/ppermute | solution.py:43
  18.5 2.7 %collective-permute-start.6 = (bf16[512,512]{1,0:T(8,128)(2,1)S(1)}, bf16[512,512]{1,0:T(8,128)(2,1)S(1)}, u32[]{:S(2)}, u32[]{:S(2)}) collective-permute-start(bf16[512,512]{1,0:T(8,128)(2,1)S(1)} %collective-permute-done.1.refs_2_), channel_id=1, source_target_pairs={{0,2},{2,0},{4,6},{6,4},{8,10},{10,8},{12,14},{14,12},{16,18},{18,... | collective-permute-start | bytes 1572872 | tf_op jit(solution)/shard_map/ppermute | solution.py:43
  19.0 13.8 %collective-permute-start.3 = (bf16[512,512]{1,0:T(8,128)(2,1)S(1)}, bf16[512,512]{1,0:T(8,128)(2,1)S(1)}, u32[]{:S(2)}, u32[]{:S(2)}) collective-permute-start(bf16[512,512]{1,0:T(8,128)(2,1)S(1)} %collective-permute-done.refs_0_), channel_id=1, source_target_pairs={{0,8},{2,10},{8,16},{10,18},{16,24},{18,26},{24,28},{26,30},{28,20... | collective-permute-start | bytes 1572872 | tf_op jit(solution)/shard_map/ppermute | solution.py:54
  20.4 13.6 %collective-permute-start.4 = (bf16[512,512]{1,0:T(8,128)(2,1)S(1)}, bf16[512,512]{1,0:T(8,128)(2,1)S(1)}, u32[]{:S(2)}, u32[]{:S(2)}) collective-permute-start(bf16[512,512]{1,0:T(8,128)(2,1)S(1)} %collective-permute-done.1.refs_2_), channel_id=1, source_target_pairs={{0,4},{2,6},{8,0},{10,2},{16,8},{18,10},{24,16},{26,18},{28,24},{3... | collective-permute-start | bytes 1572872 | tf_op jit(solution)/shard_map/ppermute | solution.py:55
  34.0 2.5 %collective-permute-start.10 = (bf16[512,512]{1,0:T(8,128)(2,1)S(1)}, bf16[512,512]{1,0:T(8,128)(2,1)S(1)}, u32[]{:S(2)}, u32[]{:S(2)}) collective-permute-start(bf16[512,512]{1,0:T(8,128)(2,1)S(1)} %collective-permute-done.4.refs_2_), channel_id=1, source_target_pairs={{0,2},{2,0},{4,6},{6,4},{8,10},{10,8},{12,14},{14,12},{16,18},{18,... | collective-permute-start | bytes 1572872 | tf_op jit(solution)/shard_map/ppermute | solution.py:43
  34.0 2.7 %collective-permute-start.9 = (bf16[512,512]{1,0:T(8,128)(2,1)S(1)}, bf16[512,512]{1,0:T(8,128)(2,1)S(1)}, u32[]{:S(2)}, u32[]{:S(2)}) collective-permute-start(bf16[512,512]{1,0:T(8,128)(2,1)S(1)} %collective-permute-done.3.refs_0_), channel_id=1, source_target_pairs={{0,2},{2,0},{4,6},{6,4},{8,10},{10,8},{12,14},{14,12},{16,18},{18,... | collective-permute-start | bytes 1572872 | tf_op jit(solution)/shard_map/ppermute | solution.py:43
  34.5 13.8 %collective-permute-start.7 = (bf16[512,512]{1,0:T(8,128)(2,1)S(1)}, bf16[512,512]{1,0:T(8,128)(2,1)S(1)}, u32[]{:S(2)}, u32[]{:S(2)}) collective-permute-start(bf16[512,512]{1,0:T(8,128)(2,1)S(1)} %collective-permute-done.3.refs_0_), channel_id=1, source_target_pairs={{0,8},{2,10},{8,16},{10,18},{16,24},{18,26},{24,28},{26,30},{28,20... | collective-permute-start | bytes 1572872 | tf_op jit(solution)/shard_map/ppermute | solution.py:54
  36.2 13.6 %collective-permute-start.8 = (bf16[512,512]{1,0:T(8,128)(2,1)S(1)}, bf16[512,512]{1,0:T(8,128)(2,1)S(1)}, u32[]{:S(2)}, u32[]{:S(2)}) collective-permute-start(bf16[512,512]{1,0:T(8,128)(2,1)S(1)} %collective-permute-done.4.refs_2_), channel_id=1, source_target_pairs={{0,4},{2,6},{8,0},{10,2},{16,8},{18,10},{24,16},{26,18},{28,24},{3... | collective-permute-start | bytes 1572872 | tf_op jit(solution)/shard_map/ppermute | solution.py:55
  49.8 2.6 %collective-permute-start.13 = (bf16[512,512]{1,0:T(8,128)(2,1)S(1)}, bf16[512,512]{1,0:T(8,128)(2,1)S(1)}, u32[]{:S(2)}, u32[]{:S(2)}) collective-permute-start(bf16[512,512]{1,0:T(8,128)(2,1)S(1)} %collective-permute-done.7.refs_0_), channel_id=1, source_target_pairs={{0,2},{2,0},{4,6},{6,4},{8,10},{10,8},{12,14},{14,12},{16,18},{18,... | collective-permute-start | bytes 1572872 | tf_op jit(solution)/shard_map/ppermute | solution.py:43
  49.8 2.7 %collective-permute-start.14 = (bf16[512,512]{1,0:T(8,128)(2,1)S(1)}, bf16[512,512]{1,0:T(8,128)(2,1)S(1)}, u32[]{:S(2)}, u32[]{:S(2)}) collective-permute-start(bf16[512,512]{1,0:T(8,128)(2,1)S(1)} %collective-permute-done.8.refs_2_), channel_id=1, source_target_pairs={{0,2},{2,0},{4,6},{6,4},{8,10},{10,8},{12,14},{14,12},{16,18},{18,... | collective-permute-start | bytes 1572872 | tf_op jit(solution)/shard_map/ppermute | solution.py:43
  50.3 10.8 %collective-permute-start.11 = (bf16[256,512]{1,0:T(8,128)(2,1)S(1)}, bf16[256,512]{1,0:T(8,128)(2,1)S(1)}, u32[]{:S(2)}, u32[]{:S(2)}) collective-permute-start(bf16[256,512]{1,0:T(8,128)(2,1)S(1)} %slice.30), channel_id=1, source_target_pairs={{0,8},{2,10},{8,16},{10,18},{16,24},{18,26},{24,28},{26,30},{28,20... | collective-permute-start | bytes 786440 | tf_op jit(solution)/shard_map/ppermute | solution.py:59
  51.7 9.4 %collective-permute-start.12 = (bf16[256,512]{1,0:T(8,128)(2,1)S(1)}, bf16[256,512]{1,0:T(8,128)(2,1)S(1)}, u32[]{:S(2)}, u32[]{:S(2)}) collective-permute-start(bf16[256,512]{1,0:T(8,128)(2,1)S(1)} %slice.31), channel_id=1, source_target_pairs={{0,4},{2,6},{8,0},{10,2},{16,8},{18,10},{24,16},{26,18},{28,24},{3... | collective-permute-start | bytes 786440 | tf_op jit(solution)/shard_map/ppermute | solution.py:60
  61.1 1.6 collective-permute-start.15
  61.4 1.8 collective-permute-start.16
  68.7 25.3 %collective-permute-start.19 = (bf16[128,4096]{1,0:T(8,128)(2,1)S(1)}, bf16[128,4096]{1,0:T(8,128)(2,1)S(1)}, u32[]{:S(2)}, u32[]{:S(2)}) collective-permute-start(bf16[128,4096]{1,0:T(8,128)(2,1)S(1)} %attend_last.1.refs_0_), channel_id=1, source_target_pairs={{0,8},{2,10},{8,16},{10,18},{16,24},{18,26},{24,28},{26,30},{28,20... | collective-permute-start | bytes 3145736 | tf_op jit(solution)/shard_map/ppermute | solution.py:54
  70.1 24.9 %collective-permute-start.20 = (bf16[128,4096]{1,0:T(8,128)(2,1)S(1)}, bf16[128,4096]{1,0:T(8,128)(2,1)S(1)}, u32[]{:S(2)}, u32[]{:S(2)}) collective-permute-start(bf16[128,4096]{1,0:T(8,128)(2,1)S(1)} %attend_last.1.refs_0_), channel_id=1, source_target_pairs={{0,4},{2,6},{8,0},{10,2},{16,8},{18,10},{24,16},{26,18},{28,24},{3... | collective-permute-start | bytes 3145736 | tf_op jit(solution)/shard_map/ppermute | solution.py:55
  70.8 94.6 %copy-start.4 = (s32[3]{0:T(128)}, s32[3]{0:T(128)S(1)}, u32[]{:S(2)}) copy-start(s32[3]{0:T(128)S(1)} %pad_add_fusion.spots_ref) | copy-start | bytes 40
  73.0 24.0 %copy-start.1 = (bf16[4096,512]{1,0:T(8,128)(2,1)S(1)}, bf16[4096,512]{1,0:T(8,128)(2,1)}, u32[]{:S(2)}) copy-start(bf16[4096,512]{1,0:T(8,128)(2,1)} %refs_2_.7) | copy-start | bytes 12582916
  78.7 25.2 %copy-start.3 = (bf16[128,1024]{1,0:T(8,128)(2,1)}, bf16[128,1024]{1,0:T(8,128)(2,1)S(1)}, u32[]{:S(2)}) copy-start(bf16[128,1024]{1,0:T(8,128)(2,1)S(1)} %product.5.refs_0_) | copy-start | bytes 786436
  95.0 24.0 %collective-permute-start.25 = (bf16[128,4096]{1,0:T(8,128)(2,1)S(1)}, bf16[128,4096]{1,0:T(8,128)(2,1)S(1)}, u32[]{:S(2)}, u32[]{:S(2)}) collective-permute-start(bf16[128,4096]{1,0:T(8,128)(2,1)S(1)} %collective-permute-done.19.refs_0_), channel_id=1, source_target_pairs={{0,8},{2,10},{8,16},{10,18},{16,24},{18,26},{24,28},{26,30},{28,20... | collective-permute-start | bytes 3145736 | tf_op jit(solution)/shard_map/ppermute | solution.py:54
  96.6 23.8 %collective-permute-start.26 = (bf16[128,4096]{1,0:T(8,128)(2,1)S(1)}, bf16[128,4096]{1,0:T(8,128)(2,1)S(1)}, u32[]{:S(2)}, u32[]{:S(2)}) collective-permute-start(bf16[128,4096]{1,0:T(8,128)(2,1)S(1)} %collective-permute-done.20.refs_1_), channel_id=1, source_target_pairs={{0,4},{2,6},{8,0},{10,2},{16,8},{18,10},{24,16},{26,18},{28,24},{3... | collective-permute-start | bytes 3145736 | tf_op jit(solution)/shard_map/ppermute | solution.py:55
  103.3 7.3 %collective-permute-start.21 = (bf16[128,1024]{1,0:T(8,128)(2,1)S(1)}, bf16[128,1024]{1,0:T(8,128)(2,1)S(1)}, u32[]{:S(2)}, u32[]{:S(2)}) collective-permute-start(bf16[128,1024]{1,0:T(8,128)(2,1)S(1)} %get-tuple-element.73), channel_id=1, source_target_pairs={{0,1},{1,0},{2,3},{3,2},{4,5},{5,4},{6,7},{7,6},{8,9},{9,8},{10,11... | collective-permute-start | bytes 786440 | tf_op jit(solution)/shard_map/ppermute | solution.py:475
  103.9 9.8 %collective-permute-start.18 = (bf16[128,1024]{1,0:T(8,128)(2,1)S(1)}, bf16[128,1024]{1,0:T(8,128)(2,1)S(1)}, u32[]{:S(2)}, u32[]{:S(2)}) collective-permute-start(bf16[128,1024]{1,0:T(8,128)(2,1)S(1)} %product.5.refs_0_), channel_id=1, source_target_pairs={{1,0},{3,2},{9,8},{11,10},{16,17},{18,19},{24,25},{26,27},{28,29},... | collective-permute-start | bytes 786440 | tf_op jit(solution)/shard_map/ppermute | solution.py:499
  113.7 15.1 %copy-start.11 = (bf16[128,1024]{1,0:T(8,128)(2,1)}, bf16[128,1024]{1,0:T(8,128)(2,1)S(1)}, u32[]{:S(2)}) copy-start(bf16[128,1024]{1,0:T(8,128)(2,1)S(1)} %collective-permute-done.18.refs_1_) | copy-start | bytes 786436
  120.4 26.8 %collective-permute-start.31 = (bf16[128,4096]{1,0:T(8,128)(2,1)S(1)}, bf16[128,4096]{1,0:T(8,128)(2,1)S(1)}, u32[]{:S(2)}, u32[]{:S(2)}) collective-permute-start(bf16[128,4096]{1,0:T(8,128)(2,1)S(1)} %collective-permute-done.25.refs_0_), channel_id=1, source_target_pairs={{0,8},{2,10},{8,16},{10,18},{16,24},{18,26},{24,28},{26,30},{28,20... | collective-permute-start | bytes 3145736 | tf_op jit(solution)/shard_map/ppermute | solution.py:54
  121.0 26.2 %collective-permute-start.32 = (bf16[128,4096]{1,0:T(8,128)(2,1)S(1)}, bf16[128,4096]{1,0:T(8,128)(2,1)S(1)}, u32[]{:S(2)}, u32[]{:S(2)}) collective-permute-start(bf16[128,4096]{1,0:T(8,128)(2,1)S(1)} %collective-permute-done.26.refs_1_), channel_id=1, source_target_pairs={{0,4},{2,6},{8,0},{10,2},{16,8},{18,10},{24,16},{26,18},{28,24},{3... | collective-permute-start | bytes 3145736 | tf_op jit(solution)/shard_map/ppermute | solution.py:55
  128.8 18.4 %collective-permute-start.27 = (bf16[128,1024]{1,0:T(8,128)(2,1)S(1)}, bf16[128,1024]{1,0:T(8,128)(2,1)S(1)}, u32[]{:S(2)}, u32[]{:S(2)}) collective-permute-start(bf16[128,1024]{1,0:T(8,128)(2,1)S(1)} %get-tuple-element.77), channel_id=1, source_target_pairs={{0,1},{1,0},{2,3},{3,2},{4,5},{5,4},{6,7},{7,6},{8,9},{9,8},{10,11... | collective-permute-start | bytes 786440 | tf_op jit(solution)/shard_map/ppermute | solution.py:475
  129.4 17.1 %collective-permute-start.22 = (bf16[64,1024]{1,0:T(8,128)(2,1)S(1)}, bf16[64,1024]{1,0:T(8,128)(2,1)S(1)}, u32[]{:S(2)}, u32[]{:S(2)}) collective-permute-start(bf16[64,1024]{1,0:T(8,128)(2,1)S(1)} %get-tuple-element.92), channel_id=1, source_target_pairs={{0,4},{2,6},{8,0},{10,2},{16,8},{18,10},{24,16},{26,18},{28,24},{3... | collective-permute-start | bytes 393224 | tf_op jit(solution)/shard_map/ppermute | solution.py:515
  129.8 16.7 %collective-permute-start.23 = (bf16[64,1024]{1,0:T(8,128)(2,1)S(1)}, bf16[64,1024]{1,0:T(8,128)(2,1)S(1)}, u32[]{:S(2)}, u32[]{:S(2)}) collective-permute-start(bf16[64,1024]{1,0:T(8,128)(2,1)S(1)} %get-tuple-element.91), channel_id=1, source_target_pairs={{0,8},{2,10},{8,16},{10,18},{16,24},{18,26},{24,28},{26,30},{28,20... | collective-permute-start | bytes 393224 | tf_op jit(solution)/shard_map/ppermute | solution.py:515
  146.5 18.9 %collective-permute-start.24 = (bf16[128,1024]{1,0:T(8,128)(2,1)S(1)}, bf16[128,1024]{1,0:T(8,128)(2,1)S(1)}, u32[]{:S(2)}, u32[]{:S(2)}) collective-permute-start(bf16[128,1024]{1,0:T(8,128)(2,1)S(1)} %pad_maximum_fusion), channel_id=1, source_target_pairs={{0,1},{1,0},{2,3},{3,2},{4,5},{5,4},{6,7},{7,6},{8,9},{9,8},{10,11... | collective-permute-start | bytes 786440 | tf_op jit(solution)/shard_map/ppermute | solution.py:475
  147.3 18.1 %collective-permute-start.34 = (bf16[64,4096]{1,0:T(8,128)(2,1)S(1)}, bf16[64,4096]{1,0:T(8,128)(2,1)S(1)}, u32[]{:S(2)}, u32[]{:S(2)}) collective-permute-start(bf16[64,4096]{1,0:T(8,128)(2,1)S(1)} %slice.36), channel_id=1, source_target_pairs={{0,8},{2,10},{8,16},{10,18},{16,24},{18,26},{24,28},{26,30},{28,20... | collective-permute-start | bytes 1572872 | tf_op jit(solution)/shard_map/ppermute | solution.py:59
  148.0 17.4 %collective-permute-start.35 = (bf16[64,4096]{1,0:T(8,128)(2,1)S(1)}, bf16[64,4096]{1,0:T(8,128)(2,1)S(1)}, u32[]{:S(2)}, u32[]{:S(2)}) collective-permute-start(bf16[64,4096]{1,0:T(8,128)(2,1)S(1)} %slice.37), channel_id=1, source_target_pairs={{0,4},{2,6},{8,0},{10,2},{16,8},{18,10},{24,16},{26,18},{28,24},{3... | collective-permute-start | bytes 1572872 | tf_op jit(solution)/shard_map/ppermute | solution.py:60
  149.5 13.1 %collective-permute-start.28 = (bf16[64,1024]{1,0:T(8,128)(2,1)S(1)}, bf16[64,1024]{1,0:T(8,128)(2,1)S(1)}, u32[]{:S(2)}, u32[]{:S(2)}) collective-permute-start(bf16[64,1024]{1,0:T(8,128)(2,1)S(1)} %get-tuple-element.90), channel_id=1, source_target_pairs={{0,12},{2,14},{8,4},{10,6},{16,0},{18,2},{24,8},{26,10},{28,16},{3... | collective-permute-start | bytes 393224 | tf_op jit(solution)/shard_map/ppermute | solution.py:515
  150.7 13.4 %collective-permute-start.29 = (bf16[64,1024]{1,0:T(8,128)(2,1)S(1)}, bf16[64,1024]{1,0:T(8,128)(2,1)S(1)}, u32[]{:S(2)}, u32[]{:S(2)}) collective-permute-start(bf16[64,1024]{1,0:T(8,128)(2,1)S(1)} %get-tuple-element.89), channel_id=1, source_target_pairs={{0,16},{2,18},{8,24},{10,26},{16,28},{18,30},{24,20},{26,22},{28,1... | collective-permute-start | bytes 393224 | tf_op jit(solution)/shard_map/ppermute | solution.py:515
  162.6 8.3 %collective-permute-start.33 = (bf16[128,1024]{1,0:T(8,128)(2,1)S(1)}, bf16[128,1024]{1,0:T(8,128)(2,1)S(1)}, u32[]{:S(2)}, u32[]{:S(2)}) collective-permute-start(bf16[128,1024]{1,0:T(8,128)(2,1)S(1)} %get-tuple-element.81), channel_id=1, source_target_pairs={{0,1},{1,0},{2,3},{3,2},{4,5},{5,4},{6,7},{7,6},{8,9},{9,8},{10,11... | collective-permute-start | bytes 786440 | tf_op jit(solution)/shard_map/ppermute | solution.py:475
  164.1 18.8 %collective-permute-start.30 = (bf16[128,1024]{1,0:T(8,128)(2,1)S(1)}, bf16[128,1024]{1,0:T(8,128)(2,1)S(1)}, u32[]{:S(2)}, u32[]{:S(2)}) collective-permute-start(bf16[128,1024]{1,0:T(8,128)(2,1)S(1)} %pad_maximum_fusion.1), channel_id=1, source_target_pairs={{0,1},{1,0},{2,3},{3,2},{4,5},{5,4},{6,7},{7,6},{8,9},{9,8},{10,11... | collective-permute-start | bytes 786440 | tf_op jit(solution)/shard_map/ppermute | solution.py:475
  171.0 16.9 %collective-permute-start.36 = (bf16[64,1024]{1,0:T(8,128)(2,1)S(1)}, bf16[64,1024]{1,0:T(8,128)(2,1)S(1)}, u32[]{:S(2)}, u32[]{:S(2)}) collective-permute-start(bf16[64,1024]{1,0:T(8,128)(2,1)S(1)} %get-tuple-element.88), channel_id=1, source_target_pairs={{0,20},{2,22},{8,12},{10,14},{17,5},{19,7},{25,1},{27,3},{29,9},{3... | collective-permute-start | bytes 393224 | tf_op jit(solution)/shard_map/ppermute | solution.py:504
  172.3 25.1 %collective-permute-start.38 = (bf16[128,1024]{1,0:T(8,128)(2,1)S(1)}, bf16[128,1024]{1,0:T(8,128)(2,1)S(1)}, u32[]{:S(2)}, u32[]{:S(2)}) collective-permute-start(bf16[128,1024]{1,0:T(8,128)(2,1)S(1)} %product.9), channel_id=1, source_target_pairs={{0,28},{2,30},{8,20},{10,22},{17,13},{19,15},{25,5},{27,7},{29,1},... | collective-permute-start | bytes 786440 | tf_op jit(solution)/shard_map/ppermute | solution.py:498
  173.6 23.8 %collective-permute-start.39 = (bf16[128,1024]{1,0:T(8,128)(2,1)S(1)}, bf16[128,1024]{1,0:T(8,128)(2,1)S(1)}, u32[]{:S(2)}, u32[]{:S(2)}) collective-permute-start(bf16[128,1024]{1,0:T(8,128)(2,1)S(1)} %product.9), channel_id=1, source_target_pairs={{1,28},{3,30},{9,20},{11,22},{16,13},{18,15},{24,5},{26,7},{28,1},... | collective-permute-start | bytes 786440 | tf_op jit(solution)/shard_map/ppermute | solution.py:499
  178.5 13.6 %collective-permute-start.37 = (bf16[64,1024]{1,0:T(8,128)(2,1)S(1)}, bf16[64,1024]{1,0:T(8,128)(2,1)S(1)}, u32[]{:S(2)}, u32[]{:S(2)}) collective-permute-start(bf16[64,1024]{1,0:T(8,128)(2,1)S(1)} %get-tuple-element.88), channel_id=1, source_target_pairs={{1,20},{3,22},{9,12},{11,14},{16,5},{18,7},{24,1},{26,3},{28,9},{3... | collective-permute-start | bytes 393224 | tf_op jit(solution)/shard_map/ppermute | solution.py:504
  182.9 14.5 %copy-start.6 = (bf16[128,1024]{1,0:T(8,128)(2,1)}, bf16[128,1024]{1,0:T(8,128)(2,1)S(1)}, u32[]{:S(2)}) copy-start(bf16[128,1024]{1,0:T(8,128)(2,1)S(1)} %collective-permute-done.30.refs_5_.refs_13_) | copy-start | bytes 786436
  182.9 9.2 %collective-permute-start.40 = (bf16[64,1024]{1,0:T(8,128)(2,1)S(1)}, bf16[64,1024]{1,0:T(8,128)(2,1)S(1)}, u32[]{:S(2)}, u32[]{:S(2)}) collective-permute-start(bf16[64,1024]{1,0:T(8,128)(2,1)S(1)} %get-tuple-element.87), channel_id=1, source_target_pairs={{0,24},{2,26},{8,28},{10,30},{17,21},{19,23},{25,13},{27,15},{29,5... | collective-permute-start | bytes 393224 | tf_op jit(solution)/shard_map/ppermute | solution.py:504
  187.9 9.6 %copy-start.14 = (bf16[64,1024]{1,0:T(8,128)(2,1)}, bf16[64,1024]{1,0:T(8,128)(2,1)S(1)}, u32[]{:S(2)}) copy-start(bf16[64,1024]{1,0:T(8,128)(2,1)S(1)} %collective-permute-done.36.refs_6_) | copy-start | bytes 393220
  187.9 9.5 %collective-permute-start.41 = (bf16[64,1024]{1,0:T(8,128)(2,1)S(1)}, bf16[64,1024]{1,0:T(8,128)(2,1)S(1)}, u32[]{:S(2)}, u32[]{:S(2)}) collective-permute-start(bf16[64,1024]{1,0:T(8,128)(2,1)S(1)} %get-tuple-element.87), channel_id=1, source_target_pairs={{1,24},{3,26},{9,28},{11,30},{16,21},{18,23},{24,13},{26,15},{28,5... | collective-permute-start | bytes 393224 | tf_op jit(solution)/shard_map/ppermute | solution.py:504
  (13 other events, 53.3 us)

commit v4 on v3

--- a/solution.py
+++ b/solution.py
@@ -11,7 +11,8 @@
 CORES = 2
 LINES = 2
 NEG = -1e30
-VMEM_LIMIT = 32 * 1024 * 1024
+VMEM_LIMIT = 24 * 1024 * 1024
+SMALL_LIMIT = 12 * 1024 * 1024
 FREE = pl.CostEstimate(flops=0, bytes_accessed=0, transcendentals=0)
 
 
@@ -44,26 +45,23 @@
 
 
 def ring_walk(block, sites, work):
-    ahead = site_perm(sites, 1)
-    back = site_perm(sites, -1)
-    here, done, late = {0: [block]}, None, []
+    steps = sites // 2
+    here, done = {0: [block]}, None
     f = b = block
-    steps = sites // 2
     for step in range(1, steps + 1):
         if step < steps or sites % 2:
-            f = lax.ppermute(f, "ctx", ahead)
-            b = lax.ppermute(b, "ctx", back)
+            f = lax.ppermute(f, "ctx", site_perm(sites, 1))
+            b = lax.ppermute(b, "ctx", site_perm(sites, -1))
             arrived = {step: [f], sites - step: [b]}
         else:
             half = block.shape[0] // 2
-            f = lax.ppermute(f[:half], "ctx", ahead)
-            b = lax.ppermute(b[half:], "ctx", back)
+            f = lax.ppermute(f[:half], "ctx", site_perm(sites, 1))
+            b = lax.ppermute(b[half:], "ctx", site_perm(sites, -1))
             arrived = {step: [f, b]}
-        done, later = work(step - 1, here, done)
-        f, b, done, _ = lax.optimization_barrier((f, b, done, late))
-        late = later
+        done = work(step - 1, here, done)
+        f, b, done = lax.optimization_barrier((f, b, done))
         here = {d: [f, b] if len(p) == 2 else [f] if d == step else [b] for d, p in arrived.items()}
-    return work(steps, here, done)[0]
+    return work(steps, here, done)
 
 
 def pack_kernel(slots, pages_ref, me_ref, nk_ref, nv_ref, pk_ref, pv_ref, out_ref):
@@ -286,49 +284,36 @@
     def body(spots_ref, *refs):
         a_refs, rest = refs[: len(pieces)], refs[len(pieces) :]
         own_ref, other_ref, *outs = rest
-
-        def run(w_ref):
-            a = jnp.concatenate([r[...] for r in a_refs], axis=0)
-            out = jnp.dot(a, w_ref[...], preferred_element_type=jnp.float32)
+        core, head = spots_ref[0], spots_ref[1]
+        a = jnp.concatenate([r[...] for r in a_refs], axis=0)
+        for t in range(2 * half):
+            w_ref = own_ref if t < half else other_ref
+            at = pl.multiple_of(lax.rem(t + half * core, 2 * half) * tile, tile)
+            lanes = pl.ds(at, tile)
+            columns = slice((t % half) * tile, (t % half + 1) * tile)
+            out = jnp.dot(a, w_ref[:, columns], preferred_element_type=jnp.float32)
             if not split:
-                outs[0][...] = out.astype(jnp.bfloat16)
-                return
+                outs[0][:, lanes] = out.astype(jnp.bfloat16)
+                continue
             keep_ref, sent_ref, acc = outs
             acc[...] = out
-            head = spots_ref[1]
             for b in range(blocks):
-                keep_ref[b * part : (b + 1) * part, :] = acc[
-                    pl.ds(pl.multiple_of((b * heads + head) * part, part), part), :
-                ]
-                sent_ref[b * part : (b + 1) * part, :] = acc[
-                    pl.ds(pl.multiple_of((b * heads + 1 - head) * part, part), part), :
-                ].astype(jnp.bfloat16)
-
-        t = pl.program_id(0)
-        pl.when(t < half)(lambda: run(own_ref))
-        pl.when(t >= half)(lambda: run(other_ref))
-
-    out_spec = pl.BlockSpec(
-        (rows // heads, tile), lambda t, s: (0, lax.rem(t + half * s[0], 2 * half))
-    )
+                mine = pl.ds(pl.multiple_of((b * heads + head) * part, part), part)
+                rest = pl.ds(pl.multiple_of((b * heads + 1 - head) * part, part), part)
+                keep_ref[b * part : (b + 1) * part, lanes] = acc[mine, :]
+                sent_ref[b * part : (b + 1) * part, lanes] = acc[rest, :].astype(jnp.bfloat16)
+
     shape = (rows // heads, 2 * cols)
     outs = [jax.ShapeDtypeStruct(shape, jnp.bfloat16)]
     if split:
         outs = [jax.ShapeDtypeStruct(shape, jnp.float32)] + outs
+    vmem = pl.BlockSpec(memory_space=pltpu.VMEM)
     return pl.pallas_call(
         body,
         out_shape=outs,
-        grid_spec=pltpu.PrefetchScalarGridSpec(
-            num_scalar_prefetch=1,
-            grid=(2 * half,),
-            in_specs=[pl.BlockSpec(p.shape, lambda t, s: (0, 0)) for p in pieces]
-            + [
-                pl.BlockSpec((depth, tile), lambda t, s: (0, jnp.minimum(t, half - 1))),
-                pl.BlockSpec((depth, tile), lambda t, s: (0, jnp.maximum(t - half, 0))),
-            ],
-            out_specs=[out_spec] * len(outs),
-            scratch_shapes=[pltpu.VMEM((rows, tile), jnp.float32)] if split else [],
-        ),
+        in_specs=[pl.BlockSpec(memory_space=pltpu.SMEM)] + [vmem] * (len(pieces) + 2),
+        out_specs=[vmem] * len(outs),
+        scratch_shapes=[pltpu.VMEM((rows, tile), jnp.float32)] if split else [],
         compiler_params=pltpu.CompilerParams(vmem_limit_bytes=VMEM_LIMIT),
         cost_estimate=pl.CostEstimate(
             flops=4 * rows * depth * cols, bytes_accessed=0, transcendentals=0
@@ -351,50 +336,30 @@
 
 
 def assemble_kernel(sites, heads, spans, spots_ref, *refs):
-    ins, (out_ref, left, right, sem) = refs[:-4], refs[-4:]
+    ins, out_ref = refs[:-1], refs[-1]
     length = sites // LINES
+    rows = out_ref.shape[0]
     cols = out_ref.shape[1] * heads // sites
-    rows = out_ref.shape[0]
     part = rows // heads
     place, head = spots_ref[2], spots_ref[1]
-
-    def each(go):
-        for d in range(sites):
-            at = lax.rem(place + d, sites)
-            line = at // length
-            z = jnp.where(line == 0, at, 2 * length - 1 - at)
-            site = z * LINES + line
-            size = rows if d in (0, sites // 2) else part
-            first, second = [ins[i].at[pl.ds(off, size)] for i, off in spans[d]]
-
-            @pl.when(site * heads // sites == head)
-            def _():
-                lane = pl.multiple_of((site - head * (sites // heads)) * cols, cols)
-                if size == rows:
-                    slot = 0 if d == 0 else 1
-                    if go is None:
-                        total = left[slot].astype(jnp.float32) + right[slot].astype(jnp.float32)
-                        out_ref[:, pl.ds(lane, cols)] = total.astype(jnp.bfloat16)
-                        return
-                    a = pltpu.make_async_copy(first, left.at[slot], sem)
-                    b = pltpu.make_async_copy(second, right.at[slot], sem)
-                elif go is None:
-                    return
-                else:
-                    mine = pl.multiple_of(head * part, part)
-                    other = pl.multiple_of((1 - head) * part, part)
-                    a = pltpu.make_async_copy(
-                        first, out_ref.at[pl.ds(mine, part), pl.ds(lane, cols)], sem
-                    )
-                    b = pltpu.make_async_copy(
-                        second, out_ref.at[pl.ds(other, part), pl.ds(lane, cols)], sem
-                    )
-                go(a)
-                go(b)
-
-    each(lambda c: c.start())
-    each(lambda c: c.wait())
-    each(None)
+    for d in range(sites):
+        at = lax.rem(place + d, sites)
+        line = at // length
+        z = jnp.where(line == 0, at, 2 * length - 1 - at)
+        site = z * LINES + line
+        (first, first_at), (second, second_at) = [(ins[i], off) for i, off in spans[d]]
+
+        @pl.when(site * heads // sites == head)
+        def _():
+            lanes = pl.ds(pl.multiple_of((site - head * (sites // heads)) * cols, cols), cols)
+            if d in (0, sites // 2):
+                total = first[...].astype(jnp.float32) + second[...].astype(jnp.float32)
+                out_ref[:, lanes] = total.astype(jnp.bfloat16)
+            else:
+                mine = pl.ds(pl.multiple_of(head * part, part), part)
+                other = pl.ds(pl.multiple_of((1 - head) * part, part), part)
+                out_ref[mine, lanes] = first[first_at : first_at + part, :]
+                out_ref[other, lanes] = second[second_at : second_at + part, :]
 
 
 def on_device(n, heads, queries, new_keys, new_values, pool_keys, pool_values, o_weight, page_list):
@@ -444,7 +409,7 @@
         for d, pieces in here.items():
             blocks.append((d, 0, pieces))
             blocks.append((d, 1, [core_swap(p, n) for p in pieces]))
-        return attend(cfg, live, me_ref, q, payload, blocks, state, step == sites // 2), []
+        return attend(cfg, live, me_ref, q, payload, blocks, state, step == sites // 2)
 
     (attended,) = ring_walk(payload, sites, look)
 
@@ -455,7 +420,7 @@
             for d, pieces in here.items():
                 (part,) = product(spots, pieces, o_weight, w_other, 0)
                 parts[d] = lax.ppermute(part, "ctx", site_perm(sites, -d)) if d else part
-            return part, []
+            return part
 
         ring_walk(attended, sites, multiply)
         order = jnp.stack(
@@ -479,8 +444,9 @@
         half = total.shape[0] // 2
         return total, ((d, total[:half]), (sites - d, total[half:]))
 
-    def cross():
+    def cross(after=()):
         for d, first, second in crossing:
+            first, second, _ = lax.optimization_barrier((first, second, after))
             got = swap_heads(jnp.concatenate([first, second], axis=0))
             half = first.shape[0]
             arrived[d], arrived[sites - d] = [(first, 0), (got, 0)], [(second, 0), (got, half)]
@@ -497,24 +463,24 @@
             within, across = back_perms(sites, heads, step)
             first = lax.ppermute(part, both, within) if step else part
             arrived[step] = [(first, 0), (lax.ppermute(part, both, across), 0)]
-            cross()
+            cross(part)
             if summing:
                 for at, piece in halves(d, keep, got)[1]:
                     arrived[at] = [
                         (lax.ppermute(piece, both, perm), 0)
                         for perm in back_perms(sites, heads, at)
                     ]
-            return [part], [arrived[step][1][0]]
+            return [part, arrived[0][1][0]] if step == 0 else [part]
         keep, sent = product(spots, here[step] + here[sites - step], o_weight, w_other, heads)
         got = swap_heads(sent)
-        crossed = cross()
+        cross()
         if step == last - 1:
             summing.extend((step, keep, got))
-            return [sent], crossed
+            return [sent]
         total, pieces = halves(step, keep, got)
         back = [lax.ppermute(p, "ctx", site_perm(sites, -at)) for at, p in pieces]
         crossing.append((step, *back))
-        return [total], back + crossed
+        return [total]
 
     ring_walk(attended, sites, multiply)
     operands, spans = [], []
@@ -524,13 +490,9 @@
     return pl.pallas_call(
         functools.partial(assemble_kernel, sites, heads, spans),
         out_shape=jax.ShapeDtypeStruct((rows, sites * CORES * cols // heads), jnp.bfloat16),
-        in_specs=[smem] + [hbm] * len(operands),
+        in_specs=[smem] + [vmem] * len(operands),
         out_specs=vmem,
-        scratch_shapes=[
-            pltpu.VMEM((2, rows, CORES * cols), jnp.bfloat16),
-            pltpu.VMEM((2, rows, CORES * cols), jnp.bfloat16),
-            pltpu.SemaphoreType.DMA,
-        ],
+        compiler_params=pltpu.CompilerParams(vmem_limit_bytes=SMALL_LIMIT),
         cost_estimate=FREE,
         name="assemble",
     )(spots, *operands)

time: 203 us -> 198 us (0.975)
  Pallas kernels: 72.4 us -> 61.7 us
  waiting for transfers between devices: 76.6 us -> 83.6 us
    pallas_call x5, Pallas kernels: 29.9 us -> 20.9 us  [product(): pl.pallas_call(body, out_shape=outs, in_specs=[pl.BlockSpec(memory_space=...]
    ppermute x16, waiting for transfers between devices: 37.8 us -> 42.9 us  [the longest x6 37.5 us: ring_walk(): f = lax.ppermute(f, 'ctx', site_perm(sites, 1))]
    ppermute x2, waiting for transfers between devices: 3.03 us -> 0.01 us  [multiply(): arrived[step] = [(first, 0), (lax.ppermute(part, both, across), 0)]]
    ppermute x4, waiting for transfers between devices: 18.9 us -> 21.9 us  [multiply(): back = [lax.ppermute(p, 'ctx', site_perm(sites, -at)) for at, p in pieces]]
    ppermute x5, waiting for transfers between devices: 3.29 us -> 6.11 us  [swap_heads(): return lax.ppermute(x, 'head', [(0, 1), (1, 0)])]
    unnamed x39 -> x9, local copies, waits for them, and re-layouts: 5.35 us -> 3.87 us
  transfers between devices with their start and end apart: 42 -> 42, of which waited for: 22 -> 21; matrix products, arithmetic and copies ran while one was open for 1% -> 1% of each run, Pallas kernels for 34% -> 30%
where the time goes in v4:
time: 198 us; the launch traced here: 197 us
  waiting for transfers between devices  83.6 us (42%)
  Pallas kernels  61.7 us (31%)
  starting transfers between devices  46.6 us (24%)
  local copies, waits for them, and re-layouts  4.04 us (2%)
    ppermute x6, waiting for transfers between devices, ring_walk(): f = lax.ppermute(f, 'ctx', site_perm(sites, 1))  37.5 us
    pallas_call x5, Pallas kernels, attend(): pl.pallas_call(body, out_shape=out_shape, in_specs=[smem, smem, vmem, hbm...  35.7 us
    ppermute x4, waiting for transfers between devices, multiply(): back = [lax.ppermute(p, 'ctx', site_perm(sites, -at)) for at, p in pieces]  21.9 us
    pallas_call x5, Pallas kernels, product(): pl.pallas_call(body, out_shape=outs, in_specs=[pl.BlockSpec(memory_space=...  20.9 us
    ppermute x4, waiting for transfers between devices, multiply(): lax.ppermute(piece, both, perm)  11.1 us
    ppermute x4, starting transfers between devices, multiply(): lax.ppermute(piece, both, perm)  9.57 us
    ppermute x2, starting transfers between devices, multiply(): arrived[step] = [(first, 0), (lax.ppermute(part, both, across), 0)]  7.31 us
    ppermute x6, starting transfers between devices, ring_walk(): f = lax.ppermute(f, 'ctx', site_perm(sites, 1))  7.28 us
  transfers between devices with their start and end apart: 42, of which 21 were waited for; matrix products, arithmetic and copies ran while one was open for 1% of the time, Pallas kernels for 30%

profile of v4, /device:TPU:6, one launch (start us, length us, event | category | flops | bytes accessed | tf_op | source)
XLA Modules:
  0.0 196.7 jit_solution(11017655041783373451)
XLA Ops:
  0.0 3.2 %pack_pages.1.own_ref.refs_0_ = bf16[512,512]{1,0:T(8,128)(2,1)} custom-call(s32[32]{0:T(128)} %pages_ref.1, s32[1]{0:T(128)} %bitcast.3.me_ref, bf16[128,4,128]{2,1,0:T(4,128)(2,1)} %nk_ref.1, bf16[128,4,128]{2,1,0:T(4,128)(2,1)} %nv_ref.1, bf16[8,32,4,128]{3,2,1,0:T(4,128)(2,1)} %pk_ref.1, bf16[8,32,4,128]{3,2,1,0:T(4,128)(2,1)} %pv_ref.1), custom_call_target="tpu_custom_call" | custom-call | tf_op jit(solution)/shard_map/pack_pages/pallas_call | solution.py:385
  4.5 1.8 collective-permute-start.1
  6.3 1.7 copy.10
  8.1 4.8 %attend.4 = (f32[4096,128]{1,0:T(8,128)S(1)}, f32[4096,128]{1,0:T(8,128)S(1)}) custom-call(s32[16]{0:T(128)S(1)} %convert_reduce_fusion.live_ref, s32[1]{0:T(128)} %bitcast.3.me_ref, bf16[128,4096]{1,0:T(8,128)(2,1)S(1)} %bitcast.8, bf16[512,512]{1,0:T(8,128)(2,1)S(1)} %copy-done.2, bf16[512,512]{1,0:T(8,128)(2,1)S(1)} %copy-done.2, ...), custom_call_target="tpu_custom_call" | custom-call | flops 1073741824 | tf_op jit(solution)/shard_map/attend/pallas_call | solution.py:255
  12.9 5.3 %collective-permute-done.refs_0_ = bf16[512,512]{1,0:T(8,128)(2,1)S(1)} collective-permute-done((bf16[512,512]{1,0:T(8,128)(2,1)}, bf16[512,512]{1,0:T(8,128)(2,1)S(1)}, u32[]{:S(2)}, u32[]{:S(2)}) %collective-permute-start) | collective-permute-done | bytes 524320 | tf_op jit(solution)/shard_map/ppermute | solution.py:53
  18.9 1.6 collective-permute-start.3
  21.0 8.3 %attend.5 = (f32[4096,128]{1,0:T(8,128)S(1)}, f32[4096,128]{1,0:T(8,128)S(1)}) custom-call(s32[16]{0:T(128)S(1)} %convert_reduce_fusion.live_ref, s32[1]{0:T(128)} %bitcast.3.me_ref, bf16[128,4096]{1,0:T(8,128)(2,1)S(1)} %bitcast.9, bf16[512,512]{1,0:T(8,128)(2,1)S(1)} %copy-done.2, bf16[512,512]{1,0:T(8,128)(2,1)S(1)} %collective-permute-done.refs_0_, ...), custom_call_target="tpu_custom_call" | custom-call | flops 2147483648 | tf_op jit(solution)/shard_map/attend/pallas_call | solution.py:255
  29.4 3.4 %collective-permute-done.3.refs_0_ = bf16[512,512]{1,0:T(8,128)(2,1)S(1)} collective-permute-done((bf16[512,512]{1,0:T(8,128)(2,1)S(1)}, bf16[512,512]{1,0:T(8,128)(2,1)S(1)}, u32[]{:S(2)}, u32[]{:S(2)}) %collective-permute-start.3) | collective-permute-done | bytes 524320 | tf_op jit(solution)/shard_map/ppermute | solution.py:53
  32.7 1.3 collective-permute-done.4.refs_2_
  34.5 1.7 collective-permute-start.7
  36.7 8.4 %attend.6 = (f32[4096,128]{1,0:T(8,128)S(1)}, f32[4096,128]{1,0:T(8,128)S(1)}) custom-call(s32[16]{0:T(128)S(1)} %convert_reduce_fusion.live_ref, s32[1]{0:T(128)} %bitcast.3.me_ref, bf16[128,4096]{1,0:T(8,128)(2,1)S(1)} %bitcast.10, bf16[512,512]{1,0:T(8,128)(2,1)S(1)} %copy-done.2, bf16[512,512]{1,0:T(8,128)(2,1)S(1)} %collective-permute-done.3.refs_0_, ...), custom_call_target="tpu_custom_call" | custom-call | flops 2147483648 | tf_op jit(solution)/shard_map/attend/pallas_call | solution.py:255
  45.0 3.3 %collective-permute-done.7.refs_0_ = bf16[512,512]{1,0:T(8,128)(2,1)S(1)} collective-permute-done((bf16[512,512]{1,0:T(8,128)(2,1)S(1)}, bf16[512,512]{1,0:T(8,128)(2,1)S(1)}, u32[]{:S(2)}, u32[]{:S(2)}) %collective-permute-start.7) | collective-permute-done | bytes 524320 | tf_op jit(solution)/shard_map/ppermute | solution.py:53
  48.4 1.4 collective-permute-done.8.refs_2_
  50.3 1.4 collective-permute-start.11
  52.4 8.7 %attend.7 = (f32[4096,128]{1,0:T(8,128)S(1)}, f32[4096,128]{1,0:T(8,128)S(1)}) custom-call(s32[16]{0:T(128)S(1)} %convert_reduce_fusion.live_ref, s32[1]{0:T(128)} %bitcast.3.me_ref, bf16[128,4096]{1,0:T(8,128)(2,1)S(1)} %bitcast.11, bf16[512,512]{1,0:T(8,128)(2,1)S(1)} %copy-done.2, bf16[512,512]{1,0:T(8,128)(2,1)S(1)} %collective-permute-done.7.refs_0_, ...), custom_call_target="tpu_custom_call" | custom-call | flops 2147483648 | tf_op jit(solution)/shard_map/attend/pallas_call | solution.py:255
  61.7 1.0 collective-permute-done.15.refs_2_
  63.1 5.5 %attend_last.1.refs_0_ = bf16[128,4096]{1,0:T(8,128)(2,1)S(1)} custom-call(s32[16]{0:T(128)S(1)} %convert_reduce_fusion.live_ref, s32[1]{0:T(128)} %bitcast.3.me_ref, bf16[128,4096]{1,0:T(8,128)(2,1)S(1)} %bitcast.12, bf16[512,512]{1,0:T(8,128)(2,1)S(1)} %copy-done.2, bf16[256,512]{1,0:T(8,128)(2,1)S(1)} %collective-permute-done.11.refs_0_, ...), custom_call_target="tpu_custom_call" | custom-call | flops 1073741824 | tf_op jit(solution)/shard_map/attend_last/pallas_call | solution.py:255
  68.7 1.4 collective-permute-start.19
  70.8 2.2 %copy-done = bf16[4096,512]{1,0:T(8,128)(2,1)S(1)} copy-done((bf16[4096,512]{1,0:T(8,128)(2,1)S(1)}, bf16[4096,512]{1,0:T(8,128)(2,1)}, u32[]{:S(2)}) %copy-start) | copy-done | bytes 4194328
  73.0 3.6 %product.5.refs_0_ = bf16[128,1024]{1,0:T(8,128)(2,1)S(1)} custom-call(s32[3]{0:T(128)S(1)} %pad_add_fusion.spots_ref, bf16[128,4096]{1,0:T(8,128)(2,1)S(1)} %attend_last.1.refs_0_, bf16[4096,512]{1,0:T(8,128)(2,1)S(1)} %copy-done, bf16[4096,512]{1,0:T(8,128)(2,1)} %collective-permute-done.17.refs_2_.refs_3_), custom_call_target="tpu_custom_call" | custom-call | flops 1073741824 | tf_op jit(solution)/shard_map/product/pallas_call | solution.py:311
  76.6 2.4 %collective-permute-start.18 = (bf16[128,1024]{1,0:T(8,128)(2,1)S(1)}, bf16[128,1024]{1,0:T(8,128)(2,1)S(1)}, u32[]{:S(2)}, u32[]{:S(2)}) collective-permute-start(bf16[128,1024]{1,0:T(8,128)(2,1)S(1)} %product.5.refs_0_), channel_id=1, source_target_pairs={{1,0},{3,2},{9,8},{11,10},{16,17},{18,19},{24,25},{26,27},{28,29},... | collective-permute-start | bytes 786440 | tf_op jit(solution)/shard_map/ppermute | solution.py:465
  79.1 14.8 %collective-permute-done.19.refs_0_ = bf16[128,4096]{1,0:T(8,128)(2,1)S(1)} collective-permute-done((bf16[128,4096]{1,0:T(8,128)(2,1)S(1)}, bf16[128,4096]{1,0:T(8,128)(2,1)S(1)}, u32[]{:S(2)}, u32[]{:S(2)}) %collective-permute-start.19) | collective-permute-done | bytes 1048608 | tf_op jit(solution)/shard_map/ppermute | solution.py:53
  93.9 1.1 collective-permute-done.20.refs_1_
  95.0 1.7 collective-permute-start.25
  97.1 4.6 %product.6 = (f32[128,1024]{1,0:T(8,128)S(1)}, bf16[128,1024]{1,0:T(8,128)(2,1)S(1)}) custom-call(s32[3]{0:T(128)S(1)} %pad_add_fusion.spots_ref, bf16[128,4096]{1,0:T(8,128)(2,1)S(1)} %collective-permute-done.19.refs_0_, bf16[128,4096]{1,0:T(8,128)(2,1)S(1)} %collective-permute-done.20.refs_1_, bf16[4096,512]{1,0:T(8,128)(2,1)S(1)} %copy-done.1, ...), custom_call_target="tpu_custom_call" | custom-call | flops 2147483648 | tf_op jit(solution)/shard_map/product/pallas_call | solution.py:311
  102.3 6.1 %collective-permute-done.21 = bf16[128,1024]{1,0:T(8,128)(2,1)S(1)} collective-permute-done((bf16[128,1024]{1,0:T(8,128)(2,1)S(1)}, bf16[128,1024]{1,0:T(8,128)(2,1)S(1)}, u32[]{:S(2)}, u32[]{:S(2)}) %collective-permute-start.21) | collective-permute-done | bytes 262176 | tf_op jit(solution)/shard_map/ppermute | solution.py:440
  108.4 10.6 %collective-permute-done.25.refs_0_ = bf16[128,4096]{1,0:T(8,128)(2,1)S(1)} collective-permute-done((bf16[128,4096]{1,0:T(8,128)(2,1)S(1)}, bf16[128,4096]{1,0:T(8,128)(2,1)S(1)}, u32[]{:S(2)}, u32[]{:S(2)}) %collective-permute-start.25) | collective-permute-done | bytes 1048608 | tf_op jit(solution)/shard_map/ppermute | solution.py:53
  119.1 1.4 collective-permute-done.26.refs_1_
  121.1 1.4 collective-permute-start.32
  122.5 4.6 %product.7 = (f32[128,1024]{1,0:T(8,128)S(1)}, bf16[128,1024]{1,0:T(8,128)(2,1)S(1)}) custom-call(s32[3]{0:T(128)S(1)} %pad_add_fusion.spots_ref, bf16[128,4096]{1,0:T(8,128)(2,1)S(1)} %collective-permute-done.25.refs_0_, bf16[128,4096]{1,0:T(8,128)(2,1)S(1)} %collective-permute-done.26.refs_1_, bf16[4096,512]{1,0:T(8,128)(2,1)S(1)} %copy-done.1, ...), custom_call_target="tpu_custom_call" | custom-call | flops 2147483648 | tf_op jit(solution)/shard_map/product/pallas_call | solution.py:311
  128.2 1.7 collective-permute-start.23
  129.9 16.8 %collective-permute-done.22.refs_2_ = bf16[64,1024]{1,0:T(8,128)(2,1)S(1)} collective-permute-done((bf16[64,1024]{1,0:T(8,128)(2,1)S(1)}, bf16[64,1024]{1,0:T(8,128)(2,1)S(1)}, u32[]{:S(2)}, u32[]{:S(2)}) %collective-permute-start.22) | collective-permute-done | bytes 131104 | tf_op jit(solution)/shard_map/ppermute | solution.py:481
  147.5 1.5 collective-permute-start.35
  150.1 2.0 collective-permute-start.29
  152.0 4.6 %product.8 = (f32[128,1024]{1,0:T(8,128)S(1)}, bf16[128,1024]{1,0:T(8,128)(2,1)S(1)}) custom-call(s32[3]{0:T(128)S(1)} %pad_add_fusion.spots_ref, bf16[128,4096]{1,0:T(8,128)(2,1)S(1)} %collective-permute-done.31.refs_0_, bf16[128,4096]{1,0:T(8,128)(2,1)S(1)} %collective-permute-done.32.refs_1_, bf16[4096,512]{1,0:T(8,128)(2,1)S(1)} %copy-done.1, ...), custom_call_target="tpu_custom_call" | custom-call | flops 2147483648 | tf_op jit(solution)/shard_map/product/pallas_call | solution.py:311
  157.3 5.0 %collective-permute-done.28.refs_4_ = bf16[64,1024]{1,0:T(8,128)(2,1)S(1)} collective-permute-done((bf16[64,1024]{1,0:T(8,128)(2,1)S(1)}, bf16[64,1024]{1,0:T(8,128)(2,1)S(1)}, u32[]{:S(2)}, u32[]{:S(2)}) %collective-permute-start.28) | collective-permute-done | bytes 131104 | tf_op jit(solution)/shard_map/ppermute | solution.py:481
  162.3 2.0 collective-permute-start.24
  164.4 3.5 %product.9 = bf16[128,1024]{1,0:T(8,128)(2,1)S(1)} custom-call(s32[3]{0:T(128)S(1)} %pad_add_fusion.spots_ref, bf16[64,4096]{1,0:T(8,128)(2,1)S(1)} %collective-permute-done.34.refs_0_, bf16[64,4096]{1,0:T(8,128)(2,1)S(1)} %collective-permute-done.35.refs_1_, bf16[4096,512]{1,0:T(8,128)(2,1)S(1)} %copy-done.1, ...), custom_call_target="tpu_custom_call" | custom-call | flops 1073741824 | tf_op jit(solution)/shard_map/product/pallas_call | solution.py:311
  168.0 1.3 collective-permute-start.36
  169.3 1.3 collective-permute-start.38
  170.6 4.9 %collective-permute-start.39 = (bf16[128,1024]{1,0:T(8,128)(2,1)S(1)}, bf16[128,1024]{1,0:T(8,128)(2,1)S(1)}, u32[]{:S(2)}, u32[]{:S(2)}) collective-permute-start(bf16[128,1024]{1,0:T(8,128)(2,1)S(1)} %product.9), channel_id=1, source_target_pairs={{1,28},{3,30},{9,20},{11,22},{16,13},{18,15},{24,5},{26,7},{28,1},... | collective-permute-start | bytes 786440 | tf_op jit(solution)/shard_map/ppermute | solution.py:465
  175.5 5.1 %collective-permute-start.37 = (bf16[64,1024]{1,0:T(8,128)(2,1)S(1)}, bf16[64,1024]{1,0:T(8,128)(2,1)S(1)}, u32[]{:S(2)}, u32[]{:S(2)}) collective-permute-start(bf16[64,1024]{1,0:T(8,128)(2,1)S(1)} %get-tuple-element.96), channel_id=1, source_target_pairs={{1,20},{3,22},{9,12},{11,14},{16,5},{18,7},{24,1},{26,3},{28,9},{3... | collective-permute-start | bytes 393224 | tf_op jit(solution)/shard_map/ppermute | solution.py:470
  180.6 1.3 collective-permute-start.40
  181.9 3.4 %collective-permute-done.36.refs_6_ = bf16[64,1024]{1,0:T(8,128)(2,1)S(1)} collective-permute-done((bf16[64,1024]{1,0:T(8,128)(2,1)S(1)}, bf16[64,1024]{1,0:T(8,128)(2,1)S(1)}, u32[]{:S(2)}, u32[]{:S(2)}) %collective-permute-start.36) | collective-permute-done | bytes 131104 | tf_op jit(solution)/shard_map/ppermute | solution.py:470
  185.4 1.9 collective-permute-start.41
  187.3 4.0 %collective-permute-done.37.refs_7_ = bf16[64,1024]{1,0:T(8,128)(2,1)S(1)} collective-permute-done((bf16[64,1024]{1,0:T(8,128)(2,1)S(1)}, bf16[64,1024]{1,0:T(8,128)(2,1)S(1)}, u32[]{:S(2)}, u32[]{:S(2)}) %collective-permute-start.37) | collective-permute-done | bytes 131104 | tf_op jit(solution)/shard_map/ppermute | solution.py:470
  191.2 3.7 %collective-permute-done.41.refs_11_ = bf16[64,1024]{1,0:T(8,128)(2,1)S(1)} collective-permute-done((bf16[64,1024]{1,0:T(8,128)(2,1)S(1)}, bf16[64,1024]{1,0:T(8,128)(2,1)S(1)}, u32[]{:S(2)}, u32[]{:S(2)}) %collective-permute-start.41) | collective-permute-done | bytes 131104 | tf_op jit(solution)/shard_map/ppermute | solution.py:470
  194.9 1.8 assemble.1
  (72 shorter events, 11.8 us)
Async XLA Ops:
  0.0 7.9 %copy-start.3 = (s32[32]{0:T(128)S(1)}, s32[32]{0:T(128)}, u32[]{:S(2)}) copy-start(s32[32]{0:T(128)} %pages_ref.1) | copy-start | bytes 388
  0.0 70.8 %collective-permute-start.17 = (bf16[4096,512]{1,0:T(8,128)(2,1)}, bf16[4096,512]{1,0:T(8,128)(2,1)}, u32[]{:S(2)}, u32[]{:S(2)}) collective-permute-start(bf16[4096,512]{1,0:T(8,128)(2,1)} %refs_2_.7), channel_id=1, source_target_pairs={{0,2},{2,0},{4,6},{6,4},{8,10},{10,8},{12,14},{14,12},{16,18},{18,... | collective-permute-start | bytes 12582920 | tf_op jit(solution)/shard_map/ppermute | solution.py:44
  3.3 4.9 %copy-start.2 = (bf16[512,512]{1,0:T(8,128)(2,1)S(1)}, bf16[512,512]{1,0:T(8,128)(2,1)}, u32[]{:S(2)}) copy-start(bf16[512,512]{1,0:T(8,128)(2,1)} %pack_pages.1.own_ref.refs_0_) | copy-start | bytes 1572868
  3.3 4.9 %collective-permute-start.2 = (bf16[512,512]{1,0:T(8,128)(2,1)}, bf16[512,512]{1,0:T(8,128)(2,1)S(1)}, u32[]{:S(2)}, u32[]{:S(2)}) collective-permute-start(bf16[512,512]{1,0:T(8,128)(2,1)} %pack_pages.1.own_ref.refs_0_), channel_id=1, source_target_pairs={{0,2},{2,0},{4,6},{6,4},{8,10},{10,8},{12,14},{14,12},{16,18},{18,... | collective-permute-start | bytes 1572872 | tf_op jit(solution)/shard_map/ppermute | solution.py:44
  4.2 14.0 %collective-permute-start = (bf16[512,512]{1,0:T(8,128)(2,1)}, bf16[512,512]{1,0:T(8,128)(2,1)S(1)}, u32[]{:S(2)}, u32[]{:S(2)}) collective-permute-start(bf16[512,512]{1,0:T(8,128)(2,1)} %pack_pages.1.own_ref.refs_0_), channel_id=1, source_target_pairs={{0,8},{2,10},{8,16},{10,18},{16,24},{18,26},{24,28},{26,30},{28,20... | collective-permute-start | bytes 1572872 | tf_op jit(solution)/shard_map/ppermute | solution.py:53
  4.5 13.9 %collective-permute-start.1 = (bf16[512,512]{1,0:T(8,128)(2,1)}, bf16[512,512]{1,0:T(8,128)(2,1)S(1)}, u32[]{:S(2)}, u32[]{:S(2)}) collective-permute-start(bf16[512,512]{1,0:T(8,128)(2,1)} %pack_pages.1.own_ref.refs_0_), channel_id=1, source_target_pairs={{0,4},{2,6},{8,0},{10,2},{16,8},{18,10},{24,16},{26,18},{28,24},{3... | collective-permute-start | bytes 1572872 | tf_op jit(solution)/shard_map/ppermute | solution.py:54
  18.4 2.5 %collective-permute-start.5 = (bf16[512,512]{1,0:T(8,128)(2,1)S(1)}, bf16[512,512]{1,0:T(8,128)(2,1)S(1)}, u32[]{:S(2)}, u32[]{:S(2)}) collective-permute-start(bf16[512,512]{1,0:T(8,128)(2,1)S(1)} %collective-permute-done.refs_0_), channel_id=1, source_target_pairs={{0,2},{2,0},{4,6},{6,4},{8,10},{10,8},{12,14},{14,12},{16,18},{18,... | collective-permute-start | bytes 1572872 | tf_op jit(solution)/shard_map/ppermute | solution.py:44
  18.4 2.7 %collective-permute-start.6 = (bf16[512,512]{1,0:T(8,128)(2,1)S(1)}, bf16[512,512]{1,0:T(8,128)(2,1)S(1)}, u32[]{:S(2)}, u32[]{:S(2)}) collective-permute-start(bf16[512,512]{1,0:T(8,128)(2,1)S(1)} %collective-permute-done.1.refs_2_), channel_id=1, source_target_pairs={{0,2},{2,0},{4,6},{6,4},{8,10},{10,8},{12,14},{14,12},{16,18},{18,... | collective-permute-start | bytes 1572872 | tf_op jit(solution)/shard_map/ppermute | solution.py:44
  18.9 13.8 %collective-permute-start.3 = (bf16[512,512]{1,0:T(8,128)(2,1)S(1)}, bf16[512,512]{1,0:T(8,128)(2,1)S(1)}, u32[]{:S(2)}, u32[]{:S(2)}) collective-permute-start(bf16[512,512]{1,0:T(8,128)(2,1)S(1)} %collective-permute-done.refs_0_), channel_id=1, source_target_pairs={{0,8},{2,10},{8,16},{10,18},{16,24},{18,26},{24,28},{26,30},{28,20... | collective-permute-start | bytes 1572872 | tf_op jit(solution)/shard_map/ppermute | solution.py:53
  20.5 13.6 %collective-permute-start.4 = (bf16[512,512]{1,0:T(8,128)(2,1)S(1)}, bf16[512,512]{1,0:T(8,128)(2,1)S(1)}, u32[]{:S(2)}, u32[]{:S(2)}) collective-permute-start(bf16[512,512]{1,0:T(8,128)(2,1)S(1)} %collective-permute-done.1.refs_2_), channel_id=1, source_target_pairs={{0,4},{2,6},{8,0},{10,2},{16,8},{18,10},{24,16},{26,18},{28,24},{3... | collective-permute-start | bytes 1572872 | tf_op jit(solution)/shard_map/ppermute | solution.py:54
  34.0 2.5 %collective-permute-start.10 = (bf16[512,512]{1,0:T(8,128)(2,1)S(1)}, bf16[512,512]{1,0:T(8,128)(2,1)S(1)}, u32[]{:S(2)}, u32[]{:S(2)}) collective-permute-start(bf16[512,512]{1,0:T(8,128)(2,1)S(1)} %collective-permute-done.4.refs_2_), channel_id=1, source_target_pairs={{0,2},{2,0},{4,6},{6,4},{8,10},{10,8},{12,14},{14,12},{16,18},{18,... | collective-permute-start | bytes 1572872 | tf_op jit(solution)/shard_map/ppermute | solution.py:44
  34.0 2.7 %collective-permute-start.9 = (bf16[512,512]{1,0:T(8,128)(2,1)S(1)}, bf16[512,512]{1,0:T(8,128)(2,1)S(1)}, u32[]{:S(2)}, u32[]{:S(2)}) collective-permute-start(bf16[512,512]{1,0:T(8,128)(2,1)S(1)} %collective-permute-done.3.refs_0_), channel_id=1, source_target_pairs={{0,2},{2,0},{4,6},{6,4},{8,10},{10,8},{12,14},{14,12},{16,18},{18,... | collective-permute-start | bytes 1572872 | tf_op jit(solution)/shard_map/ppermute | solution.py:44
  34.5 13.8 %collective-permute-start.7 = (bf16[512,512]{1,0:T(8,128)(2,1)S(1)}, bf16[512,512]{1,0:T(8,128)(2,1)S(1)}, u32[]{:S(2)}, u32[]{:S(2)}) collective-permute-start(bf16[512,512]{1,0:T(8,128)(2,1)S(1)} %collective-permute-done.3.refs_0_), channel_id=1, source_target_pairs={{0,8},{2,10},{8,16},{10,18},{16,24},{18,26},{24,28},{26,30},{28,20... | collective-permute-start | bytes 1572872 | tf_op jit(solution)/shard_map/ppermute | solution.py:53
  36.2 13.6 %collective-permute-start.8 = (bf16[512,512]{1,0:T(8,128)(2,1)S(1)}, bf16[512,512]{1,0:T(8,128)(2,1)S(1)}, u32[]{:S(2)}, u32[]{:S(2)}) collective-permute-start(bf16[512,512]{1,0:T(8,128)(2,1)S(1)} %collective-permute-done.4.refs_2_), channel_id=1, source_target_pairs={{0,4},{2,6},{8,0},{10,2},{16,8},{18,10},{24,16},{26,18},{28,24},{3... | collective-permute-start | bytes 1572872 | tf_op jit(solution)/shard_map/ppermute | solution.py:54
  49.8 2.6 %collective-permute-start.13 = (bf16[512,512]{1,0:T(8,128)(2,1)S(1)}, bf16[512,512]{1,0:T(8,128)(2,1)S(1)}, u32[]{:S(2)}, u32[]{:S(2)}) collective-permute-start(bf16[512,512]{1,0:T(8,128)(2,1)S(1)} %collective-permute-done.7.refs_0_), channel_id=1, source_target_pairs={{0,2},{2,0},{4,6},{6,4},{8,10},{10,8},{12,14},{14,12},{16,18},{18,... | collective-permute-start | bytes 1572872 | tf_op jit(solution)/shard_map/ppermute | solution.py:44
  49.8 2.7 %collective-permute-start.14 = (bf16[512,512]{1,0:T(8,128)(2,1)S(1)}, bf16[512,512]{1,0:T(8,128)(2,1)S(1)}, u32[]{:S(2)}, u32[]{:S(2)}) collective-permute-start(bf16[512,512]{1,0:T(8,128)(2,1)S(1)} %collective-permute-done.8.refs_2_), channel_id=1, source_target_pairs={{0,2},{2,0},{4,6},{6,4},{8,10},{10,8},{12,14},{14,12},{16,18},{18,... | collective-permute-start | bytes 1572872 | tf_op jit(solution)/shard_map/ppermute | solution.py:44
  50.3 10.8 %collective-permute-start.11 = (bf16[256,512]{1,0:T(8,128)(2,1)S(1)}, bf16[256,512]{1,0:T(8,128)(2,1)S(1)}, u32[]{:S(2)}, u32[]{:S(2)}) collective-permute-start(bf16[256,512]{1,0:T(8,128)(2,1)S(1)} %slice.30), channel_id=1, source_target_pairs={{0,8},{2,10},{8,16},{10,18},{16,24},{18,26},{24,28},{26,30},{28,20... | collective-permute-start | bytes 786440 | tf_op jit(solution)/shard_map/ppermute | solution.py:58
  51.8 9.4 %collective-permute-start.12 = (bf16[256,512]{1,0:T(8,128)(2,1)S(1)}, bf16[256,512]{1,0:T(8,128)(2,1)S(1)}, u32[]{:S(2)}, u32[]{:S(2)}) collective-permute-start(bf16[256,512]{1,0:T(8,128)(2,1)S(1)} %slice.31), channel_id=1, source_target_pairs={{0,4},{2,6},{8,0},{10,2},{16,8},{18,10},{24,16},{26,18},{28,24},{3... | collective-permute-start | bytes 786440 | tf_op jit(solution)/shard_map/ppermute | solution.py:59
  61.2 1.6 collective-permute-start.15
  61.4 1.8 collective-permute-start.16
  68.7 25.2 %collective-permute-start.19 = (bf16[128,4096]{1,0:T(8,128)(2,1)S(1)}, bf16[128,4096]{1,0:T(8,128)(2,1)S(1)}, u32[]{:S(2)}, u32[]{:S(2)}) collective-permute-start(bf16[128,4096]{1,0:T(8,128)(2,1)S(1)} %attend_last.1.refs_0_), channel_id=1, source_target_pairs={{0,8},{2,10},{8,16},{10,18},{16,24},{18,26},{24,28},{26,30},{28,20... | collective-permute-start | bytes 3145736 | tf_op jit(solution)/shard_map/ppermute | solution.py:53
  70.1 24.9 %collective-permute-start.20 = (bf16[128,4096]{1,0:T(8,128)(2,1)S(1)}, bf16[128,4096]{1,0:T(8,128)(2,1)S(1)}, u32[]{:S(2)}, u32[]{:S(2)}) collective-permute-start(bf16[128,4096]{1,0:T(8,128)(2,1)S(1)} %attend_last.1.refs_0_), channel_id=1, source_target_pairs={{0,4},{2,6},{8,0},{10,2},{16,8},{18,10},{24,16},{26,18},{28,24},{3... | collective-permute-start | bytes 3145736 | tf_op jit(solution)/shard_map/ppermute | solution.py:54
  70.8 2.2 %copy-start = (bf16[4096,512]{1,0:T(8,128)(2,1)S(1)}, bf16[4096,512]{1,0:T(8,128)(2,1)}, u32[]{:S(2)}) copy-start(bf16[4096,512]{1,0:T(8,128)(2,1)} %refs_2_.7) | copy-start | bytes 12582916
  73.0 24.0 %copy-start.1 = (bf16[4096,512]{1,0:T(8,128)(2,1)S(1)}, bf16[4096,512]{1,0:T(8,128)(2,1)}, u32[]{:S(2)}) copy-start(bf16[4096,512]{1,0:T(8,128)(2,1)} %refs_2_.7) | copy-start | bytes 12582916
  76.6 18.4 %collective-permute-start.18 = (bf16[128,1024]{1,0:T(8,128)(2,1)S(1)}, bf16[128,1024]{1,0:T(8,128)(2,1)S(1)}, u32[]{:S(2)}, u32[]{:S(2)}) collective-permute-start(bf16[128,1024]{1,0:T(8,128)(2,1)S(1)} %product.5.refs_0_), channel_id=1, source_target_pairs={{1,0},{3,2},{9,8},{11,10},{16,17},{18,19},{24,25},{26,27},{28,29},... | collective-permute-start | bytes 786440 | tf_op jit(solution)/shard_map/ppermute | solution.py:465
  95.0 24.1 %collective-permute-start.25 = (bf16[128,4096]{1,0:T(8,128)(2,1)S(1)}, bf16[128,4096]{1,0:T(8,128)(2,1)S(1)}, u32[]{:S(2)}, u32[]{:S(2)}) collective-permute-start(bf16[128,4096]{1,0:T(8,128)(2,1)S(1)} %collective-permute-done.19.refs_0_), channel_id=1, source_target_pairs={{0,8},{2,10},{8,16},{10,18},{16,24},{18,26},{24,28},{26,30},{28,20... | collective-permute-start | bytes 3145736 | tf_op jit(solution)/shard_map/ppermute | solution.py:53
  96.7 23.8 %collective-permute-start.26 = (bf16[128,4096]{1,0:T(8,128)(2,1)S(1)}, bf16[128,4096]{1,0:T(8,128)(2,1)S(1)}, u32[]{:S(2)}, u32[]{:S(2)}) collective-permute-start(bf16[128,4096]{1,0:T(8,128)(2,1)S(1)} %collective-permute-done.20.refs_1_), channel_id=1, source_target_pairs={{0,4},{2,6},{8,0},{10,2},{16,8},{18,10},{24,16},{26,18},{28,24},{3... | collective-permute-start | bytes 3145736 | tf_op jit(solution)/shard_map/ppermute | solution.py:54
  101.7 6.7 %collective-permute-start.21 = (bf16[128,1024]{1,0:T(8,128)(2,1)S(1)}, bf16[128,1024]{1,0:T(8,128)(2,1)S(1)}, u32[]{:S(2)}, u32[]{:S(2)}) collective-permute-start(bf16[128,1024]{1,0:T(8,128)(2,1)S(1)} %get-tuple-element.77), channel_id=1, source_target_pairs={{0,1},{1,0},{2,3},{3,2},{4,5},{5,4},{6,7},{7,6},{8,9},{9,8},{10,11... | collective-permute-start | bytes 786440 | tf_op jit(solution)/shard_map/ppermute | solution.py:440
  120.5 26.3 %collective-permute-start.31 = (bf16[128,4096]{1,0:T(8,128)(2,1)S(1)}, bf16[128,4096]{1,0:T(8,128)(2,1)S(1)}, u32[]{:S(2)}, u32[]{:S(2)}) collective-permute-start(bf16[128,4096]{1,0:T(8,128)(2,1)S(1)} %collective-permute-done.25.refs_0_), channel_id=1, source_target_pairs={{0,8},{2,10},{8,16},{10,18},{16,24},{18,26},{24,28},{26,30},{28,20... | collective-permute-start | bytes 3145736 | tf_op jit(solution)/shard_map/ppermute | solution.py:53
  121.1 25.7 %collective-permute-start.32 = (bf16[128,4096]{1,0:T(8,128)(2,1)S(1)}, bf16[128,4096]{1,0:T(8,128)(2,1)S(1)}, u32[]{:S(2)}, u32[]{:S(2)}) collective-permute-start(bf16[128,4096]{1,0:T(8,128)(2,1)S(1)} %collective-permute-done.26.refs_1_), channel_id=1, source_target_pairs={{0,4},{2,6},{8,0},{10,2},{16,8},{18,10},{24,16},{26,18},{28,24},{3... | collective-permute-start | bytes 3145736 | tf_op jit(solution)/shard_map/ppermute | solution.py:54
  127.2 19.5 %collective-permute-start.27 = (bf16[128,1024]{1,0:T(8,128)(2,1)S(1)}, bf16[128,1024]{1,0:T(8,128)(2,1)S(1)}, u32[]{:S(2)}, u32[]{:S(2)}) collective-permute-start(bf16[128,1024]{1,0:T(8,128)(2,1)S(1)} %get-tuple-element.83), channel_id=1, source_target_pairs={{0,1},{1,0},{2,3},{3,2},{4,5},{5,4},{6,7},{7,6},{8,9},{9,8},{10,11... | collective-permute-start | bytes 786440 | tf_op jit(solution)/shard_map/ppermute | solution.py:440
  127.8 18.9 %collective-permute-start.22 = (bf16[64,1024]{1,0:T(8,128)(2,1)S(1)}, bf16[64,1024]{1,0:T(8,128)(2,1)S(1)}, u32[]{:S(2)}, u32[]{:S(2)}) collective-permute-start(bf16[64,1024]{1,0:T(8,128)(2,1)S(1)} %get-tuple-element.100), channel_id=1, source_target_pairs={{0,4},{2,6},{8,0},{10,2},{16,8},{18,10},{24,16},{26,18},{28,24},{3... | collective-permute-start | bytes 393224 | tf_op jit(solution)/shard_map/ppermute | solution.py:481
  128.2 18.5 %collective-permute-start.23 = (bf16[64,1024]{1,0:T(8,128)(2,1)S(1)}, bf16[64,1024]{1,0:T(8,128)(2,1)S(1)}, u32[]{:S(2)}, u32[]{:S(2)}) collective-permute-start(bf16[64,1024]{1,0:T(8,128)(2,1)S(1)} %get-tuple-element.99), channel_id=1, source_target_pairs={{0,8},{2,10},{8,16},{10,18},{16,24},{18,26},{24,28},{26,30},{28,20... | collective-permute-start | bytes 393224 | tf_op jit(solution)/shard_map/ppermute | solution.py:481
  146.9 17.6 %collective-permute-start.34 = (bf16[64,4096]{1,0:T(8,128)(2,1)S(1)}, bf16[64,4096]{1,0:T(8,128)(2,1)S(1)}, u32[]{:S(2)}, u32[]{:S(2)}) collective-permute-start(bf16[64,4096]{1,0:T(8,128)(2,1)S(1)} %slice.36), channel_id=1, source_target_pairs={{0,8},{2,10},{8,16},{10,18},{16,24},{18,26},{24,28},{26,30},{28,20... | collective-permute-start | bytes 1572872 | tf_op jit(solution)/shard_map/ppermute | solution.py:58
  147.5 16.9 %collective-permute-start.35 = (bf16[64,4096]{1,0:T(8,128)(2,1)S(1)}, bf16[64,4096]{1,0:T(8,128)(2,1)S(1)}, u32[]{:S(2)}, u32[]{:S(2)}) collective-permute-start(bf16[64,4096]{1,0:T(8,128)(2,1)S(1)} %slice.37), channel_id=1, source_target_pairs={{0,4},{2,6},{8,0},{10,2},{16,8},{18,10},{24,16},{26,18},{28,24},{3... | collective-permute-start | bytes 1572872 | tf_op jit(solution)/shard_map/ppermute | solution.py:59
  149.1 13.3 %collective-permute-start.28 = (bf16[64,1024]{1,0:T(8,128)(2,1)S(1)}, bf16[64,1024]{1,0:T(8,128)(2,1)S(1)}, u32[]{:S(2)}, u32[]{:S(2)}) collective-permute-start(bf16[64,1024]{1,0:T(8,128)(2,1)S(1)} %get-tuple-element.98), channel_id=1, source_target_pairs={{0,12},{2,14},{8,4},{10,6},{16,0},{18,2},{24,8},{26,10},{28,16},{3... | collective-permute-start | bytes 393224 | tf_op jit(solution)/shard_map/ppermute | solution.py:481
  150.1 14.2 %collective-permute-start.29 = (bf16[64,1024]{1,0:T(8,128)(2,1)S(1)}, bf16[64,1024]{1,0:T(8,128)(2,1)S(1)}, u32[]{:S(2)}, u32[]{:S(2)}) collective-permute-start(bf16[64,1024]{1,0:T(8,128)(2,1)S(1)} %get-tuple-element.97), channel_id=1, source_target_pairs={{0,16},{2,18},{8,24},{10,26},{16,28},{18,30},{24,20},{26,22},{28,1... | collective-permute-start | bytes 393224 | tf_op jit(solution)/shard_map/ppermute | solution.py:481
  156.7 11.3 %collective-permute-start.33 = (bf16[128,1024]{1,0:T(8,128)(2,1)S(1)}, bf16[128,1024]{1,0:T(8,128)(2,1)S(1)}, u32[]{:S(2)}, u32[]{:S(2)}) collective-permute-start(bf16[128,1024]{1,0:T(8,128)(2,1)S(1)} %get-tuple-element.89), channel_id=1, source_target_pairs={{0,1},{1,0},{2,3},{3,2},{4,5},{5,4},{6,7},{7,6},{8,9},{9,8},{10,11... | collective-permute-start | bytes 786440 | tf_op jit(solution)/shard_map/ppermute | solution.py:440
  162.3 13.2 %collective-permute-start.24 = (bf16[128,1024]{1,0:T(8,128)(2,1)S(1)}, bf16[128,1024]{1,0:T(8,128)(2,1)S(1)}, u32[]{:S(2)}, u32[]{:S(2)}) collective-permute-start(bf16[128,1024]{1,0:T(8,128)(2,1)S(1)} %pad_maximum_fusion), channel_id=1, source_target_pairs={{0,1},{1,0},{2,3},{3,2},{4,5},{5,4},{6,7},{7,6},{8,9},{9,8},{10,11... | collective-permute-start | bytes 786440 | tf_op jit(solution)/shard_map/ppermute | solution.py:440
  164.3 16.3 %collective-permute-start.30 = (bf16[128,1024]{1,0:T(8,128)(2,1)S(1)}, bf16[128,1024]{1,0:T(8,128)(2,1)S(1)}, u32[]{:S(2)}, u32[]{:S(2)}) collective-permute-start(bf16[128,1024]{1,0:T(8,128)(2,1)S(1)} %pad_maximum_fusion.1), channel_id=1, source_target_pairs={{0,1},{1,0},{2,3},{3,2},{4,5},{5,4},{6,7},{7,6},{8,9},{9,8},{10,11... | collective-permute-start | bytes 786440 | tf_op jit(solution)/shard_map/ppermute | solution.py:440
  168.0 17.3 %collective-permute-start.36 = (bf16[64,1024]{1,0:T(8,128)(2,1)S(1)}, bf16[64,1024]{1,0:T(8,128)(2,1)S(1)}, u32[]{:S(2)}, u32[]{:S(2)}) collective-permute-start(bf16[64,1024]{1,0:T(8,128)(2,1)S(1)} %get-tuple-element.96), channel_id=1, source_target_pairs={{0,20},{2,22},{8,12},{10,14},{17,5},{19,7},{25,1},{27,3},{29,9},{3... | collective-permute-start | bytes 393224 | tf_op jit(solution)/shard_map/ppermute | solution.py:470
  169.3 25.6 %collective-permute-start.38 = (bf16[128,1024]{1,0:T(8,128)(2,1)S(1)}, bf16[128,1024]{1,0:T(8,128)(2,1)S(1)}, u32[]{:S(2)}, u32[]{:S(2)}) collective-permute-start(bf16[128,1024]{1,0:T(8,128)(2,1)S(1)} %product.9), channel_id=1, source_target_pairs={{0,28},{2,30},{8,20},{10,22},{17,13},{19,15},{25,5},{27,7},{29,1},... | collective-permute-start | bytes 786440 | tf_op jit(solution)/shard_map/ppermute | solution.py:464
  170.6 24.3 %collective-permute-start.39 = (bf16[128,1024]{1,0:T(8,128)(2,1)S(1)}, bf16[128,1024]{1,0:T(8,128)(2,1)S(1)}, u32[]{:S(2)}, u32[]{:S(2)}) collective-permute-start(bf16[128,1024]{1,0:T(8,128)(2,1)S(1)} %product.9), channel_id=1, source_target_pairs={{1,28},{3,30},{9,20},{11,22},{16,13},{18,15},{24,5},{26,7},{28,1},... | collective-permute-start | bytes 786440 | tf_op jit(solution)/shard_map/ppermute | solution.py:465
  175.5 15.7 %collective-permute-start.37 = (bf16[64,1024]{1,0:T(8,128)(2,1)S(1)}, bf16[64,1024]{1,0:T(8,128)(2,1)S(1)}, u32[]{:S(2)}, u32[]{:S(2)}) collective-permute-start(bf16[64,1024]{1,0:T(8,128)(2,1)S(1)} %get-tuple-element.96), channel_id=1, source_target_pairs={{1,20},{3,22},{9,12},{11,14},{16,5},{18,7},{24,1},{26,3},{28,9},{3... | collective-permute-start | bytes 393224 | tf_op jit(solution)/shard_map/ppermute | solution.py:470
  180.6 10.6 %collective-permute-start.40 = (bf16[64,1024]{1,0:T(8,128)(2,1)S(1)}, bf16[64,1024]{1,0:T(8,128)(2,1)S(1)}, u32[]{:S(2)}, u32[]{:S(2)}) collective-permute-start(bf16[64,1024]{1,0:T(8,128)(2,1)S(1)} %get-tuple-element.95), channel_id=1, source_target_pairs={{0,24},{2,26},{8,28},{10,30},{17,21},{19,23},{25,13},{27,15},{29,5... | collective-permute-start | bytes 393224 | tf_op jit(solution)/shard_map/ppermute | solution.py:470
  185.4 9.5 %collective-permute-start.41 = (bf16[64,1024]{1,0:T(8,128)(2,1)S(1)}, bf16[64,1024]{1,0:T(8,128)(2,1)S(1)}, u32[]{:S(2)}, u32[]{:S(2)}) collective-permute-start(bf16[64,1024]{1,0:T(8,128)(2,1)S(1)} %get-tuple-element.95), channel_id=1, source_target_pairs={{1,24},{3,26},{9,28},{11,30},{16,21},{18,23},{24,13},{26,15},{28,5... | collective-permute-start | bytes 393224 | tf_op jit(solution)/shard_map/ppermute | solution.py:470

commit v5 on v4

--- a/solution.py
+++ b/solution.py
@@ -362,6 +362,24 @@
                 out_ref[other, lanes] = second[second_at : second_at + part, :]
 
 
+def join_kernel(count, *refs):
+    refs[-1][...] = jnp.concatenate([r[...] for r in refs[:count]], axis=0)
+
+
+def join(pieces, after):
+    vmem = pl.BlockSpec(memory_space=pltpu.VMEM)
+    rows = sum(p.shape[0] for p in pieces)
+    return pl.pallas_call(
+        functools.partial(join_kernel, len(pieces)),
+        out_shape=jax.ShapeDtypeStruct((rows, pieces[0].shape[1]), pieces[0].dtype),
+        in_specs=[vmem] * len(pieces) + [pl.BlockSpec(memory_space=pl.ANY)],
+        out_specs=vmem,
+        compiler_params=pltpu.CompilerParams(vmem_limit_bytes=SMALL_LIMIT),
+        cost_estimate=FREE,
+        name="join",
+    )(*pieces, after)
+
+
 def on_device(n, heads, queries, new_keys, new_values, pool_keys, pool_values, o_weight, page_list):
     rows, qheads, width = queries.shape
     kvheads = new_keys.shape[1]
@@ -444,15 +462,12 @@
         half = total.shape[0] // 2
         return total, ((d, total[:half]), (sites - d, total[half:]))
 
-    def cross(after=()):
-        for d, first, second in crossing:
-            first, second, _ = lax.optimization_barrier((first, second, after))
-            got = swap_heads(jnp.concatenate([first, second], axis=0))
+    def cross(after):
+        got = swap_heads(join([p for _, *pair in crossing for p in pair], after))
+        for i, (d, first, second) in enumerate(crossing):
             half = first.shape[0]
-            arrived[d], arrived[sites - d] = [(first, 0), (got, 0)], [(second, 0), (got, half)]
-            crossing.clear()
-            return [got]
-        return []
+            arrived[d] = [(first, 0), (got, 2 * i * half)]
+            arrived[sites - d] = [(second, 0), (got, (2 * i + 1) * half)]
 
     def multiply(step, here, _):
         if step in (0, last):
@@ -463,7 +478,8 @@
             within, across = back_perms(sites, heads, step)
             first = lax.ppermute(part, both, within) if step else part
             arrived[step] = [(first, 0), (lax.ppermute(part, both, across), 0)]
-            cross(part)
+            if crossing:
+                cross(part)
             if summing:
                 for at, piece in halves(d, keep, got)[1]:
                     arrived[at] = [
@@ -473,7 +489,6 @@
             return [part, arrived[0][1][0]] if step == 0 else [part]
         keep, sent = product(spots, here[step] + here[sites - step], o_weight, w_other, heads)
         got = swap_heads(sent)
-        cross()
         if step == last - 1:
             summing.extend((step, keep, got))
             return [sent]

time: 198 us -> 195 us (0.985)
  starting transfers between devices: 46.6 us -> 40.5 us
  waiting for transfers between devices: 83.6 us -> 87.1 us
    ppermute x4, waiting for transfers between devices: 21.9 us -> 3.41 us  [multiply(): back = [lax.ppermute(p, 'ctx', site_perm(sites, -at)) for at, p in pieces]]
    ppermute x6, waiting for transfers between devices: 37.5 us -> 47.4 us  [ring_walk(): f = lax.ppermute(f, 'ctx', site_perm(sites, 1))]
    ppermute x5 -> x4, waiting for transfers between devices: 6.11 us -> 11.9 us  [swap_heads(): return lax.ppermute(x, 'head', [(0, 1), (1, 0)])]
    ppermute x2, waiting for transfers between devices: 0.01 us -> 5.56 us  [ring_walk(): f = lax.ppermute(f[:half], 'ctx', site_perm(sites, 1))]
    ppermute x5 -> x4, starting transfers between devices: 3.92 us -> 1.86 us  [swap_heads(): return lax.ppermute(x, 'head', [(0, 1), (1, 0)])]
    ppermute x4, starting transfers between devices: 9.57 us -> 7.58 us  [multiply(): lax.ppermute(piece, both, perm)]
  transfers between devices with their start and end apart: 42 -> 41, of which waited for: 21 -> 24; matrix products, arithmetic and copies ran while one was open for 1% -> 1% of each run, Pallas kernels for 30% -> 31%
where the time goes in v5:
time: 195 us; the launch traced here: 194 us
  waiting for transfers between devices  87.1 us (45%)
  Pallas kernels  62.1 us (32%)
  starting transfers between devices  40.5 us (21%)
  local copies, waits for them, and re-layouts  4.04 us (2%)
    ppermute x6, waiting for transfers between devices, ring_walk(): f = lax.ppermute(f, 'ctx', site_perm(sites, 1))  47.4 us
    pallas_call x5, Pallas kernels, attend(): pl.pallas_call(body, out_shape=out_shape, in_specs=[smem, smem, vmem, hbm...  35.7 us
    pallas_call x5, Pallas kernels, product(): pl.pallas_call(body, out_shape=outs, in_specs=[pl.BlockSpec(memory_space=...  20.9 us
    ppermute x4, waiting for transfers between devices, swap_heads(): return lax.ppermute(x, 'head', [(0, 1), (1, 0)])  11.9 us
    ppermute x4, waiting for transfers between devices, multiply(): lax.ppermute(piece, both, perm)  11.4 us
    ppermute x4, starting transfers between devices, multiply(): lax.ppermute(piece, both, perm)  7.58 us
    ppermute x6, starting transfers between devices, ring_walk(): f = lax.ppermute(f, 'ctx', site_perm(sites, 1))  7.22 us
    ppermute x2, starting transfers between devices, multiply(): arrived[step] = [(first, 0), (lax.ppermute(part, both, across), 0)]  6.09 us
  transfers between devices with their start and end apart: 41, of which 24 were waited for; matrix products, arithmetic and copies ran while one was open for 1% of the time, Pallas kernels for 31%

profile of v5, /device:TPU:6, one launch (start us, length us, event | category | flops | bytes accessed | tf_op | source)
XLA Modules:
  0.0 194.4 jit_solution(18394152663276175206)
XLA Ops:
  0.0 3.6 %pack_pages.1.own_ref.refs_0_ = bf16[512,512]{1,0:T(8,128)(2,1)} custom-call(s32[32]{0:T(128)} %pages_ref.1, s32[1]{0:T(128)} %bitcast.3.me_ref, bf16[128,4,128]{2,1,0:T(4,128)(2,1)} %nk_ref.1, bf16[128,4,128]{2,1,0:T(4,128)(2,1)} %nv_ref.1, bf16[8,32,4,128]{3,2,1,0:T(4,128)(2,1)} %pk_ref.1, bf16[8,32,4,128]{3,2,1,0:T(4,128)(2,1)} %pv_ref.1), custom_call_target="tpu_custom_call" | custom-call | tf_op jit(solution)/shard_map/pack_pages/pallas_call | solution.py:403
  4.3 1.5 collective-permute-start.1
  5.8 1.7 copy.10
  8.1 4.8 %attend.4 = (f32[4096,128]{1,0:T(8,128)S(1)}, f32[4096,128]{1,0:T(8,128)S(1)}) custom-call(s32[16]{0:T(128)S(1)} %convert_reduce_fusion.live_ref, s32[1]{0:T(128)} %bitcast.3.me_ref, bf16[128,4096]{1,0:T(8,128)(2,1)S(1)} %bitcast.8, bf16[512,512]{1,0:T(8,128)(2,1)S(1)} %copy-done.2, bf16[512,512]{1,0:T(8,128)(2,1)S(1)} %copy-done.2, ...), custom_call_target="tpu_custom_call" | custom-call | flops 1073741824 | tf_op jit(solution)/shard_map/attend/pallas_call | solution.py:255
  12.9 5.2 %collective-permute-done.refs_0_ = bf16[512,512]{1,0:T(8,128)(2,1)S(1)} collective-permute-done((bf16[512,512]{1,0:T(8,128)(2,1)}, bf16[512,512]{1,0:T(8,128)(2,1)S(1)}, u32[]{:S(2)}, u32[]{:S(2)}) %collective-permute-start) | collective-permute-done | bytes 524320 | tf_op jit(solution)/shard_map/ppermute | solution.py:53
  18.9 1.7 collective-permute-start.3
  21.0 8.3 %attend.5 = (f32[4096,128]{1,0:T(8,128)S(1)}, f32[4096,128]{1,0:T(8,128)S(1)}) custom-call(s32[16]{0:T(128)S(1)} %convert_reduce_fusion.live_ref, s32[1]{0:T(128)} %bitcast.3.me_ref, bf16[128,4096]{1,0:T(8,128)(2,1)S(1)} %bitcast.9, bf16[512,512]{1,0:T(8,128)(2,1)S(1)} %copy-done.2, bf16[512,512]{1,0:T(8,128)(2,1)S(1)} %collective-permute-done.refs_0_, ...), custom_call_target="tpu_custom_call" | custom-call | flops 2147483648 | tf_op jit(solution)/shard_map/attend/pallas_call | solution.py:255
  29.4 3.4 %collective-permute-done.3.refs_0_ = bf16[512,512]{1,0:T(8,128)(2,1)S(1)} collective-permute-done((bf16[512,512]{1,0:T(8,128)(2,1)S(1)}, bf16[512,512]{1,0:T(8,128)(2,1)S(1)}, u32[]{:S(2)}, u32[]{:S(2)}) %collective-permute-start.3) | collective-permute-done | bytes 524320 | tf_op jit(solution)/shard_map/ppermute | solution.py:53
  32.7 1.4 collective-permute-done.4.refs_2_
  34.7 1.6 collective-permute-start.7
  36.8 8.4 %attend.6 = (f32[4096,128]{1,0:T(8,128)S(1)}, f32[4096,128]{1,0:T(8,128)S(1)}) custom-call(s32[16]{0:T(128)S(1)} %convert_reduce_fusion.live_ref, s32[1]{0:T(128)} %bitcast.3.me_ref, bf16[128,4096]{1,0:T(8,128)(2,1)S(1)} %bitcast.10, bf16[512,512]{1,0:T(8,128)(2,1)S(1)} %copy-done.2, bf16[512,512]{1,0:T(8,128)(2,1)S(1)} %collective-permute-done.3.refs_0_, ...), custom_call_target="tpu_custom_call" | custom-call | flops 2147483648 | tf_op jit(solution)/shard_map/attend/pallas_call | solution.py:255
  45.2 3.3 %collective-permute-done.7.refs_0_ = bf16[512,512]{1,0:T(8,128)(2,1)S(1)} collective-permute-done((bf16[512,512]{1,0:T(8,128)(2,1)S(1)}, bf16[512,512]{1,0:T(8,128)(2,1)S(1)}, u32[]{:S(2)}, u32[]{:S(2)}) %collective-permute-start.7) | collective-permute-done | bytes 524320 | tf_op jit(solution)/shard_map/ppermute | solution.py:53
  48.5 1.3 collective-permute-done.8.refs_2_
  50.3 1.6 collective-permute-start.11
  52.4 8.7 %attend.7 = (f32[4096,128]{1,0:T(8,128)S(1)}, f32[4096,128]{1,0:T(8,128)S(1)}) custom-call(s32[16]{0:T(128)S(1)} %convert_reduce_fusion.live_ref, s32[1]{0:T(128)} %bitcast.3.me_ref, bf16[128,4096]{1,0:T(8,128)(2,1)S(1)} %bitcast.11, bf16[512,512]{1,0:T(8,128)(2,1)S(1)} %copy-done.2, bf16[512,512]{1,0:T(8,128)(2,1)S(1)} %collective-permute-done.7.refs_0_, ...), custom_call_target="tpu_custom_call" | custom-call | flops 2147483648 | tf_op jit(solution)/shard_map/attend/pallas_call | solution.py:255
  63.1 5.5 %attend_last.1.refs_0_ = bf16[128,4096]{1,0:T(8,128)(2,1)S(1)} custom-call(s32[16]{0:T(128)S(1)} %convert_reduce_fusion.live_ref, s32[1]{0:T(128)} %bitcast.3.me_ref, bf16[128,4096]{1,0:T(8,128)(2,1)S(1)} %bitcast.12, bf16[512,512]{1,0:T(8,128)(2,1)S(1)} %copy-done.2, bf16[256,512]{1,0:T(8,128)(2,1)S(1)} %collective-permute-done.11.refs_0_, ...), custom_call_target="tpu_custom_call" | custom-call | flops 1073741824 | tf_op jit(solution)/shard_map/attend_last/pallas_call | solution.py:255
  68.7 1.6 collective-permute-start.19
  70.8 2.2 %copy-done = bf16[4096,512]{1,0:T(8,128)(2,1)S(1)} copy-done((bf16[4096,512]{1,0:T(8,128)(2,1)S(1)}, bf16[4096,512]{1,0:T(8,128)(2,1)}, u32[]{:S(2)}) %copy-start) | copy-done | bytes 4194328
  73.0 3.6 %product.5.refs_0_ = bf16[128,1024]{1,0:T(8,128)(2,1)S(1)} custom-call(s32[3]{0:T(128)S(1)} %pad_add_fusion.spots_ref, bf16[128,4096]{1,0:T(8,128)(2,1)S(1)} %attend_last.1.refs_0_, bf16[4096,512]{1,0:T(8,128)(2,1)S(1)} %copy-done, bf16[4096,512]{1,0:T(8,128)(2,1)} %collective-permute-done.17.refs_2_.refs_3_), custom_call_target="tpu_custom_call" | custom-call | flops 1073741824 | tf_op jit(solution)/shard_map/product/pallas_call | solution.py:311
  76.6 2.5 %collective-permute-start.18 = (bf16[128,1024]{1,0:T(8,128)(2,1)S(1)}, bf16[128,1024]{1,0:T(8,128)(2,1)S(1)}, u32[]{:S(2)}, u32[]{:S(2)}) collective-permute-start(bf16[128,1024]{1,0:T(8,128)(2,1)S(1)} %product.5.refs_0_), channel_id=1, source_target_pairs={{1,0},{3,2},{9,8},{11,10},{16,17},{18,19},{24,25},{26,27},{28,29},... | collective-permute-start | bytes 786440 | tf_op jit(solution)/shard_map/ppermute | solution.py:480
  79.1 14.8 %collective-permute-done.19.refs_0_ = bf16[128,4096]{1,0:T(8,128)(2,1)S(1)} collective-permute-done((bf16[128,4096]{1,0:T(8,128)(2,1)S(1)}, bf16[128,4096]{1,0:T(8,128)(2,1)S(1)}, u32[]{:S(2)}, u32[]{:S(2)}) %collective-permute-start.19) | collective-permute-done | bytes 1048608 | tf_op jit(solution)/shard_map/ppermute | solution.py:53
  93.9 1.3 collective-permute-done.20.refs_1_
  97.3 4.6 %product.6 = (f32[128,1024]{1,0:T(8,128)S(1)}, bf16[128,1024]{1,0:T(8,128)(2,1)S(1)}) custom-call(s32[3]{0:T(128)S(1)} %pad_add_fusion.spots_ref, bf16[128,4096]{1,0:T(8,128)(2,1)S(1)} %collective-permute-done.19.refs_0_, bf16[128,4096]{1,0:T(8,128)(2,1)S(1)} %collective-permute-done.20.refs_1_, bf16[4096,512]{1,0:T(8,128)(2,1)S(1)} %copy-done.1, ...), custom_call_target="tpu_custom_call" | custom-call | flops 2147483648 | tf_op jit(solution)/shard_map/product/pallas_call | solution.py:311
  102.5 6.1 %collective-permute-done.21 = bf16[128,1024]{1,0:T(8,128)(2,1)S(1)} collective-permute-done((bf16[128,1024]{1,0:T(8,128)(2,1)S(1)}, bf16[128,1024]{1,0:T(8,128)(2,1)S(1)}, u32[]{:S(2)}, u32[]{:S(2)}) %collective-permute-start.21) | collective-permute-done | bytes 262176 | tf_op jit(solution)/shard_map/ppermute | solution.py:458
  108.6 10.6 %collective-permute-done.24.refs_0_ = bf16[128,4096]{1,0:T(8,128)(2,1)S(1)} collective-permute-done((bf16[128,4096]{1,0:T(8,128)(2,1)S(1)}, bf16[128,4096]{1,0:T(8,128)(2,1)S(1)}, u32[]{:S(2)}, u32[]{:S(2)}) %collective-permute-start.24) | collective-permute-done | bytes 1048608 | tf_op jit(solution)/shard_map/ppermute | solution.py:53
  120.8 1.4 collective-permute-start.30
  122.2 4.6 %product.7 = (f32[128,1024]{1,0:T(8,128)S(1)}, bf16[128,1024]{1,0:T(8,128)(2,1)S(1)}) custom-call(s32[3]{0:T(128)S(1)} %pad_add_fusion.spots_ref, bf16[128,4096]{1,0:T(8,128)(2,1)S(1)} %collective-permute-done.24.refs_0_, bf16[128,4096]{1,0:T(8,128)(2,1)S(1)} %collective-permute-done.25.refs_1_, bf16[4096,512]{1,0:T(8,128)(2,1)S(1)} %copy-done.1, ...), custom_call_target="tpu_custom_call" | custom-call | flops 2147483648 | tf_op jit(solution)/shard_map/product/pallas_call | solution.py:311
  127.5 5.8 %collective-permute-done.26 = bf16[128,1024]{1,0:T(8,128)(2,1)S(1)} collective-permute-done((bf16[128,1024]{1,0:T(8,128)(2,1)S(1)}, bf16[128,1024]{1,0:T(8,128)(2,1)S(1)}, u32[]{:S(2)}, u32[]{:S(2)}) %collective-permute-start.26) | collective-permute-done | bytes 262176 | tf_op jit(solution)/shard_map/ppermute | solution.py:458
  133.4 10.0 %collective-permute-done.29.refs_0_ = bf16[128,4096]{1,0:T(8,128)(2,1)S(1)} collective-permute-done((bf16[128,4096]{1,0:T(8,128)(2,1)S(1)}, bf16[128,4096]{1,0:T(8,128)(2,1)S(1)}, u32[]{:S(2)}, u32[]{:S(2)}) %collective-permute-start.29) | collective-permute-done | bytes 1048608 | tf_op jit(solution)/shard_map/ppermute | solution.py:53
  144.3 1.2 collective-permute-start.33
  145.6 1.7 collective-permute-start.22
  147.7 4.6 %product.8 = (f32[128,1024]{1,0:T(8,128)S(1)}, bf16[128,1024]{1,0:T(8,128)(2,1)S(1)}) custom-call(s32[3]{0:T(128)S(1)} %pad_add_fusion.spots_ref, bf16[128,4096]{1,0:T(8,128)(2,1)S(1)} %collective-permute-done.29.refs_0_, bf16[128,4096]{1,0:T(8,128)(2,1)S(1)} %collective-permute-done.30.refs_1_, bf16[4096,512]{1,0:T(8,128)(2,1)S(1)} %copy-done.1, ...), custom_call_target="tpu_custom_call" | custom-call | flops 2147483648 | tf_op jit(solution)/shard_map/product/pallas_call | solution.py:311
  152.9 5.6 %collective-permute-done.32.refs_0_ = bf16[64,4096]{1,0:T(8,128)(2,1)S(1)} collective-permute-done((bf16[64,4096]{1,0:T(8,128)(2,1)S(1)}, bf16[64,4096]{1,0:T(8,128)(2,1)S(1)}, u32[]{:S(2)}, u32[]{:S(2)}) %collective-permute-start.32) | collective-permute-done | bytes 524320 | tf_op jit(solution)/shard_map/ppermute | solution.py:58
  158.5 1.2 collective-permute-start.27
  159.7 1.7 collective-permute-start.28
  161.4 3.5 %product.9.refs_4_ = bf16[128,1024]{1,0:T(8,128)(2,1)S(1)} custom-call(s32[3]{0:T(128)S(1)} %pad_add_fusion.spots_ref, bf16[64,4096]{1,0:T(8,128)(2,1)S(1)} %collective-permute-done.32.refs_0_, bf16[64,4096]{1,0:T(8,128)(2,1)S(1)} %collective-permute-done.33.refs_1_, bf16[4096,512]{1,0:T(8,128)(2,1)S(1)} %copy-done.1, ...), custom_call_target="tpu_custom_call" | custom-call | flops 1073741824 | tf_op jit(solution)/shard_map/product/pallas_call | solution.py:311
  164.9 3.4 %collective-permute-done.28.refs_3_.refs_12_ = bf16[64,1024]{1,0:T(8,128)(2,1)S(1)} collective-permute-done((bf16[64,1024]{1,0:T(8,128)(2,1)S(1)}, bf16[64,1024]{1,0:T(8,128)(2,1)S(1)}, u32[]{:S(2)}, u32[]{:S(2)}) %collective-permute-start.28) | collective-permute-done | bytes 131104 | tf_op jit(solution)/shard_map/ppermute | solution.py:496
  168.6 1.3 collective-permute-start.35
  169.9 3.1 %collective-permute-start.36 = (bf16[64,1024]{1,0:T(8,128)(2,1)S(1)}, bf16[64,1024]{1,0:T(8,128)(2,1)S(1)}, u32[]{:S(2)}, u32[]{:S(2)}) collective-permute-start(bf16[64,1024]{1,0:T(8,128)(2,1)S(1)} %get-tuple-element.88), channel_id=1, source_target_pairs={{1,20},{3,22},{9,12},{11,14},{16,5},{18,7},{24,1},{26,3},{28,9},{3... | collective-permute-start | bytes 393224 | tf_op jit(solution)/shard_map/ppermute | solution.py:486
  173.0 1.3 collective-permute-start.37
  174.3 3.6 %collective-permute-start.38 = (bf16[128,1024]{1,0:T(8,128)(2,1)S(1)}, bf16[128,1024]{1,0:T(8,128)(2,1)S(1)}, u32[]{:S(2)}, u32[]{:S(2)}) collective-permute-start(bf16[128,1024]{1,0:T(8,128)(2,1)S(1)} %product.9.refs_4_), channel_id=1, source_target_pairs={{1,28},{3,30},{9,20},{11,22},{16,13},{18,15},{24,5},{26,7},{28,1},... | collective-permute-start | bytes 786440 | tf_op jit(solution)/shard_map/ppermute | solution.py:480
  177.9 2.1 %collective-permute-done.35.refs_6_ = bf16[64,1024]{1,0:T(8,128)(2,1)S(1)} collective-permute-done((bf16[64,1024]{1,0:T(8,128)(2,1)S(1)}, bf16[64,1024]{1,0:T(8,128)(2,1)S(1)}, u32[]{:S(2)}, u32[]{:S(2)}) %collective-permute-start.35) | collective-permute-done | bytes 131104 | tf_op jit(solution)/shard_map/ppermute | solution.py:486
  180.0 1.3 collective-permute-start.39
  181.3 1.7 collective-permute-done.36.refs_7_
  183.0 1.9 collective-permute-start.40
  184.9 3.8 %collective-permute-done.39.refs_10_ = bf16[64,1024]{1,0:T(8,128)(2,1)S(1)} collective-permute-done((bf16[64,1024]{1,0:T(8,128)(2,1)S(1)}, bf16[64,1024]{1,0:T(8,128)(2,1)S(1)}, u32[]{:S(2)}, u32[]{:S(2)}) %collective-permute-start.39) | collective-permute-done | bytes 131104 | tf_op jit(solution)/shard_map/ppermute | solution.py:486
  188.7 3.8 %collective-permute-done.40.refs_11_ = bf16[64,1024]{1,0:T(8,128)(2,1)S(1)} collective-permute-done((bf16[64,1024]{1,0:T(8,128)(2,1)S(1)}, bf16[64,1024]{1,0:T(8,128)(2,1)S(1)}, u32[]{:S(2)}, u32[]{:S(2)}) %collective-permute-start.40) | collective-permute-done | bytes 131104 | tf_op jit(solution)/shard_map/ppermute | solution.py:486
  192.6 1.8 assemble.1
  (69 shorter events, 14.1 us)
Async XLA Ops:
  0.0 7.5 %copy-start.3 = (s32[32]{0:T(128)S(1)}, s32[32]{0:T(128)}, u32[]{:S(2)}) copy-start(s32[32]{0:T(128)} %pages_ref.1) | copy-start | bytes 388
  0.0 70.8 %collective-permute-start.17 = (bf16[4096,512]{1,0:T(8,128)(2,1)}, bf16[4096,512]{1,0:T(8,128)(2,1)}, u32[]{:S(2)}, u32[]{:S(2)}) collective-permute-start(bf16[4096,512]{1,0:T(8,128)(2,1)} %refs_2_.7), channel_id=1, source_target_pairs={{0,2},{2,0},{4,6},{6,4},{8,10},{10,8},{12,14},{14,12},{16,18},{18,... | collective-permute-start | bytes 12582920 | tf_op jit(solution)/shard_map/ppermute | solution.py:44
  3.6 4.5 %copy-start.2 = (bf16[512,512]{1,0:T(8,128)(2,1)S(1)}, bf16[512,512]{1,0:T(8,128)(2,1)}, u32[]{:S(2)}) copy-start(bf16[512,512]{1,0:T(8,128)(2,1)} %pack_pages.1.own_ref.refs_0_) | copy-start | bytes 1572868
  3.6 4.5 %collective-permute-start.2 = (bf16[512,512]{1,0:T(8,128)(2,1)}, bf16[512,512]{1,0:T(8,128)(2,1)S(1)}, u32[]{:S(2)}, u32[]{:S(2)}) collective-permute-start(bf16[512,512]{1,0:T(8,128)(2,1)} %pack_pages.1.own_ref.refs_0_), channel_id=1, source_target_pairs={{0,2},{2,0},{4,6},{6,4},{8,10},{10,8},{12,14},{14,12},{16,18},{18,... | collective-permute-start | bytes 1572872 | tf_op jit(solution)/shard_map/ppermute | solution.py:44
  3.8 14.4 %collective-permute-start = (bf16[512,512]{1,0:T(8,128)(2,1)}, bf16[512,512]{1,0:T(8,128)(2,1)S(1)}, u32[]{:S(2)}, u32[]{:S(2)}) collective-permute-start(bf16[512,512]{1,0:T(8,128)(2,1)} %pack_pages.1.own_ref.refs_0_), channel_id=1, source_target_pairs={{0,8},{2,10},{8,16},{10,18},{16,24},{18,26},{24,28},{26,30},{28,20... | collective-permute-start | bytes 1572872 | tf_op jit(solution)/shard_map/ppermute | solution.py:53
  4.3 14.1 %collective-permute-start.1 = (bf16[512,512]{1,0:T(8,128)(2,1)}, bf16[512,512]{1,0:T(8,128)(2,1)S(1)}, u32[]{:S(2)}, u32[]{:S(2)}) collective-permute-start(bf16[512,512]{1,0:T(8,128)(2,1)} %pack_pages.1.own_ref.refs_0_), channel_id=1, source_target_pairs={{0,4},{2,6},{8,0},{10,2},{16,8},{18,10},{24,16},{26,18},{28,24},{3... | collective-permute-start | bytes 1572872 | tf_op jit(solution)/shard_map/ppermute | solution.py:54
  18.4 2.5 %collective-permute-start.5 = (bf16[512,512]{1,0:T(8,128)(2,1)S(1)}, bf16[512,512]{1,0:T(8,128)(2,1)S(1)}, u32[]{:S(2)}, u32[]{:S(2)}) collective-permute-start(bf16[512,512]{1,0:T(8,128)(2,1)S(1)} %collective-permute-done.refs_0_), channel_id=1, source_target_pairs={{0,2},{2,0},{4,6},{6,4},{8,10},{10,8},{12,14},{14,12},{16,18},{18,... | collective-permute-start | bytes 1572872 | tf_op jit(solution)/shard_map/ppermute | solution.py:44
  18.4 2.7 %collective-permute-start.6 = (bf16[512,512]{1,0:T(8,128)(2,1)S(1)}, bf16[512,512]{1,0:T(8,128)(2,1)S(1)}, u32[]{:S(2)}, u32[]{:S(2)}) collective-permute-start(bf16[512,512]{1,0:T(8,128)(2,1)S(1)} %collective-permute-done.1.refs_2_), channel_id=1, source_target_pairs={{0,2},{2,0},{4,6},{6,4},{8,10},{10,8},{12,14},{14,12},{16,18},{18,... | collective-permute-start | bytes 1572872 | tf_op jit(solution)/shard_map/ppermute | solution.py:44
  18.9 13.8 %collective-permute-start.3 = (bf16[512,512]{1,0:T(8,128)(2,1)S(1)}, bf16[512,512]{1,0:T(8,128)(2,1)S(1)}, u32[]{:S(2)}, u32[]{:S(2)}) collective-permute-start(bf16[512,512]{1,0:T(8,128)(2,1)S(1)} %collective-permute-done.refs_0_), channel_id=1, source_target_pairs={{0,8},{2,10},{8,16},{10,18},{16,24},{18,26},{24,28},{26,30},{28,20... | collective-permute-start | bytes 1572872 | tf_op jit(solution)/shard_map/ppermute | solution.py:53
  20.6 13.6 %collective-permute-start.4 = (bf16[512,512]{1,0:T(8,128)(2,1)S(1)}, bf16[512,512]{1,0:T(8,128)(2,1)S(1)}, u32[]{:S(2)}, u32[]{:S(2)}) collective-permute-start(bf16[512,512]{1,0:T(8,128)(2,1)S(1)} %collective-permute-done.1.refs_2_), channel_id=1, source_target_pairs={{0,4},{2,6},{8,0},{10,2},{16,8},{18,10},{24,16},{26,18},{28,24},{3... | collective-permute-start | bytes 1572872 | tf_op jit(solution)/shard_map/ppermute | solution.py:54
  34.1 2.5 %collective-permute-start.10 = (bf16[512,512]{1,0:T(8,128)(2,1)S(1)}, bf16[512,512]{1,0:T(8,128)(2,1)S(1)}, u32[]{:S(2)}, u32[]{:S(2)}) collective-permute-start(bf16[512,512]{1,0:T(8,128)(2,1)S(1)} %collective-permute-done.4.refs_2_), channel_id=1, source_target_pairs={{0,2},{2,0},{4,6},{6,4},{8,10},{10,8},{12,14},{14,12},{16,18},{18,... | collective-permute-start | bytes 1572872 | tf_op jit(solution)/shard_map/ppermute | solution.py:44
  34.1 2.7 %collective-permute-start.9 = (bf16[512,512]{1,0:T(8,128)(2,1)S(1)}, bf16[512,512]{1,0:T(8,128)(2,1)S(1)}, u32[]{:S(2)}, u32[]{:S(2)}) collective-permute-start(bf16[512,512]{1,0:T(8,128)(2,1)S(1)} %collective-permute-done.3.refs_0_), channel_id=1, source_target_pairs={{0,2},{2,0},{4,6},{6,4},{8,10},{10,8},{12,14},{14,12},{16,18},{18,... | collective-permute-start | bytes 1572872 | tf_op jit(solution)/shard_map/ppermute | solution.py:44
  34.7 13.8 %collective-permute-start.7 = (bf16[512,512]{1,0:T(8,128)(2,1)S(1)}, bf16[512,512]{1,0:T(8,128)(2,1)S(1)}, u32[]{:S(2)}, u32[]{:S(2)}) collective-permute-start(bf16[512,512]{1,0:T(8,128)(2,1)S(1)} %collective-permute-done.3.refs_0_), channel_id=1, source_target_pairs={{0,8},{2,10},{8,16},{10,18},{16,24},{18,26},{24,28},{26,30},{28,20... | collective-permute-start | bytes 1572872 | tf_op jit(solution)/shard_map/ppermute | solution.py:53
  36.2 13.6 %collective-permute-start.8 = (bf16[512,512]{1,0:T(8,128)(2,1)S(1)}, bf16[512,512]{1,0:T(8,128)(2,1)S(1)}, u32[]{:S(2)}, u32[]{:S(2)}) collective-permute-start(bf16[512,512]{1,0:T(8,128)(2,1)S(1)} %collective-permute-done.4.refs_2_), channel_id=1, source_target_pairs={{0,4},{2,6},{8,0},{10,2},{16,8},{18,10},{24,16},{26,18},{28,24},{3... | collective-permute-start | bytes 1572872 | tf_op jit(solution)/shard_map/ppermute | solution.py:54
  49.8 2.6 %collective-permute-start.13 = (bf16[512,512]{1,0:T(8,128)(2,1)S(1)}, bf16[512,512]{1,0:T(8,128)(2,1)S(1)}, u32[]{:S(2)}, u32[]{:S(2)}) collective-permute-start(bf16[512,512]{1,0:T(8,128)(2,1)S(1)} %collective-permute-done.7.refs_0_), channel_id=1, source_target_pairs={{0,2},{2,0},{4,6},{6,4},{8,10},{10,8},{12,14},{14,12},{16,18},{18,... | collective-permute-start | bytes 1572872 | tf_op jit(solution)/shard_map/ppermute | solution.py:44
  49.8 2.7 %collective-permute-start.14 = (bf16[512,512]{1,0:T(8,128)(2,1)S(1)}, bf16[512,512]{1,0:T(8,128)(2,1)S(1)}, u32[]{:S(2)}, u32[]{:S(2)}) collective-permute-start(bf16[512,512]{1,0:T(8,128)(2,1)S(1)} %collective-permute-done.8.refs_2_), channel_id=1, source_target_pairs={{0,2},{2,0},{4,6},{6,4},{8,10},{10,8},{12,14},{14,12},{16,18},{18,... | collective-permute-start | bytes 1572872 | tf_op jit(solution)/shard_map/ppermute | solution.py:44
  50.3 10.8 %collective-permute-start.11 = (bf16[256,512]{1,0:T(8,128)(2,1)S(1)}, bf16[256,512]{1,0:T(8,128)(2,1)S(1)}, u32[]{:S(2)}, u32[]{:S(2)}) collective-permute-start(bf16[256,512]{1,0:T(8,128)(2,1)S(1)} %slice.30), channel_id=1, source_target_pairs={{0,8},{2,10},{8,16},{10,18},{16,24},{18,26},{24,28},{26,30},{28,20... | collective-permute-start | bytes 786440 | tf_op jit(solution)/shard_map/ppermute | solution.py:58
  52.0 9.2 %collective-permute-start.12 = (bf16[256,512]{1,0:T(8,128)(2,1)S(1)}, bf16[256,512]{1,0:T(8,128)(2,1)S(1)}, u32[]{:S(2)}, u32[]{:S(2)}) collective-permute-start(bf16[256,512]{1,0:T(8,128)(2,1)S(1)} %slice.31), channel_id=1, source_target_pairs={{0,4},{2,6},{8,0},{10,2},{16,8},{18,10},{24,16},{26,18},{28,24},{3... | collective-permute-start | bytes 786440 | tf_op jit(solution)/shard_map/ppermute | solution.py:59
  61.2 1.6 collective-permute-start.15
  61.4 1.8 collective-permute-start.16
  68.7 25.3 %collective-permute-start.19 = (bf16[128,4096]{1,0:T(8,128)(2,1)S(1)}, bf16[128,4096]{1,0:T(8,128)(2,1)S(1)}, u32[]{:S(2)}, u32[]{:S(2)}) collective-permute-start(bf16[128,4096]{1,0:T(8,128)(2,1)S(1)} %attend_last.1.refs_0_), channel_id=1, source_target_pairs={{0,8},{2,10},{8,16},{10,18},{16,24},{18,26},{24,28},{26,30},{28,20... | collective-permute-start | bytes 3145736 | tf_op jit(solution)/shard_map/ppermute | solution.py:53
  70.3 24.9 %collective-permute-start.20 = (bf16[128,4096]{1,0:T(8,128)(2,1)S(1)}, bf16[128,4096]{1,0:T(8,128)(2,1)S(1)}, u32[]{:S(2)}, u32[]{:S(2)}) collective-permute-start(bf16[128,4096]{1,0:T(8,128)(2,1)S(1)} %attend_last.1.refs_0_), channel_id=1, source_target_pairs={{0,4},{2,6},{8,0},{10,2},{16,8},{18,10},{24,16},{26,18},{28,24},{3... | collective-permute-start | bytes 3145736 | tf_op jit(solution)/shard_map/ppermute | solution.py:54
  70.8 2.2 %copy-start = (bf16[4096,512]{1,0:T(8,128)(2,1)S(1)}, bf16[4096,512]{1,0:T(8,128)(2,1)}, u32[]{:S(2)}) copy-start(bf16[4096,512]{1,0:T(8,128)(2,1)} %refs_2_.7) | copy-start | bytes 12582916
  73.0 24.2 %copy-start.1 = (bf16[4096,512]{1,0:T(8,128)(2,1)S(1)}, bf16[4096,512]{1,0:T(8,128)(2,1)}, u32[]{:S(2)}) copy-start(bf16[4096,512]{1,0:T(8,128)(2,1)} %refs_2_.7) | copy-start | bytes 12582916
  76.6 18.6 %collective-permute-start.18 = (bf16[128,1024]{1,0:T(8,128)(2,1)S(1)}, bf16[128,1024]{1,0:T(8,128)(2,1)S(1)}, u32[]{:S(2)}, u32[]{:S(2)}) collective-permute-start(bf16[128,1024]{1,0:T(8,128)(2,1)S(1)} %product.5.refs_0_), channel_id=1, source_target_pairs={{1,0},{3,2},{9,8},{11,10},{16,17},{18,19},{24,25},{26,27},{28,29},... | collective-permute-start | bytes 786440 | tf_op jit(solution)/shard_map/ppermute | solution.py:480
  95.2 24.1 %collective-permute-start.24 = (bf16[128,4096]{1,0:T(8,128)(2,1)S(1)}, bf16[128,4096]{1,0:T(8,128)(2,1)S(1)}, u32[]{:S(2)}, u32[]{:S(2)}) collective-permute-start(bf16[128,4096]{1,0:T(8,128)(2,1)S(1)} %collective-permute-done.19.refs_0_), channel_id=1, source_target_pairs={{0,8},{2,10},{8,16},{10,18},{16,24},{18,26},{24,28},{26,30},{28,20... | collective-permute-start | bytes 3145736 | tf_op jit(solution)/shard_map/ppermute | solution.py:53
  96.4 23.8 %collective-permute-start.25 = (bf16[128,4096]{1,0:T(8,128)(2,1)S(1)}, bf16[128,4096]{1,0:T(8,128)(2,1)S(1)}, u32[]{:S(2)}, u32[]{:S(2)}) collective-permute-start(bf16[128,4096]{1,0:T(8,128)(2,1)S(1)} %collective-permute-done.20.refs_1_), channel_id=1, source_target_pairs={{0,4},{2,6},{8,0},{10,2},{16,8},{18,10},{24,16},{26,18},{28,24},{3... | collective-permute-start | bytes 3145736 | tf_op jit(solution)/shard_map/ppermute | solution.py:54
  101.9 6.7 %collective-permute-start.21 = (bf16[128,1024]{1,0:T(8,128)(2,1)S(1)}, bf16[128,1024]{1,0:T(8,128)(2,1)S(1)}, u32[]{:S(2)}, u32[]{:S(2)}) collective-permute-start(bf16[128,1024]{1,0:T(8,128)(2,1)S(1)} %get-tuple-element.73), channel_id=1, source_target_pairs={{0,1},{1,0},{2,3},{3,2},{4,5},{5,4},{6,7},{7,6},{8,9},{9,8},{10,11... | collective-permute-start | bytes 786440 | tf_op jit(solution)/shard_map/ppermute | solution.py:458
  120.2 23.2 %collective-permute-start.29 = (bf16[128,4096]{1,0:T(8,128)(2,1)S(1)}, bf16[128,4096]{1,0:T(8,128)(2,1)S(1)}, u32[]{:S(2)}, u32[]{:S(2)}) collective-permute-start(bf16[128,4096]{1,0:T(8,128)(2,1)S(1)} %collective-permute-done.24.refs_0_), channel_id=1, source_target_pairs={{0,8},{2,10},{8,16},{10,18},{16,24},{18,26},{24,28},{26,30},{28,20... | collective-permute-start | bytes 3145736 | tf_op jit(solution)/shard_map/ppermute | solution.py:53
  120.8 22.6 %collective-permute-start.30 = (bf16[128,4096]{1,0:T(8,128)(2,1)S(1)}, bf16[128,4096]{1,0:T(8,128)(2,1)S(1)}, u32[]{:S(2)}, u32[]{:S(2)}) collective-permute-start(bf16[128,4096]{1,0:T(8,128)(2,1)S(1)} %collective-permute-done.25.refs_1_), channel_id=1, source_target_pairs={{0,4},{2,6},{8,0},{10,2},{16,8},{18,10},{24,16},{26,18},{28,24},{3... | collective-permute-start | bytes 3145736 | tf_op jit(solution)/shard_map/ppermute | solution.py:54
  126.9 6.4 %collective-permute-start.26 = (bf16[128,1024]{1,0:T(8,128)(2,1)S(1)}, bf16[128,1024]{1,0:T(8,128)(2,1)S(1)}, u32[]{:S(2)}, u32[]{:S(2)}) collective-permute-start(bf16[128,1024]{1,0:T(8,128)(2,1)S(1)} %get-tuple-element.77), channel_id=1, source_target_pairs={{0,1},{1,0},{2,3},{3,2},{4,5},{5,4},{6,7},{7,6},{8,9},{9,8},{10,11... | collective-permute-start | bytes 786440 | tf_op jit(solution)/shard_map/ppermute | solution.py:458
  143.4 15.1 %collective-permute-start.32 = (bf16[64,4096]{1,0:T(8,128)(2,1)S(1)}, bf16[64,4096]{1,0:T(8,128)(2,1)S(1)}, u32[]{:S(2)}, u32[]{:S(2)}) collective-permute-start(bf16[64,4096]{1,0:T(8,128)(2,1)S(1)} %slice.36), channel_id=1, source_target_pairs={{0,8},{2,10},{8,16},{10,18},{16,24},{18,26},{24,28},{26,30},{28,20... | collective-permute-start | bytes 1572872 | tf_op jit(solution)/shard_map/ppermute | solution.py:58
  144.3 15.4 %collective-permute-start.33 = (bf16[64,4096]{1,0:T(8,128)(2,1)S(1)}, bf16[64,4096]{1,0:T(8,128)(2,1)S(1)}, u32[]{:S(2)}, u32[]{:S(2)}) collective-permute-start(bf16[64,4096]{1,0:T(8,128)(2,1)S(1)} %slice.37), channel_id=1, source_target_pairs={{0,4},{2,6},{8,0},{10,2},{16,8},{18,10},{24,16},{26,18},{28,24},{3... | collective-permute-start | bytes 1572872 | tf_op jit(solution)/shard_map/ppermute | solution.py:59
  145.6 19.3 %collective-permute-start.22 = (bf16[64,1024]{1,0:T(8,128)(2,1)S(1)}, bf16[64,1024]{1,0:T(8,128)(2,1)S(1)}, u32[]{:S(2)}, u32[]{:S(2)}) collective-permute-start(bf16[64,1024]{1,0:T(8,128)(2,1)S(1)} %get-tuple-element.92), channel_id=1, source_target_pairs={{0,4},{2,6},{8,0},{10,2},{16,8},{18,10},{24,16},{26,18},{28,24},{3... | collective-permute-start | bytes 393224 | tf_op jit(solution)/shard_map/ppermute | solution.py:496
  147.3 17.6 %collective-permute-start.23 = (bf16[64,1024]{1,0:T(8,128)(2,1)S(1)}, bf16[64,1024]{1,0:T(8,128)(2,1)S(1)}, u32[]{:S(2)}, u32[]{:S(2)}) collective-permute-start(bf16[64,1024]{1,0:T(8,128)(2,1)S(1)} %get-tuple-element.91), channel_id=1, source_target_pairs={{0,8},{2,10},{8,16},{10,18},{16,24},{18,26},{24,28},{26,30},{28,20... | collective-permute-start | bytes 393224 | tf_op jit(solution)/shard_map/ppermute | solution.py:496
  152.3 12.6 %collective-permute-start.31 = (bf16[128,1024]{1,0:T(8,128)(2,1)S(1)}, bf16[128,1024]{1,0:T(8,128)(2,1)S(1)}, u32[]{:S(2)}, u32[]{:S(2)}) collective-permute-start(bf16[128,1024]{1,0:T(8,128)(2,1)S(1)} %get-tuple-element.81), channel_id=1, source_target_pairs={{0,1},{1,0},{2,3},{3,2},{4,5},{5,4},{6,7},{7,6},{8,9},{9,8},{10,11... | collective-permute-start | bytes 786440 | tf_op jit(solution)/shard_map/ppermute | solution.py:458
  158.5 6.4 %collective-permute-start.27 = (bf16[64,1024]{1,0:T(8,128)(2,1)S(1)}, bf16[64,1024]{1,0:T(8,128)(2,1)S(1)}, u32[]{:S(2)}, u32[]{:S(2)}) collective-permute-start(bf16[64,1024]{1,0:T(8,128)(2,1)S(1)} %get-tuple-element.90), channel_id=1, source_target_pairs={{0,12},{2,14},{8,4},{10,6},{16,0},{18,2},{24,8},{26,10},{28,16},{3... | collective-permute-start | bytes 393224 | tf_op jit(solution)/shard_map/ppermute | solution.py:496
  159.7 8.6 %collective-permute-start.28 = (bf16[64,1024]{1,0:T(8,128)(2,1)S(1)}, bf16[64,1024]{1,0:T(8,128)(2,1)S(1)}, u32[]{:S(2)}, u32[]{:S(2)}) collective-permute-start(bf16[64,1024]{1,0:T(8,128)(2,1)S(1)} %get-tuple-element.89), channel_id=1, source_target_pairs={{0,16},{2,18},{8,24},{10,26},{16,28},{18,30},{24,20},{26,22},{28,1... | collective-permute-start | bytes 393224 | tf_op jit(solution)/shard_map/ppermute | solution.py:496
  168.4 24.2 %collective-permute-start.34 = (bf16[256,1024]{1,0:T(8,128)(2,1)S(1)}, bf16[256,1024]{1,0:T(8,128)(2,1)S(1)}, u32[]{:S(2)}, u32[]{:S(2)}) collective-permute-start(bf16[256,1024]{1,0:T(8,128)(2,1)S(1)} %join.1), channel_id=1, source_target_pairs={{0,1},{1,0},{2,3},{3,2},{4,5},{5,4},{6,7},{7,6},{8,9},{9,8},{10,11... | collective-permute-start | bytes 1572872 | tf_op jit(solution)/shard_map/ppermute | solution.py:458
  168.6 11.4 %collective-permute-start.35 = (bf16[64,1024]{1,0:T(8,128)(2,1)S(1)}, bf16[64,1024]{1,0:T(8,128)(2,1)S(1)}, u32[]{:S(2)}, u32[]{:S(2)}) collective-permute-start(bf16[64,1024]{1,0:T(8,128)(2,1)S(1)} %get-tuple-element.88), channel_id=1, source_target_pairs={{0,20},{2,22},{8,12},{10,14},{17,5},{19,7},{25,1},{27,3},{29,9},{3... | collective-permute-start | bytes 393224 | tf_op jit(solution)/shard_map/ppermute | solution.py:486
  169.9 13.1 %collective-permute-start.36 = (bf16[64,1024]{1,0:T(8,128)(2,1)S(1)}, bf16[64,1024]{1,0:T(8,128)(2,1)S(1)}, u32[]{:S(2)}, u32[]{:S(2)}) collective-permute-start(bf16[64,1024]{1,0:T(8,128)(2,1)S(1)} %get-tuple-element.88), channel_id=1, source_target_pairs={{1,20},{3,22},{9,12},{11,14},{16,5},{18,7},{24,1},{26,3},{28,9},{3... | collective-permute-start | bytes 393224 | tf_op jit(solution)/shard_map/ppermute | solution.py:486
  173.0 19.6 %collective-permute-start.37 = (bf16[128,1024]{1,0:T(8,128)(2,1)S(1)}, bf16[128,1024]{1,0:T(8,128)(2,1)S(1)}, u32[]{:S(2)}, u32[]{:S(2)}) collective-permute-start(bf16[128,1024]{1,0:T(8,128)(2,1)S(1)} %product.9.refs_4_), channel_id=1, source_target_pairs={{0,28},{2,30},{8,20},{10,22},{17,13},{19,15},{25,5},{27,7},{29,1},... | collective-permute-start | bytes 786440 | tf_op jit(solution)/shard_map/ppermute | solution.py:479
  174.3 18.3 %collective-permute-start.38 = (bf16[128,1024]{1,0:T(8,128)(2,1)S(1)}, bf16[128,1024]{1,0:T(8,128)(2,1)S(1)}, u32[]{:S(2)}, u32[]{:S(2)}) collective-permute-start(bf16[128,1024]{1,0:T(8,128)(2,1)S(1)} %product.9.refs_4_), channel_id=1, source_target_pairs={{1,28},{3,30},{9,20},{11,22},{16,13},{18,15},{24,5},{26,7},{28,1},... | collective-permute-start | bytes 786440 | tf_op jit(solution)/shard_map/ppermute | solution.py:480
  180.0 8.8 %collective-permute-start.39 = (bf16[64,1024]{1,0:T(8,128)(2,1)S(1)}, bf16[64,1024]{1,0:T(8,128)(2,1)S(1)}, u32[]{:S(2)}, u32[]{:S(2)}) collective-permute-start(bf16[64,1024]{1,0:T(8,128)(2,1)S(1)} %get-tuple-element.87), channel_id=1, source_target_pairs={{0,24},{2,26},{8,28},{10,30},{17,21},{19,23},{25,13},{27,15},{29,5... | collective-permute-start | bytes 393224 | tf_op jit(solution)/shard_map/ppermute | solution.py:486
  183.0 9.5 %collective-permute-start.40 = (bf16[64,1024]{1,0:T(8,128)(2,1)S(1)}, bf16[64,1024]{1,0:T(8,128)(2,1)S(1)}, u32[]{:S(2)}, u32[]{:S(2)}) collective-permute-start(bf16[64,1024]{1,0:T(8,128)(2,1)S(1)} %get-tuple-element.87), channel_id=1, source_target_pairs={{1,24},{3,26},{9,28},{11,30},{16,21},{18,23},{24,13},{26,15},{28,5... | collective-permute-start | bytes 393224 | tf_op jit(solution)/shard_map/ppermute | solution.py:486

commit v6 on v5

--- a/solution.py
+++ b/solution.py
@@ -78,12 +78,11 @@
     me = me_ref[0]
 
     def one(p, count):
-        slot = pages_ref[p]
-        mine = slot // slots == me
+        local = pages_ref[p] - me * slots
+        mine = jnp.logical_and(local >= 0, local < slots)
 
         @pl.when(jnp.logical_and(mine, count < kept))
         def _():
-            local = slot % slots
             at = pl.multiple_of(rows + count * page, page)
             for h in range(heads):
                 lanes = slice(h * width, (h + 1) * width)

time: 195 us -> 195 us (level)
  starting transfers between devices: 40.5 us -> 44.2 us
  waiting for transfers between devices: 87.1 us -> 84.7 us
    ppermute x4, waiting for transfers between devices: 3.41 us -> 0.94 us  [multiply(): back = [lax.ppermute(p, 'ctx', site_perm(sites, -at)) for at, p in pieces]]
  transfers between devices with their start and end apart: 41 -> 41, of which waited for: 24 -> 25; matrix products, arithmetic and copies ran while one was open for 1% -> 1% of each run, Pallas kernels for 31% -> 31%
where the time goes in v6:
time: 195 us
  waiting for transfers between devices  84.7 us (43%)
  Pallas kernels  61.6 us (32%)
  starting transfers between devices  44.2 us (23%)
  local copies, waits for them, and re-layouts  4.04 us (2%)
    ppermute x6, waiting for transfers between devices, ring_walk(): f = lax.ppermute(f, 'ctx', site_perm(sites, 1))  46.8 us
    pallas_call x5, Pallas kernels, attend(): pl.pallas_call(body, out_shape=out_shape, in_specs=[smem, smem, vmem, hbm...  35.7 us
    pallas_call x5, Pallas kernels, product(): pl.pallas_call(body, out_shape=outs, in_specs=[pl.BlockSpec(memory_space=...  20.9 us
    ppermute x4, waiting for transfers between devices, swap_heads(): return lax.ppermute(x, 'head', [(0, 1), (1, 0)])  11.9 us
    ppermute x4, waiting for transfers between devices, multiply(): lax.ppermute(piece, both, perm)  11.4 us
    ppermute x4, starting transfers between devices, multiply(): lax.ppermute(piece, both, perm)  8.71 us
    ppermute x6, starting transfers between devices, ring_walk(): f = lax.ppermute(f, 'ctx', site_perm(sites, 1))  7.66 us
    ppermute x2, starting transfers between devices, multiply(): arrived[step] = [(first, 0), (lax.ppermute(part, both, across), 0)]  7.45 us
  transfers between devices with their start and end apart: 41, of which 25 were waited for; matrix products, arithmetic and copies ran while one was open for 1% of the time, Pallas kernels for 31%

profile of v6, /device:TPU:6, one launch (start us, length us, event | category | flops | bytes accessed | tf_op | source)
XLA Modules:
  0.0 195.2 jit_solution(4632741461576849766)
XLA Ops:
  0.0 3.1 %pack_pages.1.own_ref.refs_0_ = bf16[512,512]{1,0:T(8,128)(2,1)} custom-call(s32[32]{0:T(128)} %pages_ref.1, s32[1]{0:T(128)} %bitcast.3.me_ref, bf16[128,4,128]{2,1,0:T(4,128)(2,1)} %nk_ref.1, bf16[128,4,128]{2,1,0:T(4,128)(2,1)} %nv_ref.1, bf16[8,32,4,128]{3,2,1,0:T(4,128)(2,1)} %pk_ref.1, bf16[8,32,4,128]{3,2,1,0:T(4,128)(2,1)} %pv_ref.1), custom_call_target="tpu_custom_call" | custom-call | tf_op jit(solution)/shard_map/pack_pages/pallas_call | solution.py:402
  4.5 1.4 collective-permute-start.1
  5.9 1.7 copy.10
  8.1 4.8 %attend.4 = (f32[4096,128]{1,0:T(8,128)S(1)}, f32[4096,128]{1,0:T(8,128)S(1)}) custom-call(s32[16]{0:T(128)S(1)} %convert_reduce_fusion.live_ref, s32[1]{0:T(128)} %bitcast.3.me_ref, bf16[128,4096]{1,0:T(8,128)(2,1)S(1)} %bitcast.8, bf16[512,512]{1,0:T(8,128)(2,1)S(1)} %copy-done.2, bf16[512,512]{1,0:T(8,128)(2,1)S(1)} %copy-done.2, ...), custom_call_target="tpu_custom_call" | custom-call | flops 1073741824 | tf_op jit(solution)/shard_map/attend/pallas_call | solution.py:254
  12.9 5.0 %collective-permute-done.refs_0_ = bf16[512,512]{1,0:T(8,128)(2,1)S(1)} collective-permute-done((bf16[512,512]{1,0:T(8,128)(2,1)}, bf16[512,512]{1,0:T(8,128)(2,1)S(1)}, u32[]{:S(2)}, u32[]{:S(2)}) %collective-permute-start) | collective-permute-done | bytes 524320 | tf_op jit(solution)/shard_map/ppermute | solution.py:53
  18.8 1.7 collective-permute-start.3
  20.9 8.3 %attend.5 = (f32[4096,128]{1,0:T(8,128)S(1)}, f32[4096,128]{1,0:T(8,128)S(1)}) custom-call(s32[16]{0:T(128)S(1)} %convert_reduce_fusion.live_ref, s32[1]{0:T(128)} %bitcast.3.me_ref, bf16[128,4096]{1,0:T(8,128)(2,1)S(1)} %bitcast.9, bf16[512,512]{1,0:T(8,128)(2,1)S(1)} %copy-done.2, bf16[512,512]{1,0:T(8,128)(2,1)S(1)} %collective-permute-done.refs_0_, ...), custom_call_target="tpu_custom_call" | custom-call | flops 2147483648 | tf_op jit(solution)/shard_map/attend/pallas_call | solution.py:254
  29.2 3.4 %collective-permute-done.3.refs_0_ = bf16[512,512]{1,0:T(8,128)(2,1)S(1)} collective-permute-done((bf16[512,512]{1,0:T(8,128)(2,1)S(1)}, bf16[512,512]{1,0:T(8,128)(2,1)S(1)}, u32[]{:S(2)}, u32[]{:S(2)}) %collective-permute-start.3) | collective-permute-done | bytes 524320 | tf_op jit(solution)/shard_map/ppermute | solution.py:53
  32.6 1.4 collective-permute-done.4.refs_2_
  34.5 1.6 collective-permute-start.7
  36.7 8.4 %attend.6 = (f32[4096,128]{1,0:T(8,128)S(1)}, f32[4096,128]{1,0:T(8,128)S(1)}) custom-call(s32[16]{0:T(128)S(1)} %convert_reduce_fusion.live_ref, s32[1]{0:T(128)} %bitcast.3.me_ref, bf16[128,4096]{1,0:T(8,128)(2,1)S(1)} %bitcast.10, bf16[512,512]{1,0:T(8,128)(2,1)S(1)} %copy-done.2, bf16[512,512]{1,0:T(8,128)(2,1)S(1)} %collective-permute-done.3.refs_0_, ...), custom_call_target="tpu_custom_call" | custom-call | flops 2147483648 | tf_op jit(solution)/shard_map/attend/pallas_call | solution.py:254
  45.0 3.3 %collective-permute-done.7.refs_0_ = bf16[512,512]{1,0:T(8,128)(2,1)S(1)} collective-permute-done((bf16[512,512]{1,0:T(8,128)(2,1)S(1)}, bf16[512,512]{1,0:T(8,128)(2,1)S(1)}, u32[]{:S(2)}, u32[]{:S(2)}) %collective-permute-start.7) | collective-permute-done | bytes 524320 | tf_op jit(solution)/shard_map/ppermute | solution.py:53
  48.3 1.3 collective-permute-done.8.refs_2_
  50.2 1.6 collective-permute-start.11
  52.3 8.7 %attend.7 = (f32[4096,128]{1,0:T(8,128)S(1)}, f32[4096,128]{1,0:T(8,128)S(1)}) custom-call(s32[16]{0:T(128)S(1)} %convert_reduce_fusion.live_ref, s32[1]{0:T(128)} %bitcast.3.me_ref, bf16[128,4096]{1,0:T(8,128)(2,1)S(1)} %bitcast.11, bf16[512,512]{1,0:T(8,128)(2,1)S(1)} %copy-done.2, bf16[512,512]{1,0:T(8,128)(2,1)S(1)} %collective-permute-done.7.refs_0_, ...), custom_call_target="tpu_custom_call" | custom-call | flops 2147483648 | tf_op jit(solution)/shard_map/attend/pallas_call | solution.py:254
  63.0 5.5 %attend_last.1.refs_0_ = bf16[128,4096]{1,0:T(8,128)(2,1)S(1)} custom-call(s32[16]{0:T(128)S(1)} %convert_reduce_fusion.live_ref, s32[1]{0:T(128)} %bitcast.3.me_ref, bf16[128,4096]{1,0:T(8,128)(2,1)S(1)} %bitcast.12, bf16[512,512]{1,0:T(8,128)(2,1)S(1)} %copy-done.2, bf16[256,512]{1,0:T(8,128)(2,1)S(1)} %collective-permute-done.11.refs_0_, ...), custom_call_target="tpu_custom_call" | custom-call | flops 1073741824 | tf_op jit(solution)/shard_map/attend_last/pallas_call | solution.py:254
  68.5 1.6 collective-permute-start.19
  70.7 2.2 %copy-done = bf16[4096,512]{1,0:T(8,128)(2,1)S(1)} copy-done((bf16[4096,512]{1,0:T(8,128)(2,1)S(1)}, bf16[4096,512]{1,0:T(8,128)(2,1)}, u32[]{:S(2)}) %copy-start) | copy-done | bytes 4194328
  72.9 3.6 %product.5.refs_0_ = bf16[128,1024]{1,0:T(8,128)(2,1)S(1)} custom-call(s32[3]{0:T(128)S(1)} %pad_add_fusion.spots_ref, bf16[128,4096]{1,0:T(8,128)(2,1)S(1)} %attend_last.1.refs_0_, bf16[4096,512]{1,0:T(8,128)(2,1)S(1)} %copy-done, bf16[4096,512]{1,0:T(8,128)(2,1)} %collective-permute-done.17.refs_2_.refs_3_), custom_call_target="tpu_custom_call" | custom-call | flops 1073741824 | tf_op jit(solution)/shard_map/product/pallas_call | solution.py:310
  76.5 2.5 %collective-permute-start.18 = (bf16[128,1024]{1,0:T(8,128)(2,1)S(1)}, bf16[128,1024]{1,0:T(8,128)(2,1)S(1)}, u32[]{:S(2)}, u32[]{:S(2)}) collective-permute-start(bf16[128,1024]{1,0:T(8,128)(2,1)S(1)} %product.5.refs_0_), channel_id=1, source_target_pairs={{1,0},{3,2},{9,8},{11,10},{16,17},{18,19},{24,25},{26,27},{28,29},... | collective-permute-start | bytes 786440 | tf_op jit(solution)/shard_map/ppermute | solution.py:479
  78.9 14.8 %collective-permute-done.19.refs_0_ = bf16[128,4096]{1,0:T(8,128)(2,1)S(1)} collective-permute-done((bf16[128,4096]{1,0:T(8,128)(2,1)S(1)}, bf16[128,4096]{1,0:T(8,128)(2,1)S(1)}, u32[]{:S(2)}, u32[]{:S(2)}) %collective-permute-start.19) | collective-permute-done | bytes 1048608 | tf_op jit(solution)/shard_map/ppermute | solution.py:53
  93.8 1.3 collective-permute-done.20.refs_1_
  95.1 1.5 collective-permute-start.24
  97.1 4.6 %product.6 = (f32[128,1024]{1,0:T(8,128)S(1)}, bf16[128,1024]{1,0:T(8,128)(2,1)S(1)}) custom-call(s32[3]{0:T(128)S(1)} %pad_add_fusion.spots_ref, bf16[128,4096]{1,0:T(8,128)(2,1)S(1)} %collective-permute-done.19.refs_0_, bf16[128,4096]{1,0:T(8,128)(2,1)S(1)} %collective-permute-done.20.refs_1_, bf16[4096,512]{1,0:T(8,128)(2,1)S(1)} %copy-done.1, ...), custom_call_target="tpu_custom_call" | custom-call | flops 2147483648 | tf_op jit(solution)/shard_map/product/pallas_call | solution.py:310
  102.3 6.1 %collective-permute-done.21 = bf16[128,1024]{1,0:T(8,128)(2,1)S(1)} collective-permute-done((bf16[128,1024]{1,0:T(8,128)(2,1)S(1)}, bf16[128,1024]{1,0:T(8,128)(2,1)S(1)}, u32[]{:S(2)}, u32[]{:S(2)}) %collective-permute-start.21) | collective-permute-done | bytes 262176 | tf_op jit(solution)/shard_map/ppermute | solution.py:457
  108.5 10.6 %collective-permute-done.24.refs_0_ = bf16[128,4096]{1,0:T(8,128)(2,1)S(1)} collective-permute-done((bf16[128,4096]{1,0:T(8,128)(2,1)S(1)}, bf16[128,4096]{1,0:T(8,128)(2,1)S(1)}, u32[]{:S(2)}, u32[]{:S(2)}) %collective-permute-start.24) | collective-permute-done | bytes 1048608 | tf_op jit(solution)/shard_map/ppermute | solution.py:53
  119.1 1.2 collective-permute-done.25.refs_1_
  121.0 1.4 collective-permute-start.30
  122.4 4.6 %product.7 = (f32[128,1024]{1,0:T(8,128)S(1)}, bf16[128,1024]{1,0:T(8,128)(2,1)S(1)}) custom-call(s32[3]{0:T(128)S(1)} %pad_add_fusion.spots_ref, bf16[128,4096]{1,0:T(8,128)(2,1)S(1)} %collective-permute-done.24.refs_0_, bf16[128,4096]{1,0:T(8,128)(2,1)S(1)} %collective-permute-done.25.refs_1_, bf16[4096,512]{1,0:T(8,128)(2,1)S(1)} %copy-done.1, ...), custom_call_target="tpu_custom_call" | custom-call | flops 2147483648 | tf_op jit(solution)/shard_map/product/pallas_call | solution.py:310
  127.7 5.8 %collective-permute-done.26 = bf16[128,1024]{1,0:T(8,128)(2,1)S(1)} collective-permute-done((bf16[128,1024]{1,0:T(8,128)(2,1)S(1)}, bf16[128,1024]{1,0:T(8,128)(2,1)S(1)}, u32[]{:S(2)}, u32[]{:S(2)}) %collective-permute-start.26) | collective-permute-done | bytes 262176 | tf_op jit(solution)/shard_map/ppermute | solution.py:457
  133.6 9.7 %collective-permute-done.29.refs_0_ = bf16[128,4096]{1,0:T(8,128)(2,1)S(1)} collective-permute-done((bf16[128,4096]{1,0:T(8,128)(2,1)S(1)}, bf16[128,4096]{1,0:T(8,128)(2,1)S(1)}, u32[]{:S(2)}, u32[]{:S(2)}) %collective-permute-start.29) | collective-permute-done | bytes 1048608 | tf_op jit(solution)/shard_map/ppermute | solution.py:53
  144.5 1.5 collective-permute-start.33
  146.0 1.2 collective-permute-start.22
  148.1 4.6 %product.8 = (f32[128,1024]{1,0:T(8,128)S(1)}, bf16[128,1024]{1,0:T(8,128)(2,1)S(1)}) custom-call(s32[3]{0:T(128)S(1)} %pad_add_fusion.spots_ref, bf16[128,4096]{1,0:T(8,128)(2,1)S(1)} %collective-permute-done.29.refs_0_, bf16[128,4096]{1,0:T(8,128)(2,1)S(1)} %collective-permute-done.30.refs_1_, bf16[4096,512]{1,0:T(8,128)(2,1)S(1)} %copy-done.1, ...), custom_call_target="tpu_custom_call" | custom-call | flops 2147483648 | tf_op jit(solution)/shard_map/product/pallas_call | solution.py:310
  153.4 5.4 %collective-permute-done.32.refs_0_ = bf16[64,4096]{1,0:T(8,128)(2,1)S(1)} collective-permute-done((bf16[64,4096]{1,0:T(8,128)(2,1)S(1)}, bf16[64,4096]{1,0:T(8,128)(2,1)S(1)}, u32[]{:S(2)}, u32[]{:S(2)}) %collective-permute-start.32) | collective-permute-done | bytes 524320 | tf_op jit(solution)/shard_map/ppermute | solution.py:58
  158.9 2.8 %collective-permute-start.28 = (bf16[64,1024]{1,0:T(8,128)(2,1)S(1)}, bf16[64,1024]{1,0:T(8,128)(2,1)S(1)}, u32[]{:S(2)}, u32[]{:S(2)}) collective-permute-start(bf16[64,1024]{1,0:T(8,128)(2,1)S(1)} %get-tuple-element.89), channel_id=1, source_target_pairs={{0,16},{2,18},{8,24},{10,26},{16,28},{18,30},{24,20},{26,22},{28,1... | collective-permute-start | bytes 393224 | tf_op jit(solution)/shard_map/ppermute | solution.py:495
  161.7 3.5 %product.9.refs_4_ = bf16[128,1024]{1,0:T(8,128)(2,1)S(1)} custom-call(s32[3]{0:T(128)S(1)} %pad_add_fusion.spots_ref, bf16[64,4096]{1,0:T(8,128)(2,1)S(1)} %collective-permute-done.32.refs_0_, bf16[64,4096]{1,0:T(8,128)(2,1)S(1)} %collective-permute-done.33.refs_1_, bf16[4096,512]{1,0:T(8,128)(2,1)S(1)} %copy-done.1, ...), custom_call_target="tpu_custom_call" | custom-call | flops 1073741824 | tf_op jit(solution)/shard_map/product/pallas_call | solution.py:310
  167.0 1.3 collective-permute-start.35
  168.3 4.2 %collective-permute-start.36 = (bf16[64,1024]{1,0:T(8,128)(2,1)S(1)}, bf16[64,1024]{1,0:T(8,128)(2,1)S(1)}, u32[]{:S(2)}, u32[]{:S(2)}) collective-permute-start(bf16[64,1024]{1,0:T(8,128)(2,1)S(1)} %get-tuple-element.88), channel_id=1, source_target_pairs={{1,20},{3,22},{9,12},{11,14},{16,5},{18,7},{24,1},{26,3},{28,9},{3... | collective-permute-start | bytes 393224 | tf_op jit(solution)/shard_map/ppermute | solution.py:485
  172.5 1.3 collective-permute-start.37
  173.8 5.0 %collective-permute-start.38 = (bf16[128,1024]{1,0:T(8,128)(2,1)S(1)}, bf16[128,1024]{1,0:T(8,128)(2,1)S(1)}, u32[]{:S(2)}, u32[]{:S(2)}) collective-permute-start(bf16[128,1024]{1,0:T(8,128)(2,1)S(1)} %product.9.refs_4_), channel_id=1, source_target_pairs={{1,28},{3,30},{9,20},{11,22},{16,13},{18,15},{24,5},{26,7},{28,1},... | collective-permute-start | bytes 786440 | tf_op jit(solution)/shard_map/ppermute | solution.py:479
  178.8 1.7 collective-permute-done.35.refs_6_
  180.6 1.3 collective-permute-start.39
  181.8 2.0 %collective-permute-done.36.refs_7_ = bf16[64,1024]{1,0:T(8,128)(2,1)S(1)} collective-permute-done((bf16[64,1024]{1,0:T(8,128)(2,1)S(1)}, bf16[64,1024]{1,0:T(8,128)(2,1)S(1)}, u32[]{:S(2)}, u32[]{:S(2)}) %collective-permute-start.36) | collective-permute-done | bytes 131104 | tf_op jit(solution)/shard_map/ppermute | solution.py:485
  183.8 1.9 collective-permute-start.40
  185.7 3.6 %collective-permute-done.39.refs_10_ = bf16[64,1024]{1,0:T(8,128)(2,1)S(1)} collective-permute-done((bf16[64,1024]{1,0:T(8,128)(2,1)S(1)}, bf16[64,1024]{1,0:T(8,128)(2,1)S(1)}, u32[]{:S(2)}, u32[]{:S(2)}) %collective-permute-start.39) | collective-permute-done | bytes 131104 | tf_op jit(solution)/shard_map/ppermute | solution.py:485
  189.3 4.1 %collective-permute-done.40.refs_11_ = bf16[64,1024]{1,0:T(8,128)(2,1)S(1)} collective-permute-done((bf16[64,1024]{1,0:T(8,128)(2,1)S(1)}, bf16[64,1024]{1,0:T(8,128)(2,1)S(1)}, u32[]{:S(2)}, u32[]{:S(2)}) %collective-permute-start.40) | collective-permute-done | bytes 131104 | tf_op jit(solution)/shard_map/ppermute | solution.py:485
  193.4 1.8 assemble.1
  (69 shorter events, 14.9 us)
Async XLA Ops:
  0.0 7.6 %copy-start.3 = (s32[32]{0:T(128)S(1)}, s32[32]{0:T(128)}, u32[]{:S(2)}) copy-start(s32[32]{0:T(128)} %pages_ref.1) | copy-start | bytes 388
  0.0 70.7 %collective-permute-start.17 = (bf16[4096,512]{1,0:T(8,128)(2,1)}, bf16[4096,512]{1,0:T(8,128)(2,1)}, u32[]{:S(2)}, u32[]{:S(2)}) collective-permute-start(bf16[4096,512]{1,0:T(8,128)(2,1)} %refs_2_.7), channel_id=1, source_target_pairs={{0,2},{2,0},{4,6},{6,4},{8,10},{10,8},{12,14},{14,12},{16,18},{18,... | collective-permute-start | bytes 12582920 | tf_op jit(solution)/shard_map/ppermute | solution.py:44
  3.1 5.0 %copy-start.2 = (bf16[512,512]{1,0:T(8,128)(2,1)S(1)}, bf16[512,512]{1,0:T(8,128)(2,1)}, u32[]{:S(2)}) copy-start(bf16[512,512]{1,0:T(8,128)(2,1)} %pack_pages.1.own_ref.refs_0_) | copy-start | bytes 1572868
  3.1 5.0 %collective-permute-start.2 = (bf16[512,512]{1,0:T(8,128)(2,1)}, bf16[512,512]{1,0:T(8,128)(2,1)S(1)}, u32[]{:S(2)}, u32[]{:S(2)}) collective-permute-start(bf16[512,512]{1,0:T(8,128)(2,1)} %pack_pages.1.own_ref.refs_0_), channel_id=1, source_target_pairs={{0,2},{2,0},{4,6},{6,4},{8,10},{10,8},{12,14},{14,12},{16,18},{18,... | collective-permute-start | bytes 1572872 | tf_op jit(solution)/shard_map/ppermute | solution.py:44
  3.9 14.0 %collective-permute-start = (bf16[512,512]{1,0:T(8,128)(2,1)}, bf16[512,512]{1,0:T(8,128)(2,1)S(1)}, u32[]{:S(2)}, u32[]{:S(2)}) collective-permute-start(bf16[512,512]{1,0:T(8,128)(2,1)} %pack_pages.1.own_ref.refs_0_), channel_id=1, source_target_pairs={{0,8},{2,10},{8,16},{10,18},{16,24},{18,26},{24,28},{26,30},{28,20... | collective-permute-start | bytes 1572872 | tf_op jit(solution)/shard_map/ppermute | solution.py:53
  4.5 13.8 %collective-permute-start.1 = (bf16[512,512]{1,0:T(8,128)(2,1)}, bf16[512,512]{1,0:T(8,128)(2,1)S(1)}, u32[]{:S(2)}, u32[]{:S(2)}) collective-permute-start(bf16[512,512]{1,0:T(8,128)(2,1)} %pack_pages.1.own_ref.refs_0_), channel_id=1, source_target_pairs={{0,4},{2,6},{8,0},{10,2},{16,8},{18,10},{24,16},{26,18},{28,24},{3... | collective-permute-start | bytes 1572872 | tf_op jit(solution)/shard_map/ppermute | solution.py:54
  18.3 2.5 %collective-permute-start.5 = (bf16[512,512]{1,0:T(8,128)(2,1)S(1)}, bf16[512,512]{1,0:T(8,128)(2,1)S(1)}, u32[]{:S(2)}, u32[]{:S(2)}) collective-permute-start(bf16[512,512]{1,0:T(8,128)(2,1)S(1)} %collective-permute-done.refs_0_), channel_id=1, source_target_pairs={{0,2},{2,0},{4,6},{6,4},{8,10},{10,8},{12,14},{14,12},{16,18},{18,... | collective-permute-start | bytes 1572872 | tf_op jit(solution)/shard_map/ppermute | solution.py:44
  18.3 2.7 %collective-permute-start.6 = (bf16[512,512]{1,0:T(8,128)(2,1)S(1)}, bf16[512,512]{1,0:T(8,128)(2,1)S(1)}, u32[]{:S(2)}, u32[]{:S(2)}) collective-permute-start(bf16[512,512]{1,0:T(8,128)(2,1)S(1)} %collective-permute-done.1.refs_2_), channel_id=1, source_target_pairs={{0,2},{2,0},{4,6},{6,4},{8,10},{10,8},{12,14},{14,12},{16,18},{18,... | collective-permute-start | bytes 1572872 | tf_op jit(solution)/shard_map/ppermute | solution.py:44
  18.8 13.8 %collective-permute-start.3 = (bf16[512,512]{1,0:T(8,128)(2,1)S(1)}, bf16[512,512]{1,0:T(8,128)(2,1)S(1)}, u32[]{:S(2)}, u32[]{:S(2)}) collective-permute-start(bf16[512,512]{1,0:T(8,128)(2,1)S(1)} %collective-permute-done.refs_0_), channel_id=1, source_target_pairs={{0,8},{2,10},{8,16},{10,18},{16,24},{18,26},{24,28},{26,30},{28,20... | collective-permute-start | bytes 1572872 | tf_op jit(solution)/shard_map/ppermute | solution.py:53
  20.4 13.6 %collective-permute-start.4 = (bf16[512,512]{1,0:T(8,128)(2,1)S(1)}, bf16[512,512]{1,0:T(8,128)(2,1)S(1)}, u32[]{:S(2)}, u32[]{:S(2)}) collective-permute-start(bf16[512,512]{1,0:T(8,128)(2,1)S(1)} %collective-permute-done.1.refs_2_), channel_id=1, source_target_pairs={{0,4},{2,6},{8,0},{10,2},{16,8},{18,10},{24,16},{26,18},{28,24},{3... | collective-permute-start | bytes 1572872 | tf_op jit(solution)/shard_map/ppermute | solution.py:54
  34.0 2.5 %collective-permute-start.10 = (bf16[512,512]{1,0:T(8,128)(2,1)S(1)}, bf16[512,512]{1,0:T(8,128)(2,1)S(1)}, u32[]{:S(2)}, u32[]{:S(2)}) collective-permute-start(bf16[512,512]{1,0:T(8,128)(2,1)S(1)} %collective-permute-done.4.refs_2_), channel_id=1, source_target_pairs={{0,2},{2,0},{4,6},{6,4},{8,10},{10,8},{12,14},{14,12},{16,18},{18,... | collective-permute-start | bytes 1572872 | tf_op jit(solution)/shard_map/ppermute | solution.py:44
  34.0 2.7 %collective-permute-start.9 = (bf16[512,512]{1,0:T(8,128)(2,1)S(1)}, bf16[512,512]{1,0:T(8,128)(2,1)S(1)}, u32[]{:S(2)}, u32[]{:S(2)}) collective-permute-start(bf16[512,512]{1,0:T(8,128)(2,1)S(1)} %collective-permute-done.3.refs_0_), channel_id=1, source_target_pairs={{0,2},{2,0},{4,6},{6,4},{8,10},{10,8},{12,14},{14,12},{16,18},{18,... | collective-permute-start | bytes 1572872 | tf_op jit(solution)/shard_map/ppermute | solution.py:44
  34.5 13.8 %collective-permute-start.7 = (bf16[512,512]{1,0:T(8,128)(2,1)S(1)}, bf16[512,512]{1,0:T(8,128)(2,1)S(1)}, u32[]{:S(2)}, u32[]{:S(2)}) collective-permute-start(bf16[512,512]{1,0:T(8,128)(2,1)S(1)} %collective-permute-done.3.refs_0_), channel_id=1, source_target_pairs={{0,8},{2,10},{8,16},{10,18},{16,24},{18,26},{24,28},{26,30},{28,20... | collective-permute-start | bytes 1572872 | tf_op jit(solution)/shard_map/ppermute | solution.py:53
  36.1 13.6 %collective-permute-start.8 = (bf16[512,512]{1,0:T(8,128)(2,1)S(1)}, bf16[512,512]{1,0:T(8,128)(2,1)S(1)}, u32[]{:S(2)}, u32[]{:S(2)}) collective-permute-start(bf16[512,512]{1,0:T(8,128)(2,1)S(1)} %collective-permute-done.4.refs_2_), channel_id=1, source_target_pairs={{0,4},{2,6},{8,0},{10,2},{16,8},{18,10},{24,16},{26,18},{28,24},{3... | collective-permute-start | bytes 1572872 | tf_op jit(solution)/shard_map/ppermute | solution.py:54
  49.6 2.6 %collective-permute-start.13 = (bf16[512,512]{1,0:T(8,128)(2,1)S(1)}, bf16[512,512]{1,0:T(8,128)(2,1)S(1)}, u32[]{:S(2)}, u32[]{:S(2)}) collective-permute-start(bf16[512,512]{1,0:T(8,128)(2,1)S(1)} %collective-permute-done.7.refs_0_), channel_id=1, source_target_pairs={{0,2},{2,0},{4,6},{6,4},{8,10},{10,8},{12,14},{14,12},{16,18},{18,... | collective-permute-start | bytes 1572872 | tf_op jit(solution)/shard_map/ppermute | solution.py:44
  49.6 2.7 %collective-permute-start.14 = (bf16[512,512]{1,0:T(8,128)(2,1)S(1)}, bf16[512,512]{1,0:T(8,128)(2,1)S(1)}, u32[]{:S(2)}, u32[]{:S(2)}) collective-permute-start(bf16[512,512]{1,0:T(8,128)(2,1)S(1)} %collective-permute-done.8.refs_2_), channel_id=1, source_target_pairs={{0,2},{2,0},{4,6},{6,4},{8,10},{10,8},{12,14},{14,12},{16,18},{18,... | collective-permute-start | bytes 1572872 | tf_op jit(solution)/shard_map/ppermute | solution.py:44
  50.2 10.8 %collective-permute-start.11 = (bf16[256,512]{1,0:T(8,128)(2,1)S(1)}, bf16[256,512]{1,0:T(8,128)(2,1)S(1)}, u32[]{:S(2)}, u32[]{:S(2)}) collective-permute-start(bf16[256,512]{1,0:T(8,128)(2,1)S(1)} %slice.30), channel_id=1, source_target_pairs={{0,8},{2,10},{8,16},{10,18},{16,24},{18,26},{24,28},{26,30},{28,20... | collective-permute-start | bytes 786440 | tf_op jit(solution)/shard_map/ppermute | solution.py:58
  51.8 9.2 %collective-permute-start.12 = (bf16[256,512]{1,0:T(8,128)(2,1)S(1)}, bf16[256,512]{1,0:T(8,128)(2,1)S(1)}, u32[]{:S(2)}, u32[]{:S(2)}) collective-permute-start(bf16[256,512]{1,0:T(8,128)(2,1)S(1)} %slice.31), channel_id=1, source_target_pairs={{0,4},{2,6},{8,0},{10,2},{16,8},{18,10},{24,16},{26,18},{28,24},{3... | collective-permute-start | bytes 786440 | tf_op jit(solution)/shard_map/ppermute | solution.py:59
  61.0 1.6 collective-permute-start.15
  61.2 1.8 collective-permute-start.16
  68.5 25.3 %collective-permute-start.19 = (bf16[128,4096]{1,0:T(8,128)(2,1)S(1)}, bf16[128,4096]{1,0:T(8,128)(2,1)S(1)}, u32[]{:S(2)}, u32[]{:S(2)}) collective-permute-start(bf16[128,4096]{1,0:T(8,128)(2,1)S(1)} %attend_last.1.refs_0_), channel_id=1, source_target_pairs={{0,8},{2,10},{8,16},{10,18},{16,24},{18,26},{24,28},{26,30},{28,20... | collective-permute-start | bytes 3145736 | tf_op jit(solution)/shard_map/ppermute | solution.py:53
  70.2 24.9 %collective-permute-start.20 = (bf16[128,4096]{1,0:T(8,128)(2,1)S(1)}, bf16[128,4096]{1,0:T(8,128)(2,1)S(1)}, u32[]{:S(2)}, u32[]{:S(2)}) collective-permute-start(bf16[128,4096]{1,0:T(8,128)(2,1)S(1)} %attend_last.1.refs_0_), channel_id=1, source_target_pairs={{0,4},{2,6},{8,0},{10,2},{16,8},{18,10},{24,16},{26,18},{28,24},{3... | collective-permute-start | bytes 3145736 | tf_op jit(solution)/shard_map/ppermute | solution.py:54
  70.7 2.2 %copy-start = (bf16[4096,512]{1,0:T(8,128)(2,1)S(1)}, bf16[4096,512]{1,0:T(8,128)(2,1)}, u32[]{:S(2)}) copy-start(bf16[4096,512]{1,0:T(8,128)(2,1)} %refs_2_.7) | copy-start | bytes 12582916
  72.9 24.3 %copy-start.1 = (bf16[4096,512]{1,0:T(8,128)(2,1)S(1)}, bf16[4096,512]{1,0:T(8,128)(2,1)}, u32[]{:S(2)}) copy-start(bf16[4096,512]{1,0:T(8,128)(2,1)} %refs_2_.7) | copy-start | bytes 12582916
  76.5 18.6 %collective-permute-start.18 = (bf16[128,1024]{1,0:T(8,128)(2,1)S(1)}, bf16[128,1024]{1,0:T(8,128)(2,1)S(1)}, u32[]{:S(2)}, u32[]{:S(2)}) collective-permute-start(bf16[128,1024]{1,0:T(8,128)(2,1)S(1)} %product.5.refs_0_), channel_id=1, source_target_pairs={{1,0},{3,2},{9,8},{11,10},{16,17},{18,19},{24,25},{26,27},{28,29},... | collective-permute-start | bytes 786440 | tf_op jit(solution)/shard_map/ppermute | solution.py:479
  95.1 24.0 %collective-permute-start.24 = (bf16[128,4096]{1,0:T(8,128)(2,1)S(1)}, bf16[128,4096]{1,0:T(8,128)(2,1)S(1)}, u32[]{:S(2)}, u32[]{:S(2)}) collective-permute-start(bf16[128,4096]{1,0:T(8,128)(2,1)S(1)} %collective-permute-done.19.refs_0_), channel_id=1, source_target_pairs={{0,8},{2,10},{8,16},{10,18},{16,24},{18,26},{24,28},{26,30},{28,20... | collective-permute-start | bytes 3145736 | tf_op jit(solution)/shard_map/ppermute | solution.py:53
  96.6 23.8 %collective-permute-start.25 = (bf16[128,4096]{1,0:T(8,128)(2,1)S(1)}, bf16[128,4096]{1,0:T(8,128)(2,1)S(1)}, u32[]{:S(2)}, u32[]{:S(2)}) collective-permute-start(bf16[128,4096]{1,0:T(8,128)(2,1)S(1)} %collective-permute-done.20.refs_1_), channel_id=1, source_target_pairs={{0,4},{2,6},{8,0},{10,2},{16,8},{18,10},{24,16},{26,18},{28,24},{3... | collective-permute-start | bytes 3145736 | tf_op jit(solution)/shard_map/ppermute | solution.py:54
  101.7 6.7 %collective-permute-start.21 = (bf16[128,1024]{1,0:T(8,128)(2,1)S(1)}, bf16[128,1024]{1,0:T(8,128)(2,1)S(1)}, u32[]{:S(2)}, u32[]{:S(2)}) collective-permute-start(bf16[128,1024]{1,0:T(8,128)(2,1)S(1)} %get-tuple-element.73), channel_id=1, source_target_pairs={{0,1},{1,0},{2,3},{3,2},{4,5},{5,4},{6,7},{7,6},{8,9},{9,8},{10,11... | collective-permute-start | bytes 786440 | tf_op jit(solution)/shard_map/ppermute | solution.py:457
  120.4 22.8 %collective-permute-start.29 = (bf16[128,4096]{1,0:T(8,128)(2,1)S(1)}, bf16[128,4096]{1,0:T(8,128)(2,1)S(1)}, u32[]{:S(2)}, u32[]{:S(2)}) collective-permute-start(bf16[128,4096]{1,0:T(8,128)(2,1)S(1)} %collective-permute-done.24.refs_0_), channel_id=1, source_target_pairs={{0,8},{2,10},{8,16},{10,18},{16,24},{18,26},{24,28},{26,30},{28,20... | collective-permute-start | bytes 3145736 | tf_op jit(solution)/shard_map/ppermute | solution.py:53
  121.0 22.8 %collective-permute-start.30 = (bf16[128,4096]{1,0:T(8,128)(2,1)S(1)}, bf16[128,4096]{1,0:T(8,128)(2,1)S(1)}, u32[]{:S(2)}, u32[]{:S(2)}) collective-permute-start(bf16[128,4096]{1,0:T(8,128)(2,1)S(1)} %collective-permute-done.25.refs_1_), channel_id=1, source_target_pairs={{0,4},{2,6},{8,0},{10,2},{16,8},{18,10},{24,16},{26,18},{28,24},{3... | collective-permute-start | bytes 3145736 | tf_op jit(solution)/shard_map/ppermute | solution.py:54
  127.1 6.4 %collective-permute-start.26 = (bf16[128,1024]{1,0:T(8,128)(2,1)S(1)}, bf16[128,1024]{1,0:T(8,128)(2,1)S(1)}, u32[]{:S(2)}, u32[]{:S(2)}) collective-permute-start(bf16[128,1024]{1,0:T(8,128)(2,1)S(1)} %get-tuple-element.77), channel_id=1, source_target_pairs={{0,1},{1,0},{2,3},{3,2},{4,5},{5,4},{6,7},{7,6},{8,9},{9,8},{10,11... | collective-permute-start | bytes 786440 | tf_op jit(solution)/shard_map/ppermute | solution.py:457
  143.9 14.9 %collective-permute-start.32 = (bf16[64,4096]{1,0:T(8,128)(2,1)S(1)}, bf16[64,4096]{1,0:T(8,128)(2,1)S(1)}, u32[]{:S(2)}, u32[]{:S(2)}) collective-permute-start(bf16[64,4096]{1,0:T(8,128)(2,1)S(1)} %slice.36), channel_id=1, source_target_pairs={{0,8},{2,10},{8,16},{10,18},{16,24},{18,26},{24,28},{26,30},{28,20... | collective-permute-start | bytes 1572872 | tf_op jit(solution)/shard_map/ppermute | solution.py:58
  144.5 14.4 %collective-permute-start.33 = (bf16[64,4096]{1,0:T(8,128)(2,1)S(1)}, bf16[64,4096]{1,0:T(8,128)(2,1)S(1)}, u32[]{:S(2)}, u32[]{:S(2)}) collective-permute-start(bf16[64,4096]{1,0:T(8,128)(2,1)S(1)} %slice.37), channel_id=1, source_target_pairs={{0,4},{2,6},{8,0},{10,2},{16,8},{18,10},{24,16},{26,18},{28,24},{3... | collective-permute-start | bytes 1572872 | tf_op jit(solution)/shard_map/ppermute | solution.py:59
  146.0 19.2 %collective-permute-start.22 = (bf16[64,1024]{1,0:T(8,128)(2,1)S(1)}, bf16[64,1024]{1,0:T(8,128)(2,1)S(1)}, u32[]{:S(2)}, u32[]{:S(2)}) collective-permute-start(bf16[64,1024]{1,0:T(8,128)(2,1)S(1)} %get-tuple-element.92), channel_id=1, source_target_pairs={{0,4},{2,6},{8,0},{10,2},{16,8},{18,10},{24,16},{26,18},{28,24},{3... | collective-permute-start | bytes 393224 | tf_op jit(solution)/shard_map/ppermute | solution.py:495
  147.3 18.0 %collective-permute-start.23 = (bf16[64,1024]{1,0:T(8,128)(2,1)S(1)}, bf16[64,1024]{1,0:T(8,128)(2,1)S(1)}, u32[]{:S(2)}, u32[]{:S(2)}) collective-permute-start(bf16[64,1024]{1,0:T(8,128)(2,1)S(1)} %get-tuple-element.91), channel_id=1, source_target_pairs={{0,8},{2,10},{8,16},{10,18},{16,24},{18,26},{24,28},{26,30},{28,20... | collective-permute-start | bytes 393224 | tf_op jit(solution)/shard_map/ppermute | solution.py:495
  152.7 12.5 %collective-permute-start.31 = (bf16[128,1024]{1,0:T(8,128)(2,1)S(1)}, bf16[128,1024]{1,0:T(8,128)(2,1)S(1)}, u32[]{:S(2)}, u32[]{:S(2)}) collective-permute-start(bf16[128,1024]{1,0:T(8,128)(2,1)S(1)} %get-tuple-element.81), channel_id=1, source_target_pairs={{0,1},{1,0},{2,3},{3,2},{4,5},{5,4},{6,7},{7,6},{8,9},{9,8},{10,11... | collective-permute-start | bytes 786440 | tf_op jit(solution)/shard_map/ppermute | solution.py:457
  158.8 6.5 %collective-permute-start.27 = (bf16[64,1024]{1,0:T(8,128)(2,1)S(1)}, bf16[64,1024]{1,0:T(8,128)(2,1)S(1)}, u32[]{:S(2)}, u32[]{:S(2)}) collective-permute-start(bf16[64,1024]{1,0:T(8,128)(2,1)S(1)} %get-tuple-element.90), channel_id=1, source_target_pairs={{0,12},{2,14},{8,4},{10,6},{16,0},{18,2},{24,8},{26,10},{28,16},{3... | collective-permute-start | bytes 393224 | tf_op jit(solution)/shard_map/ppermute | solution.py:495
  158.9 7.3 %collective-permute-start.28 = (bf16[64,1024]{1,0:T(8,128)(2,1)S(1)}, bf16[64,1024]{1,0:T(8,128)(2,1)S(1)}, u32[]{:S(2)}, u32[]{:S(2)}) collective-permute-start(bf16[64,1024]{1,0:T(8,128)(2,1)S(1)} %get-tuple-element.89), channel_id=1, source_target_pairs={{0,16},{2,18},{8,24},{10,26},{16,28},{18,30},{24,20},{26,22},{28,1... | collective-permute-start | bytes 393224 | tf_op jit(solution)/shard_map/ppermute | solution.py:495
  166.2 27.2 %collective-permute-start.34 = (bf16[256,1024]{1,0:T(8,128)(2,1)S(1)}, bf16[256,1024]{1,0:T(8,128)(2,1)S(1)}, u32[]{:S(2)}, u32[]{:S(2)}) collective-permute-start(bf16[256,1024]{1,0:T(8,128)(2,1)S(1)} %join.1), channel_id=1, source_target_pairs={{0,1},{1,0},{2,3},{3,2},{4,5},{5,4},{6,7},{7,6},{8,9},{9,8},{10,11... | collective-permute-start | bytes 1572872 | tf_op jit(solution)/shard_map/ppermute | solution.py:457
  167.0 13.6 %collective-permute-start.35 = (bf16[64,1024]{1,0:T(8,128)(2,1)S(1)}, bf16[64,1024]{1,0:T(8,128)(2,1)S(1)}, u32[]{:S(2)}, u32[]{:S(2)}) collective-permute-start(bf16[64,1024]{1,0:T(8,128)(2,1)S(1)} %get-tuple-element.88), channel_id=1, source_target_pairs={{0,20},{2,22},{8,12},{10,14},{17,5},{19,7},{25,1},{27,3},{29,9},{3... | collective-permute-start | bytes 393224 | tf_op jit(solution)/shard_map/ppermute | solution.py:485
  168.3 15.6 %collective-permute-start.36 = (bf16[64,1024]{1,0:T(8,128)(2,1)S(1)}, bf16[64,1024]{1,0:T(8,128)(2,1)S(1)}, u32[]{:S(2)}, u32[]{:S(2)}) collective-permute-start(bf16[64,1024]{1,0:T(8,128)(2,1)S(1)} %get-tuple-element.88), channel_id=1, source_target_pairs={{1,20},{3,22},{9,12},{11,14},{16,5},{18,7},{24,1},{26,3},{28,9},{3... | collective-permute-start | bytes 393224 | tf_op jit(solution)/shard_map/ppermute | solution.py:485
  172.5 20.9 %collective-permute-start.37 = (bf16[128,1024]{1,0:T(8,128)(2,1)S(1)}, bf16[128,1024]{1,0:T(8,128)(2,1)S(1)}, u32[]{:S(2)}, u32[]{:S(2)}) collective-permute-start(bf16[128,1024]{1,0:T(8,128)(2,1)S(1)} %product.9.refs_4_), channel_id=1, source_target_pairs={{0,28},{2,30},{8,20},{10,22},{17,13},{19,15},{25,5},{27,7},{29,1},... | collective-permute-start | bytes 786440 | tf_op jit(solution)/shard_map/ppermute | solution.py:478
  173.8 19.6 %collective-permute-start.38 = (bf16[128,1024]{1,0:T(8,128)(2,1)S(1)}, bf16[128,1024]{1,0:T(8,128)(2,1)S(1)}, u32[]{:S(2)}, u32[]{:S(2)}) collective-permute-start(bf16[128,1024]{1,0:T(8,128)(2,1)S(1)} %product.9.refs_4_), channel_id=1, source_target_pairs={{1,28},{3,30},{9,20},{11,22},{16,13},{18,15},{24,5},{26,7},{28,1},... | collective-permute-start | bytes 786440 | tf_op jit(solution)/shard_map/ppermute | solution.py:479
  180.6 8.8 %collective-permute-start.39 = (bf16[64,1024]{1,0:T(8,128)(2,1)S(1)}, bf16[64,1024]{1,0:T(8,128)(2,1)S(1)}, u32[]{:S(2)}, u32[]{:S(2)}) collective-permute-start(bf16[64,1024]{1,0:T(8,128)(2,1)S(1)} %get-tuple-element.87), channel_id=1, source_target_pairs={{0,24},{2,26},{8,28},{10,30},{17,21},{19,23},{25,13},{27,15},{29,5... | collective-permute-start | bytes 393224 | tf_op jit(solution)/shard_map/ppermute | solution.py:485
  183.8 9.5 %collective-permute-start.40 = (bf16[64,1024]{1,0:T(8,128)(2,1)S(1)}, bf16[64,1024]{1,0:T(8,128)(2,1)S(1)}, u32[]{:S(2)}, u32[]{:S(2)}) collective-permute-start(bf16[64,1024]{1,0:T(8,128)(2,1)S(1)} %get-tuple-element.87), channel_id=1, source_target_pairs={{1,24},{3,26},{9,28},{11,30},{16,21},{18,23},{24,13},{26,15},{28,5... | collective-permute-start | bytes 393224 | tf_op jit(solution)/shard_map/ppermute | solution.py:485
